TPU v7x, 32 devices: a whole 2x2x4 slice. The times are simulated.
32 devices in a mesh: dir: 4 (over x, core), space: 8 (over z, y).
Axes of the slice: x: 2, y: 2, z: 4, core: 2. Of those that a mesh axis runs over, the one named last changes fastest.
Arguments:
- store: float32 [4, 2, 32, 512, 128], P('dir', None, 'space'), may hold values from 0.2 to 1.5
- rate: float32 [32, 512, 128], P('space'), may hold values from 0.3 to 3
- directions: float32 [8, 8, 8192], P('dir', 'space'), may hold values from -6 to 6
- owner_map: int32 [4], replicated, may hold values from 0 to 3, each once
- block_map: int32 [8], replicated, may hold values from 0 to 7, each once
Outputs:
- tangent: float32 [8, 2, 32, 512, 128], P('dir', None, 'space')
- sens: float32 [8, 8, 8192], P('dir', 'space')
All inputs are finite; a program needn't handle non-finite values.
Results may differ from a plain program's by a relative error of at most 0.000071.
Values sent between devices are 32-bit elements; how exact they have to be, the bound alone decides.
No kernel may reach another device: no remote copies, remote signals or barrier semaphores. Data moves between devices by JAX's collectives and lax.ppermute only.
A program may use at most 192 MiB of HBM per device.

v0:
```python
import jax
import jax.numpy as jnp
from jax import lax
from jax.sharding import PartitionSpec as P

STEPS = 2
SUBSTEPS = 3


spread_a = 0.08
spread_b = 0.06
drift = 0.25
decay_rate = 0.05
rate_scale = 0.1


def spread(value, axis, source):
    kept = jnp.where(lax.axis_index(axis) == source, value, 0).astype(value.dtype)
    return lax.psum(kept, axis)


def padded(block, sides, width):
    for axis, dim in sides:
        count = lax.axis_size(axis)
        forward = [(i, i + 1) for i in range(count - 1)]
        backward = [(target, source) for source, target in forward]
        low = lax.ppermute(
            lax.slice_in_dim(block, block.shape[dim] - width, None, axis=dim), axis, forward
        )
        high = lax.ppermute(lax.slice_in_dim(block, 0, width, axis=dim), axis, backward)
        block = jnp.concatenate([low, block, high], axis=dim)
    return block


def across_yz(field):
    lead = ((0, 0),) * (field.ndim - 2)
    total = jnp.pad(field[..., 1:, :], lead + ((0, 1), (0, 0)))
    total = total + jnp.pad(field[..., :-1, :], lead + ((1, 0), (0, 0)))
    total = total + jnp.pad(field[..., :, 1:], lead + ((0, 0), (0, 1)))
    total = total + jnp.pad(field[..., :, :-1], lead + ((0, 0), (1, 0)))
    return total


def advance(
    first, first_lower, first_upper, second, second_lower, second_upper, conc_a, conc_b, rate, vfine
):
    lap_first = first_lower + first_upper + across_yz(first) - 6.0 * first
    lap_second = second_lower + second_upper + across_yz(second) - 6.0 * second
    source = rate_scale * rate * (vfine * conc_a * conc_b + first * conc_b + conc_a * second)
    first_new = first + spread_a * lap_first - drift * (first - first_lower) - source
    second_new = (
        second
        + spread_b * lap_second
        - drift * (second - second_lower)
        + source
        - decay_rate * second
    )
    return (first_new, second_new)


def local(store, rate, directions, owner_map, block_map):
    dirs_dev = directions.shape[0]
    width_x, width_y, width_z = rate.shape
    mine = lax.axis_index("space")
    n_space = lax.axis_size("space")
    every = lax.all_gather(directions, "space", axis=1, tiled=True)
    clipped = jnp.clip(mine, 0, n_space - 1)
    picked_row = lax.dynamic_index_in_dim(every, block_map[clipped], 1, keepdims=False)
    coarse_one = picked_row.reshape(dirs_dev, width_x // 2, width_y // 4, width_z // 4)
    fine_one = jnp.repeat(jnp.repeat(jnp.repeat(coarse_one, 2, 1), 4, 2), 4, 3)
    valid = ((mine >= 0) & (mine < n_space)).astype(jnp.float32)
    vfine = fine_one * valid
    first = jnp.zeros((dirs_dev, width_x, width_y, width_z), jnp.float32)
    second = jnp.zeros((dirs_dev, width_x, width_y, width_z), jnp.float32)
    for step in range(STEPS):
        slab = spread(store, "dir", owner_map[step])[0]
        for inner in range(SUBSTEPS):
            edges = jnp.stack(
                [
                    jnp.concatenate([first[:, :1], first[:, -1:]], 1),
                    jnp.concatenate([second[:, :1], second[:, -1:]], 1),
                ],
                0,
            )
            wide = padded(edges, (("space", 2),), 1)
            first_lower = jnp.concatenate([wide[0, :, 0:1], first[:, :-1]], 1)
            first_upper = jnp.concatenate([first[:, 1:], wide[0, :, 3:4]], 1)
            second_lower = jnp.concatenate([wide[1, :, 0:1], second[:, :-1]], 1)
            second_upper = jnp.concatenate([second[:, 1:], wide[1, :, 3:4]], 1)
            first, second = advance(
                first,
                first_lower,
                first_upper,
                second,
                second_lower,
                second_upper,
                slab[0],
                slab[1],
                rate,
                vfine,
            )
    tangent = jnp.stack([first, second], 1)
    means = second.reshape(dirs_dev, width_x // 2, 2, width_y // 4, 4, width_z // 4, 4).mean(
        axis=(2, 4, 6)
    )
    coarse_q = means.reshape(dirs_dev, 1, -1)
    gathered = lax.all_gather(coarse_q, "space", axis=1, tiled=True)
    weights = (block_map == mine).astype(jnp.float32)
    sens = jnp.einsum("s,dsc->dc", weights, gathered, precision=lax.Precision.HIGHEST)[:, None]
    return (tangent, sens)


def solution(mesh):
    return jax.shard_map(
        local,
        mesh=mesh,
        in_specs=(
            P("dir", None, "space", None, None),
            P("space", None, None),
            P("dir", "space", None),
            P(),
            P(),
        ),
        out_specs=(P("dir", None, "space", None, None), P("dir", "space", None)),
        check_vma=False,
    )
```

profile of v0, /device:TPU:0, one launch (start us, length us, event | category | flops | bytes accessed | tf_op | source)
XLA Modules:
  0.0 648.1 jit_solution(14284519689713102604)
XLA Ops:
  16.7 6.5 %collective-permute-start = (f32[2,2,1,512,128]{3,2,4,1,0:T(1,128)}, f32[2,2,1,512,128]{3,2,4,1,0:T(1,128)}, u32[]{:S(2)}, u32[]{:S(2)}) collective-permute-start(f32[2,2,1,512,128]{3,2,4,1,0:T(1,128)} %broadcast.158), channel_id=1, source_target_pairs={{0,1},{1,2},{2,3},{3,4},{4,5},{5,6},{6,7},{8,9},{9,10},{10,11},{11... | collective-permute-start | bytes 3145736 | tf_op jit(solution)/shard_map/ppermute | solution.py:27
  25.8 66.8 %all_gather.6 = f32[2,8,8192]{2,0,1:T(2,128)S(1)} all-gather(f32[2,1,8192]{2,0,1:T(2,128)S(1)} %copy.83), channel_id=1, replica_groups=mesh['dir'=4,'space'=8] {'space'}, dimensions={1}, use_global_device_ids=true | all-gather | bytes 589824 | tf_op jit(solution)/shard_map/all_gather | solution.py:66
  119.4 4.9 fusion.3
  157.7 29.9 %collective-permute-done.2 = f32[2,2,1,512,128]{3,2,4,1,0:T(1,128)} collective-permute-done((f32[2,2,1,512,128]{3,2,4,1,0:T(1,128)}, f32[2,2,1,512,128]{3,2,4,1,0:T(1,128)}, u32[]{:S(2)}, u32[]{:S(2)}) %collective-permute-start.2) | collective-permute-done | bytes 1048608 | tf_op jit(solution)/shard_map/ppermute | solution.py:27
  192.4 5.3 fusion.15
  202.5 6.3 fusion.22
  218.8 11.8 %collective-permute-start.5 = (f32[2,2,1,512,128]{3,2,4,1,0:T(1,128)}, f32[2,2,1,512,128]{3,2,4,1,0:T(1,128)S(1)}, u32[]{:S(2)}, u32[]{:S(2)}) collective-permute-start(f32[2,2,1,512,128]{3,2,4,1,0:T(1,128)} %get-tuple-element.79), channel_id=1, source_target_pairs={{1,0},{2,1},{3,2},{4,3},{5,4},{6,5},{7,6},{9,8},{10,9},{11,10},{12... | collective-permute-start | bytes 3145736 | tf_op jit(solution)/shard_map/ppermute | solution.py:30
  235.6 27.0 %collective-permute-done.4 = f32[2,2,1,512,128]{3,2,4,1,0:T(1,128)S(1)} collective-permute-done((f32[2,2,1,512,128]{3,2,4,1,0:T(1,128)S(1)}, f32[2,2,1,512,128]{3,2,4,1,0:T(1,128)S(1)}, u32[]{:S(2)}, u32[]{:S(2)}) %collective-permute-start.4) | collective-permute-done | bytes 1048608 | tf_op jit(solution)/shard_map/ppermute | solution.py:27
  264.8 5.0 fusion.28
  274.6 6.3 fusion.35
  297.5 36.5 %collective-permute-done.6 = f32[2,2,1,512,128]{3,2,4,1,0:T(1,128)S(1)} collective-permute-done((f32[2,2,1,512,128]{3,2,4,1,0:T(1,128)}, f32[2,2,1,512,128]{3,2,4,1,0:T(1,128)S(1)}, u32[]{:S(2)}, u32[]{:S(2)}) %collective-permute-start.6) | collective-permute-done | bytes 1048608 | tf_op jit(solution)/shard_map/ppermute | solution.py:27
  336.3 5.0 fusion.41
  346.0 6.3 fusion.48
  368.7 35.5 %collective-permute-done.8 = f32[2,2,1,512,128]{3,2,4,1,0:T(1,128)S(1)} collective-permute-done((f32[2,2,1,512,128]{3,2,4,1,0:T(1,128)S(1)}, f32[2,2,1,512,128]{3,2,4,1,0:T(1,128)S(1)}, u32[]{:S(2)}, u32[]{:S(2)}) %collective-permute-start.8) | collective-permute-done | bytes 1048608 | tf_op jit(solution)/shard_map/ppermute | solution.py:27
  406.4 5.0 fusion.54
  422.0 5.1 fusion.61
  431.5 4.5 collective-permute-start.10
  440.5 36.5 %collective-permute-done.10 = f32[2,2,1,512,128]{3,2,4,1,0:T(1,128)S(1)} collective-permute-done((f32[2,2,1,512,128]{3,2,4,1,0:T(1,128)S(1)}, f32[2,2,1,512,128]{3,2,4,1,0:T(1,128)S(1)}, u32[]{:S(2)}, u32[]{:S(2)}) %collective-permute-start.10) | collective-permute-done | bytes 1048608 | tf_op jit(solution)/shard_map/ppermute | solution.py:27
  480.0 5.9 fusion.75
  488.9 9.0 %fusion.68 = f32[2,1,4,512,128]{3,2,4,0,1:T(4,128)S(1)} fusion(f32[2,4,512,128]{2,1,3,0:T(4,128)} %copy-done, f32[2,1,512,128]{2,1,3,0:T(1,128)} %get-tuple-element.112, f32[2,3,512,128]{2,1,3,0:T(4,128)} %get-tuple-element.17, f32[2,3,512,128]{2,1,3,0:T(4,128)} %get-tuple-element.16, f32[2,1,512,128]{2,1,3,0:T(1,128)} %get-tuple-element.110, ...), kind=kLoop, calls=%fused_computation.101 | loop fusion | flops 11534336 | bytes 24076288 | tf_op jit(solution)/shard_map/stack | solution.py:102
  501.0 5.4 copy.92
  506.5 70.6 %reshape.42 = f32[2,2,2,128,4,32,4]{6,5,4,3,2,1,0:T(8,128)} reshape(f32[2,4,512,128]{3,2,1,0:T(8,128)S(1)} %copy-done.13) | data formatting | bytes 4194304 | tf_op jit(solution)/shard_map/reshape | solution.py:103
  577.1 20.8 %reduce_sum.9 = f32[2,2,128,32]{3,2,1,0:T(8,128)S(1)} reduce(f32[2,2,2,128,4,32,4]{6,5,4,3,2,1,0:T(8,128)} %reshape.42, f32[]{:T(128)} %constant.13.clone.1), dimensions={2,4,6}, to_apply=%region_2.3 | reduce | flops 507904 | bytes 2162692 | tf_op jit(solution)/shard_map/reduce_sum | solution.py:103
  598.1 41.6 %all_gather.7 = f32[2,8,8192]{2,0,1:T(2,128)S(1)} all-gather(f32[2,1,8192]{2,0,1:T(2,128)S(1)} %div.10), channel_id=1, replica_groups=mesh['dir'=4,'space'=8] {'space'}, dimensions={1}, use_global_device_ids=true | all-gather | bytes 589824 | tf_op jit(solution)/shard_map/all_gather | solution.py:107
  (202 shorter events, 172.1 us)
Async XLA Ops:
  7.2 95.2 %all-reduce.51.cloned.1.call-start = ((), (), s32[]{:S(2)}) async-start(), calls=%async_computation | async-start | bytes 8388608 | tf_op jit(solution)/shard_map/psum | solution.py:19
  13.9 78.9 %copy-start.39 = (f32[4,512,128]{2,1,0:T(8,128)S(1)}, f32[4,512,128]{2,1,0:T(8,128)}, u32[]{:S(2)}) copy-start(f32[4,512,128]{2,1,0:T(8,128)} %param.6) | copy-start | bytes 3145732
  15.4 79.8 %collective-permute-start.1 = (f32[2,2,1,512,128]{3,2,4,1,0:T(1,128)}, f32[2,2,1,512,128]{3,2,4,1,0:T(1,128)}, u32[]{:S(2)}, u32[]{:S(2)}) collective-permute-start(f32[2,2,1,512,128]{3,2,4,1,0:T(1,128)} %broadcast.158), channel_id=1, source_target_pairs={{1,0},{2,1},{3,2},{4,3},{5,4},{6,5},{7,6},{9,8},{10,9},{11,10},{12... | collective-permute-start | bytes 3145736 | tf_op jit(solution)/shard_map/ppermute | solution.py:30
  16.7 81.4 %collective-permute-start = (f32[2,2,1,512,128]{3,2,4,1,0:T(1,128)}, f32[2,2,1,512,128]{3,2,4,1,0:T(1,128)}, u32[]{:S(2)}, u32[]{:S(2)}) collective-permute-start(f32[2,2,1,512,128]{3,2,4,1,0:T(1,128)} %broadcast.158), channel_id=1, source_target_pairs={{0,1},{1,2},{2,3},{3,4},{4,5},{5,6},{6,7},{8,9},{9,10},{10,11},{11... | collective-permute-start | bytes 3145736 | tf_op jit(solution)/shard_map/ppermute | solution.py:27
  139.3 48.4 %collective-permute-start.2 = (f32[2,2,1,512,128]{3,2,4,1,0:T(1,128)}, f32[2,2,1,512,128]{3,2,4,1,0:T(1,128)}, u32[]{:S(2)}, u32[]{:S(2)}) collective-permute-start(f32[2,2,1,512,128]{3,2,4,1,0:T(1,128)} %get-tuple-element.96), channel_id=1, source_target_pairs={{0,1},{1,2},{2,3},{3,4},{4,5},{5,6},{6,7},{8,9},{9,10},{10,11},{11... | collective-permute-start | bytes 3145736 | tf_op jit(solution)/shard_map/ppermute | solution.py:27
  143.7 45.9 %collective-permute-start.3 = (f32[2,2,1,512,128]{3,2,4,1,0:T(1,128)}, f32[2,2,1,512,128]{3,2,4,1,0:T(1,128)}, u32[]{:S(2)}, u32[]{:S(2)}) collective-permute-start(f32[2,2,1,512,128]{3,2,4,1,0:T(1,128)} %get-tuple-element.97), channel_id=1, source_target_pairs={{1,0},{2,1},{3,2},{4,3},{5,4},{6,5},{7,6},{9,8},{10,9},{11,10},{12... | collective-permute-start | bytes 3145736 | tf_op jit(solution)/shard_map/ppermute | solution.py:30
  153.0 39.3 %copy-start.19 = (f32[2,4,512,127]{2,1,3,0:T(4,128)S(1)}, f32[2,4,512,127]{2,1,3,0:T(4,128)}, u32[]{:S(2)}) copy-start(f32[2,4,512,127]{2,1,3,0:T(4,128)} %get-tuple-element.86) | copy-start | bytes 6242308
  153.0 39.3 %copy-start.20 = (f32[2,4,512,127]{2,1,3,0:T(4,128)S(1)}, f32[2,4,512,127]{2,1,3,0:T(4,128)}, u32[]{:S(2)}) copy-start(f32[2,4,512,127]{2,1,3,0:T(4,128)} %get-tuple-element.87) | copy-start | bytes 6242308
  156.9 35.5 %copy-start.14 = (f32[2,4,511,128]{2,1,3,0:T(4,128)S(1)}, f32[2,4,511,128]{2,1,3,0:T(4,128)}, u32[]{:S(2)}) copy-start(f32[2,4,511,128]{2,1,3,0:T(4,128)} %get-tuple-element.84) | copy-start | bytes 6279172
  156.9 35.5 %copy-start.15 = (f32[2,4,511,128]{2,1,3,0:T(4,128)S(1)}, f32[2,4,511,128]{2,1,3,0:T(4,128)}, u32[]{:S(2)}) copy-start(f32[2,4,511,128]{2,1,3,0:T(4,128)} %get-tuple-element.85) | copy-start | bytes 6279172
  156.9 35.5 %copy-start.16 = (f32[2,3,512,128]{2,1,3,0:T(4,128)S(1)}, f32[2,3,512,128]{2,1,3,0:T(4,128)}, u32[]{:S(2)}) copy-start(f32[2,3,512,128]{2,1,3,0:T(4,128)} %get-tuple-element.88) | copy-start | bytes 4718596
  214.4 48.2 %collective-permute-start.4 = (f32[2,2,1,512,128]{3,2,4,1,0:T(1,128)S(1)}, f32[2,2,1,512,128]{3,2,4,1,0:T(1,128)S(1)}, u32[]{:S(2)}, u32[]{:S(2)}) collective-permute-start(f32[2,2,1,512,128]{3,2,4,1,0:T(1,128)S(1)} %get-tuple-element.78), channel_id=1, source_target_pairs={{0,1},{1,2},{2,3},{3,4},{4,5},{5,6},{6,7},{8,9},{9,10},{10,11},{11... | collective-permute-start | bytes 3145736 | tf_op jit(solution)/shard_map/ppermute | solution.py:27
  218.8 44.5 %collective-permute-start.5 = (f32[2,2,1,512,128]{3,2,4,1,0:T(1,128)}, f32[2,2,1,512,128]{3,2,4,1,0:T(1,128)S(1)}, u32[]{:S(2)}, u32[]{:S(2)}) collective-permute-start(f32[2,2,1,512,128]{3,2,4,1,0:T(1,128)} %get-tuple-element.79), channel_id=1, source_target_pairs={{1,0},{2,1},{3,2},{4,3},{5,4},{6,5},{7,6},{9,8},{10,9},{11,10},{12... | collective-permute-start | bytes 3145736 | tf_op jit(solution)/shard_map/ppermute | solution.py:30
  286.4 47.6 %collective-permute-start.6 = (f32[2,2,1,512,128]{3,2,4,1,0:T(1,128)}, f32[2,2,1,512,128]{3,2,4,1,0:T(1,128)S(1)}, u32[]{:S(2)}, u32[]{:S(2)}) collective-permute-start(f32[2,2,1,512,128]{3,2,4,1,0:T(1,128)} %get-tuple-element.60), channel_id=1, source_target_pairs={{0,1},{1,2},{2,3},{3,4},{4,5},{5,6},{6,7},{8,9},{9,10},{10,11},{11... | collective-permute-start | bytes 3145736 | tf_op jit(solution)/shard_map/ppermute | solution.py:27
  290.9 43.9 %collective-permute-start.7 = (f32[2,2,1,512,128]{3,2,4,1,0:T(1,128)S(1)}, f32[2,2,1,512,128]{3,2,4,1,0:T(1,128)S(1)}, u32[]{:S(2)}, u32[]{:S(2)}) collective-permute-start(f32[2,2,1,512,128]{3,2,4,1,0:T(1,128)S(1)} %get-tuple-element.61), channel_id=1, source_target_pairs={{1,0},{2,1},{3,2},{4,3},{5,4},{6,5},{7,6},{9,8},{10,9},{11,10},{12... | collective-permute-start | bytes 3145736 | tf_op jit(solution)/shard_map/ppermute | solution.py:30
  297.5 38.8 %copy-start.6 = (f32[4,512,128]{1,0,2:T(4,128)S(1)}, f32[4,512,128]{1,0,2:T(4,128)}, u32[]{:S(2)}) copy-start(f32[4,512,128]{1,0,2:T(4,128)} %copy.89) | copy-start | bytes 3145732
  297.5 38.8 %copy-start.7 = (f32[4,512,128]{1,0,2:T(4,128)S(1)}, f32[4,512,128]{1,0,2:T(4,128)}, u32[]{:S(2)}) copy-start(f32[4,512,128]{1,0,2:T(4,128)} %copy.90) | copy-start | bytes 3145732
  357.9 46.3 %collective-permute-start.8 = (f32[2,2,1,512,128]{3,2,4,1,0:T(1,128)S(1)}, f32[2,2,1,512,128]{3,2,4,1,0:T(1,128)S(1)}, u32[]{:S(2)}, u32[]{:S(2)}) collective-permute-start(f32[2,2,1,512,128]{3,2,4,1,0:T(1,128)S(1)} %get-tuple-element.40), channel_id=1, source_target_pairs={{0,1},{1,2},{2,3},{3,4},{4,5},{5,6},{6,7},{8,9},{9,10},{10,11},{11... | collective-permute-start | bytes 3145736 | tf_op jit(solution)/shard_map/ppermute | solution.py:27
  362.2 42.7 %collective-permute-start.9 = (f32[2,2,1,512,128]{3,2,4,1,0:T(1,128)}, f32[2,2,1,512,128]{3,2,4,1,0:T(1,128)S(1)}, u32[]{:S(2)}, u32[]{:S(2)}) collective-permute-start(f32[2,2,1,512,128]{3,2,4,1,0:T(1,128)} %get-tuple-element.41), channel_id=1, source_target_pairs={{1,0},{2,1},{3,2},{4,3},{5,4},{6,5},{7,6},{9,8},{10,9},{11,10},{12... | collective-permute-start | bytes 3145736 | tf_op jit(solution)/shard_map/ppermute | solution.py:30
  411.4 68.6 %copy-start = (f32[2,4,512,128]{2,1,3,0:T(4,128)}, f32[2,4,512,128]{2,1,3,0:T(4,128)S(1)}, u32[]{:S(2)}) copy-start(f32[2,4,512,128]{2,1,3,0:T(4,128)S(1)} %fusion.54) | copy-start | bytes 6291460
  427.1 52.9 %copy-start.5 = (f32[2,4,512,128]{2,1,3,0:T(4,128)}, f32[2,4,512,128]{2,1,3,0:T(4,128)S(1)}, u32[]{:S(2)}) copy-start(f32[2,4,512,128]{2,1,3,0:T(4,128)S(1)} %fusion.61) | copy-start | bytes 6291460
  431.5 45.5 %collective-permute-start.10 = (f32[2,2,1,512,128]{3,2,4,1,0:T(1,128)S(1)}, f32[2,2,1,512,128]{3,2,4,1,0:T(1,128)S(1)}, u32[]{:S(2)}, u32[]{:S(2)}) collective-permute-start(f32[2,2,1,512,128]{3,2,4,1,0:T(1,128)S(1)} %get-tuple-element.22), channel_id=1, source_target_pairs={{0,1},{1,2},{2,3},{3,4},{4,5},{5,6},{6,7},{8,9},{9,10},{10,11},{11... | collective-permute-start | bytes 3145736 | tf_op jit(solution)/shard_map/ppermute | solution.py:27
  436.0 42.5 %collective-permute-start.11 = (f32[2,2,1,512,128]{3,2,4,1,0:T(1,128)S(1)}, f32[2,2,1,512,128]{3,2,4,1,0:T(1,128)S(1)}, u32[]{:S(2)}, u32[]{:S(2)}) collective-permute-start(f32[2,2,1,512,128]{3,2,4,1,0:T(1,128)S(1)} %get-tuple-element.23), channel_id=1, source_target_pairs={{1,0},{2,1},{3,2},{4,3},{5,4},{6,5},{7,6},{9,8},{10,9},{11,10},{12... | collective-permute-start | bytes 3145736 | tf_op jit(solution)/shard_map/ppermute | solution.py:30
  577.1 62.6 %copy-start.42 = (s32[8]{0:T(128)S(1)}, s32[8]{0:T(128)}, u32[]{:S(2)}) copy-start(s32[8]{0:T(128)} %param.9) | copy-start | bytes 100
  (32 other events, 254.1 us)
Sparse Core Ops, SparseCore 0:
  14.0 88.3 all-reduce.50
where the time goes:
time: 655 us; the launch traced here: 648 us
  local copies, waits for them, and re-layouts  189 us (29%)
  waiting for transfers between devices  167 us (25%)
  other arithmetic  116 us (18%)
  blocking collectives  108 us (16%)
  starting transfers between devices  47.9 us (7%)
  between operations  18.5 us (3%)
    ppermute x6, waiting for transfers between devices, padded(): lax.ppermute(lax.slice_in_dim(block, block.shape[dim] - width, None, axis...  166 us
    reshape x1, local copies, waits for them, and re-layouts, local(): second.reshape(dirs_dev, width_x // 2, 2, width_y // 4, 4, width_z // 4, 4)  70.6 us
    all_gather x1, blocking collectives, local(): every = lax.all_gather(directions, 'space', axis=1, tiled=True)  66.8 us
    all_gather x1, blocking collectives, local(): gathered = lax.all_gather(coarse_q, 'space', axis=1, tiled=True)  41.6 us
    sub x5, other arithmetic, advance(): second + spread_b * lap_second - drift * (second - second_lower) + source  29.9 us
    ppermute x6, starting transfers between devices, padded(): lax.ppermute(lax.slice_in_dim(block, block.shape[dim] - width, None, axis...  28.6 us
    sub x5, other arithmetic, advance(): first + spread_a * lap_first - drift * (first - first_lower) - source  25.1 us
    another operation x15, other arithmetic, local(): jnp.stack([jnp.concatenate([first[:, :1], first[:, -1:]], 1), jnp.concate...  21.2 us
  transfers between devices with their start and end apart: 13, of which 6 were waited for; matrix products, arithmetic and copies ran while one was open for 7% of the time, Pallas kernels for 0%

commit v1 on v0

v1 whole, which is shorter than its diff:
```python
import functools

import jax
import jax.numpy as jnp
from jax import lax
from jax.experimental import pallas as pl
from jax.experimental.pallas import tpu as pltpu
from jax.sharding import PartitionSpec as P

spread_a = 0.08
spread_b = 0.06
drift = 0.25
decay_rate = 0.05
rate_scale = 0.1

keep_a = 1.0 - 6.0 * spread_a - drift
keep_b = 1.0 - 6.0 * spread_b - drift - decay_rate
back_a = (spread_a + drift) / spread_a
back_b = (spread_b + drift) / spread_b

EDGE = 8
PAD = 8
CHUNK = 24
ANY = pl.BlockSpec(memory_space=pl.ANY)
SMEM = pl.BlockSpec(memory_space=pltpu.SMEM)
VMEM = pl.BlockSpec(memory_space=pltpu.VMEM)


def chunks(rows):
    return [(at, min(CHUNK, rows - at)) for at in range(0, rows, CHUNK)]


def run_all(copies):
    for copy in copies:
        copy.start()
    for copy in copies:
        copy.wait()


def arrange(scal, store, rate, mine, other, rate_m, sems):
    core, odd = scal[0], scal[1]
    rows = mine.shape[2]
    shift = rate.shape[1] // 2 - EDGE
    first = pl.multiple_of(core * shift, 8)
    second = pl.multiple_of((1 - core) * shift, 8)
    copies = []
    for m in range(4):
        layer = jnp.where(odd == 1, 3 - m, m)
        for start, target in ((second, other), (first, mine)):
            copies.append((store.at[0, :, layer, pl.ds(start, rows)], target.at[:, m]))
        copies.append((rate.at[layer, pl.ds(first, rows)], rate_m.at[m]))
    run_all([pltpu.make_async_copy(a, b, sems.at[i]) for i, (a, b) in enumerate(copies)])


def exact_dot(a, b):
    return jnp.dot(a, b, precision=lax.Precision.HIGHEST, preferred_element_type=jnp.float32)


def expand(scal, own, sib, vfine):
    core = scal[0]
    rows = vfine.shape[2]
    shift = rows - 2 * EDGE
    packed = own.shape[3]
    row = lax.broadcasted_iota(jnp.int32, (rows, 4 * packed), 0) + core * shift
    column = lax.broadcasted_iota(jnp.int32, (rows, 4 * packed), 1)
    coarse = row // 4
    pick_rows = (coarse == 4 * (column % packed) + column // packed).astype(jnp.float32)
    lane = lax.broadcasted_iota(jnp.int32, (128, 512), 0)
    z = lax.broadcasted_iota(jnp.int32, (128, 512), 1)
    pick_lanes = (lane == 32 * (z // 128) + (z % 128) // 4).astype(jnp.float32)
    for k in range(8):
        blocks = [(own if d < 2 else sib)[scal[3 + k], d % 2, scal[11 + k]] for d in range(4)]
        wide = exact_dot(jnp.concatenate(blocks, 0), pick_lanes)
        table = jnp.concatenate(
            [
                jnp.concatenate(
                    [wide[packed * d : packed * (d + 1), 128 * j : 128 * (j + 1)] for j in range(4)], 0
                )
                for d in range(4)
            ],
            1,
        )
        filled = exact_dot(pick_rows, table)
        for d in range(4):
            vfine[d, k] = filled[:, 128 * d : 128 * (d + 1)]


def masks(rows):
    lane = lax.broadcasted_iota(jnp.int32, (rows, 128), 1)
    return lane == 0, lane == 127


def around(ref, lead, layer, before, after, at, rows):
    first, last = masks(rows)
    here = ref[lead, layer, pl.ds(PAD + at, rows)]
    total = ref[lead, layer, pl.ds(PAD - 1 + at, rows)] + ref[lead, layer, pl.ds(PAD + 1 + at, rows)]
    total = total + jnp.where(first, 0.0, pltpu.roll(here, 1, 1))
    total = total + jnp.where(last, 0.0, pltpu.roll(here, 127, 1))
    total = total + ref[lead, after, pl.ds(PAD + at, rows)]
    return here, total, ref[lead, before, pl.ds(PAD + at, rows)]


def clear_pads(ref):
    dirs, layers, rows, lanes = ref.shape
    zero = jnp.zeros((dirs, PAD, lanes), jnp.float32)

    @pl.loop(0, layers)
    def _(i):
        ref[:, i, pl.ds(0, PAD)] = zero
        ref[:, i, pl.ds(rows - PAD, PAD)] = zero


def clear_layer(ref, layer):
    ref[:, layer] = jnp.zeros((ref.shape[0], ref.shape[2], ref.shape[3]), jnp.float32)


def update(source, target, field_at, state_at, out_at, sigma, fields, weight, rows):
    p_ref, q_ref = source
    p_out, q_out, pad = target
    for at, n in chunks(rows):
        a = fields[0, field_at, pl.ds(at, n)]
        b = fields[1, field_at, pl.ds(at, n)]
        hold_a = keep_a - b
        hold_b = keep_b + a
        for d in range(4):
            p, p_sum, p_back = around(p_ref, d, state_at, state_at - sigma, state_at + sigma, at, n)
            q, q_sum, q_back = around(q_ref, d, state_at, state_at - sigma, state_at + sigma, at, n)
            w = weight[d, field_at, pl.ds(at, n)]
            p_out[d, out_at, pl.ds(pad + at, n)] = (
                spread_a * (p_sum + back_a * p_back) + hold_a * p - (a * q + w)
            )
            q_out[d, out_at, pl.ds(pad + at, n)] = (
                spread_b * (q_sum + back_b * q_back) + hold_b * q + (b * p + w)
            )


def first_step(
    scal, rate_m, rate_e, rate_l, s_a, s_b, e_a, e_b, l_a, l_b, far_e, far_l, vfine,
    p3, q3, rate, slab, far, v, q1, p2, q2, sems,
):
    sigma = 1 - 2 * scal[1]
    has_late = scal[2]
    rows = rate.shape[1]
    moves = [(rate_m, rate.at[pl.ds(4, 4)])]
    moves += [(s_a, slab.at[:, pl.ds(4, 2)]), (s_b, slab.at[:, pl.ds(6, 2)])]
    for j in range(4):
        moves.append((rate_e.at[j], rate.at[11 - j]))
        moves.append((rate_l.at[j], rate.at[3 - j]))
    for j in range(2):
        moves.append((e_a.at[:, j], slab.at[:, 11 - j]))
        moves.append((e_b.at[:, j], slab.at[:, 9 - j]))
        moves.append((l_a.at[:, j], slab.at[:, 3 - j]))
        moves.append((l_b.at[:, j], slab.at[:, 1 - j]))
    moves += [(far_l, far.at[0]), (far_e, far.at[1]), (vfine, v)]
    copies = [pltpu.make_async_copy(a, b, sems.at[i]) for i, (a, b) in enumerate(moves)]
    for copy in copies:
        copy.start()
    for ref in (q1, p2, q2, p3, q3):
        clear_pads(ref)
    for ref in (p2, q2):
        clear_layer(ref, 3)
    for ref in (p3, q3):
        clear_layer(ref, 2)
    for copy in copies:
        copy.wait()

    for i, (layer, coarse) in enumerate(((0, 0), (13, 7))):
        for at, n in chunks(rows):
            w = far[i, pl.ds(at, n)]
            for d in range(4):
                q1[d, layer, pl.ds(PAD + at, n)] = w * v[d, coarse, pl.ds(at, n)]

    @pl.loop(0, 12)
    def _(i):
        coarse = (i + 2) // 2
        for at, n in chunks(rows):
            scaled = rate_scale * rate[i, pl.ds(at, n)]
            b = slab[1, i, pl.ds(at, n)]
            a = scaled * slab[0, i, pl.ds(at, n)]
            w = a * b
            slab[0, i, pl.ds(at, n)] = a
            slab[1, i, pl.ds(at, n)] = scaled * b
            for d in range(4):
                q1[d, i + 1, pl.ds(PAD + at, n)] = w * v[d, coarse, pl.ds(at, n)]

    @pl.loop(jnp.where(has_late == 1, 0, 4), 12)
    def _(i):
        for at, n in chunks(rows):
            both = slab[0, i, pl.ds(at, n)] - slab[1, i, pl.ds(at, n)]
            hold_a = both + (1.0 + keep_a)
            hold_b = both + (1.0 + keep_b)
            for d in range(4):
                q, total, back = around(q1, d, i + 1, i + 1 - sigma, i + 1 + sigma, at, n)
                p2[d, i, pl.ds(PAD + at, n)] = -(spread_a * (total + back_a * back) + hold_a * q)
                q2[d, i, pl.ds(PAD + at, n)] = spread_b * (total + back_b * back) + hold_b * q

    @pl.loop(jnp.where(has_late == 1, 0, 3), 10)
    def _(i):
        for at, n in chunks(rows):
            a = slab[0, i + 1, pl.ds(at, n)]
            b = slab[1, i + 1, pl.ds(at, n)]
            hold_a = keep_a - b
            hold_b = keep_b + a
            for d in range(4):
                p, p_sum, p_back = around(p2, d, i + 1, i + 1 - sigma, i + 1 + sigma, at, n)
                q, q_sum, q_back = around(q2, d, i + 1, i + 1 - sigma, i + 1 + sigma, at, n)
                w = q1[d, i + 2, pl.ds(PAD + at, n)]
                p3[d, i, pl.ds(PAD + at, n)] = (
                    spread_a * (p_sum + back_a * p_back) + hold_a * p - (a * q + w)
                )
                q3[d, i, pl.ds(PAD + at, n)] = (
                    spread_b * (q_sum + back_b * q_back) + hold_b * q + (b * p + w)
                )


def second_step(
    scal, rate_m, rate_e, rate_l, s_a, s_b, e_b, l_a, vfine, p3_in, q3_in,
    tangent, sent, means, rate, slab, v, p3, q3, weight, p4, q4, p5, q5, p6, q6, sems, out_sems,
):
    core, odd, has_late = scal[0], scal[1], scal[2]
    sigma = 1 - 2 * odd
    rows = rate.shape[1]
    half = rows - EDGE
    moves = [(p3_in, p3), (q3_in, q3), (rate_m, rate.at[pl.ds(2, 4)])]
    moves += [(s_a, slab.at[:, pl.ds(2, 2)]), (s_b, slab.at[:, pl.ds(4, 2)])]
    for j in range(2):
        moves.append((rate_e.at[3 - j], rate.at[6 + j]))
        moves.append((rate_l.at[j], rate.at[1 - j]))
        moves.append((e_b.at[:, 1 - j], slab.at[:, 6 + j]))
        moves.append((l_a.at[:, j], slab.at[:, 1 - j]))
    moves.append((vfine.at[:, pl.ds(2, 4)], v))
    copies = [pltpu.make_async_copy(a, b, sems.at[i]) for i, (a, b) in enumerate(moves)]
    for copy in copies:
        copy.start()
    for ref in (p4, q4, p5, q5):
        clear_pads(ref)
    for ref in (p4, q4):
        clear_layer(ref, 1)
    for ref in (p5, q5):
        clear_layer(ref, 0)
    for copy in copies:
        copy.wait()

    @pl.loop(0, 8)
    def _(i):
        coarse = i // 2
        for at, n in chunks(rows):
            scaled = rate_scale * rate[i, pl.ds(at, n)]
            b = slab[1, i, pl.ds(at, n)]
            a = scaled * slab[0, i, pl.ds(at, n)]
            w = a * b
            slab[0, i, pl.ds(at, n)] = a
            slab[1, i, pl.ds(at, n)] = scaled * b
            for d in range(4):
                weight[d, i, pl.ds(at, n)] = w * v[d, coarse, pl.ds(at, n)]

    @pl.loop(jnp.where(has_late == 1, 0, 2), 8)
    def _(i):
        update((p3, q3), (p4, q4, PAD), i, i + 1, i, sigma, slab, weight, rows)

    @pl.loop(jnp.where(has_late == 1, 0, 1), 6)
    def _(i):
        update((p4, q4), (p5, q5, PAD), i + 1, i + 1, i, sigma, slab, weight, rows)

    start = pl.multiple_of(core * EDGE, 8)
    place = pl.multiple_of(core * half, 8)

    def writes(i):
        layer = jnp.where(odd == 1, 3 - i, i)
        for j, ref in enumerate((p6, q6)):
            yield pltpu.make_async_copy(
                ref.at[pl.ds(0, 2), i, pl.ds(start, half)],
                tangent.at[:, j, layer, pl.ds(place, half)],
                out_sems.at[i, j],
            )
            yield pltpu.make_async_copy(
                ref.at[pl.ds(2, 2), i, pl.ds(start, half)],
                sent.at[:, j, layer],
                out_sems.at[i, 2 + j],
            )

    @pl.loop(0, 4)
    def _(i):
        update((p5, q5), (p6, q6, 0), i + 2, i + 1, i, sigma, slab, weight, rows)
        for copy in writes(i):
            copy.start()

    packed = half // 16
    row = lax.broadcasted_iota(jnp.int32, (4 * packed, half), 0)
    column = lax.broadcasted_iota(jnp.int32, (4 * packed, half), 1)
    sum_rows = (column // 4 == 4 * (row % packed) + row // packed).astype(jnp.float32)
    lane = lax.broadcasted_iota(jnp.int32, (512, 128), 1)
    z = lax.broadcasted_iota(jnp.int32, (512, 128), 0)
    sum_lanes = (lane == 32 * (z // 128) + (z % 128) // 4).astype(jnp.float32)
    pairs = [
        q6[d, 2 * k, pl.ds(start, half)] + q6[d, 2 * k + 1, pl.ds(start, half)]
        for d in range(4)
        for k in range(2)
    ]
    summed = exact_dot(sum_rows, jnp.concatenate(pairs, 1))
    spread = jnp.concatenate(
        [
            jnp.concatenate(
                [summed[packed * j : packed * (j + 1), 128 * i : 128 * (i + 1)] for j in range(4)], 1
            )
            for i in range(8)
        ],
        0,
    )
    total = exact_dot(spread, sum_lanes) * (1.0 / 32.0)
    for d in range(4):
        for k in range(2):
            layer = jnp.where(odd == 1, 1 - k, k)
            means[d, layer] = total[packed * (2 * d + k) : packed * (2 * d + k + 1)]

    @pl.loop(0, 4)
    def _(i):
        for copy in writes(i):
            copy.wait()


def finish(scal, held, received, tangent, stage, sems):
    half = received.shape[3]
    place = pl.multiple_of((1 - scal[0]) * half, 8)
    parts = [(i, j) for i in range(2) for j in range(2)]
    loads = [
        pltpu.make_async_copy(received.at[i, j], stage.at[i, j], sems.at[0, 2 * i + j]) for i, j in parts
    ]
    stores = [
        pltpu.make_async_copy(
            stage.at[i, j], tangent.at[i, j, :, pl.ds(place, half)], sems.at[1, 2 * i + j]
        )
        for i, j in parts
    ]
    for copy in loads:
        copy.start()
    for load, store in zip(loads, stores):
        load.wait()
        store.start()
    for copy in stores:
        copy.wait()


def cost(flops, moved):
    return pl.CostEstimate(flops=flops, bytes_accessed=moved, transcendentals=0)


def params(megabytes):
    return pltpu.CompilerParams(vmem_limit_bytes=megabytes << 20)


def shape(*dims):
    return jax.ShapeDtypeStruct(dims, jnp.float32)


def local(store, rate, directions, owner_map, block_map):
    layers, width_y, width_z = rate.shape
    half = width_y // 2
    rows = half + EDGE
    n_space = lax.axis_size("space")
    mine = lax.axis_index("space")
    group = lax.axis_index("dir")
    core, column = group % 2, group // 2
    odd = mine % 2
    has_late = ((mine > 0) & (mine < n_space - 1)).astype(jnp.int32)

    across_core = [(i, i ^ 1) for i in range(4)]
    across_column = [(i, i ^ 2) for i in range(4)]
    swap = [(i, i ^ 1) for i in range(n_space)]
    ahead = [(i, i + 2) for i in range(0, n_space - 2, 2)] + [(i, i - 2) for i in range(3, n_space, 2)]
    behind = [(b, a) for a, b in ahead]
    to_core = functools.partial(lax.ppermute, axis_name="dir", perm=across_core)
    to_column = functools.partial(lax.ppermute, axis_name="dir", perm=across_column)
    to_pair = functools.partial(lax.ppermute, axis_name="space", perm=swap)
    to_ahead = functools.partial(lax.ppermute, axis_name="space", perm=ahead)
    to_behind = functools.partial(lax.ppermute, axis_name="space", perm=behind)

    gathered = directions.reshape(1, 2, 2, 32, 128)
    reach = 1
    while reach < n_space:
        pairs = [(i, i ^ reach) for i in range(n_space)]
        gathered = jnp.concatenate([gathered, lax.ppermute(gathered, "space", pairs)], 0)
        reach *= 2
    gathered_sib = to_core(gathered)
    local_coarse = jnp.arange(8, dtype=jnp.int32) - 3
    coarse_at = 2 * mine + jnp.where(odd == 1, 1 - local_coarse, local_coarse)
    block = jnp.clip(coarse_at // 2, 0, n_space - 1)
    scal = jnp.concatenate(
        [
            jnp.stack([core, odd, has_late]).astype(jnp.int32),
            (block_map[block] ^ mine).astype(jnp.int32),
            (coarse_at % 2).astype(jnp.int32),
        ]
    )

    own, other, rate_m = pl.pallas_call(
        arrange,
        out_shape=(shape(2, 4, rows, width_z), shape(2, 4, rows, width_z), shape(4, rows, width_z)),
        in_specs=[SMEM, ANY, ANY],
        out_specs=[VMEM] * 3,
        cost_estimate=cost(0, 6 << 20),
        scratch_shapes=[pltpu.SemaphoreType.DMA((12,))],
        name="arrange",
    )(scal, store, rate)
    received = to_core(other)
    rate_e = to_pair(rate_m)
    rate_l = to_ahead(rate_e)

    def slab(step):
        owner = owner_map[step]
        parts = []
        for at in (0, 2):
            have = jnp.where(group == owner, own[:, at : at + 2], received[:, at : at + 2])
            came = to_column(have)
            parts.append(jnp.where(column == owner // 2, have, came))
        return parts

    s0_a, s0_b = slab(0)
    e0_a = to_pair(s0_a)
    e0_b = to_pair(s0_b)
    l0_a = to_ahead(e0_a)
    l0_b = to_ahead(e0_b)
    w_near = rate_scale * rate_m[0] * s0_a[0, 0] * s0_a[1, 0]
    w_late = rate_scale * rate_m[3] * s0_b[0, 1] * s0_b[1, 1]
    far_e = to_behind(w_near)
    far_l = to_ahead(w_late)
    s1_a, s1_b = slab(1)
    e1_a = to_pair(s1_a)
    l1_a = to_ahead(e1_a)
    e1_b = to_pair(s1_b)

    vfine = pl.pallas_call(
        expand,
        out_shape=shape(4, 8, rows, width_z),
        in_specs=[SMEM, VMEM, VMEM],
        out_specs=VMEM,
        name="expand",
        cost_estimate=cost(0, 25 << 20),
        compiler_params=params(32),
    )(scal, gathered, gathered_sib)

    tall = rows + 2 * PAD

    def vmem(*dims):
        return pltpu.VMEM(dims, jnp.float32)

    p3, q3 = pl.pallas_call(
        first_step,
        out_shape=(shape(4, 10, tall, width_z),) * 2,
        in_specs=[SMEM] + [ANY] * 12,
        out_specs=[VMEM] * 2,
        scratch_shapes=[
            vmem(12, rows, width_z),
            vmem(2, 12, rows, width_z),
            vmem(2, rows, width_z),
            vmem(4, 8, rows, width_z),
            vmem(4, 14, tall, width_z),
            vmem(4, 12, tall, width_z),
            vmem(4, 12, tall, width_z),
            pltpu.SemaphoreType.DMA((22,)),
        ],
        name="first_step",
        cost_estimate=cost(0, 50 << 20),
        compiler_params=params(50),
    )(scal, rate_m, rate_e, rate_l, s0_a, s0_b, e0_a, e0_b, l0_a, l0_b, far_e, far_l, vfine)

    tangent, sent, means = pl.pallas_call(
        second_step,
        out_shape=(
            shape(2, 2, 4, width_y, width_z),
            shape(2, 2, 4, half, width_z),
            shape(4, 2, half // 16, 128),
        ),
        in_specs=[SMEM] + [ANY] * 10,
        out_specs=[ANY, ANY, VMEM],
        scratch_shapes=[
            vmem(8, rows, width_z),
            vmem(2, 8, rows, width_z),
            vmem(4, 4, rows, width_z),
            vmem(4, 10, tall, width_z),
            vmem(4, 10, tall, width_z),
            vmem(4, 8, rows, width_z),
            vmem(4, 8, tall, width_z),
            vmem(4, 8, tall, width_z),
            vmem(4, 6, tall, width_z),
            vmem(4, 6, tall, width_z),
            vmem(4, 4, rows, width_z),
            vmem(4, 4, rows, width_z),
            pltpu.SemaphoreType.DMA((14,)),
            pltpu.SemaphoreType.DMA((4, 4)),
        ],
        name="second_step",
        cost_estimate=cost(0, 55 << 20),
        compiler_params=params(56),
    )(scal, rate_m, rate_e, rate_l, s1_a, s1_b, e1_b, l1_a, vfine, p3, q3)

    first, second = means[:2], means[2:]

    def joined(a, b):
        return jnp.where(core == 0, jnp.concatenate([a, b], 2), jnp.concatenate([b, a], 2))

    both = [(i * n_space + j, (i ^ 1) * n_space + (j ^ 1)) for i in range(4) for j in range(n_space)]
    here = joined(first, to_core(second))
    there = joined(to_pair(first), lax.ppermute(second, ("dir", "space"), both))
    partner = mine ^ 1
    source = jnp.argmax(block_map == mine).astype(jnp.int32)
    sens = jnp.where(source == mine, here, there)
    for j in range(2, n_space, 2):
        target = mine ^ j
        row = jnp.where(block_map[mine] == target, here, there)
        pairs = [(i, i ^ j) for i in range(n_space)]
        came = lax.ppermute(row, "space", pairs)
        sens = jnp.where(source // 2 == target // 2, came, sens)

    tangent = pl.pallas_call(
        finish,
        out_shape=shape(2, 2, 4, width_y, width_z),
        in_specs=[SMEM, ANY, ANY],
        out_specs=ANY,
        scratch_shapes=[vmem(2, 2, 4, half, width_z), pltpu.SemaphoreType.DMA((2, 4))],
        input_output_aliases={1: 0},
        cost_estimate=cost(0, 2 << 22),
        name="finish",
    )(scal, tangent, to_core(sent))
    return tangent, sens.reshape(2, 1, -1)


def solution(mesh):
    return jax.shard_map(
        local,
        mesh=mesh,
        in_specs=(
            P("dir", None, "space", None, None),
            P("space", None, None),
            P("dir", "space", None),
            P(),
            P(),
        ),
        out_specs=(P("dir", None, "space", None, None), P("dir", "space", None)),
        check_vma=False,
    )
```

time: 655 us -> 185 us (0.28)
  local copies, waits for them, and re-layouts: 189 us -> 10.9 us
  waiting for transfers between devices: 167 us -> 53.2 us
  other arithmetic: 116 us -> 4.16 us
  blocking collectives: 108 us -> 0 us
  Pallas kernels: 0 us -> 52 us
    ppermute x12 -> x27, waiting for transfers between devices: 166 us -> 53.2 us  [the longest x4 24.8 us: slab(): came = to_column(have)]
    all_gather x2 -> x0, blocking collectives: 108 us -> none  [the longest x1 66.8 us: local(): every = lax.all_gather(directions, 'space', axis=1, tiled=True)]
    reshape x1 -> x0, local copies, waits for them, and re-layouts: 70.6 us -> none  [local(): second.reshape(dirs_dev, width_x // 2, 2, width_y // 4, 4, width_z // 4, 4)]
    slice x41 -> x2, local copies, waits for them, and re-layouts: 63.8 us -> 1.38 us  [the longest x1 0.78 us: local(): first, second = (means[:2], means[2:])]
    sub x10 -> x0, other arithmetic: 55 us -> none  [the longest x5 29.9 us: advance(): second + spread_b * lap_second - drift * (second - second_lower) + source]
    pallas_call x0 -> x5, Pallas kernels: none -> 52 us  [the longest x1 19.8 us: local(): pl.pallas_call(second_step, out_shape=(shape(2, 2, 4, width_y, width_z),...]
    another operation x18 -> x1, other arithmetic: 36.4 us -> 0.66 us  [local(): source = jnp.argmax(block_map == mine).astype(jnp.int32)]
    reduce_sum x1 -> x0, other arithmetic: 20.8 us -> none  [local(): second.reshape(dirs_dev, width_x // 2, 2, width_y // 4, 4, width_z // 4, 4)]
  transfers between devices with their start and end apart: 13 -> 27, of which waited for: 6 -> 10; matrix products, arithmetic and copies ran while one was open for 7% -> 2% of each run, Pallas kernels for 0% -> 14%
where the time goes in v1:
time: 185 us
  waiting for transfers between devices  53.2 us (29%)
  Pallas kernels  52 us (28%)
  starting transfers between devices  51.8 us (28%)
  between operations  12.5 us (7%)
  local copies, waits for them, and re-layouts  10.9 us (6%)
  other arithmetic  4.16 us (2%)
    ppermute x4, waiting for transfers between devices, slab(): came = to_column(have)  24.8 us
    pallas_call x1, Pallas kernels, local(): pl.pallas_call(second_step, out_shape=(shape(2, 2, 4, width_y, width_z),...  19.8 us
    pallas_call x1, Pallas kernels, local(): pl.pallas_call(first_step, out_shape=(shape(4, 10, tall, width_z),) * 2,...  18.4 us
    ppermute x1, waiting for transfers between devices, local(): far_l = to_ahead(w_late)  13.2 us
    ppermute x2, starting transfers between devices, local(): there = joined(to_pair(first), lax.ppermute(second, ('dir', 'space'), both))  9.37 us
    unnamed x32, local copies, waits for them, and re-layouts  6.93 us
    pallas_call x1, Pallas kernels, local(): pl.pallas_call(expand, out_shape=shape(4, 8, rows, width_z), in_specs=[SM...  6.74 us
    ppermute x3, starting transfers between devices, local(): lax.ppermute(gathered, 'space', pairs)  5.75 us
  transfers between devices with their start and end apart: 27, of which 10 were waited for; matrix products, arithmetic and copies ran while one was open for 2% of the time, Pallas kernels for 14%

profile of v1, /device:TPU:0, one launch (start us, length us, event | category | flops | bytes accessed | tf_op | source)
XLA Modules:
  0.0 184.6 jit_solution(18210250422362404828)
XLA Ops:
  2.7 4.0 %arrange.1 = (f32[2,4,264,128]{3,2,1,0:T(8,128)}, f32[2,4,264,128]{3,2,1,0:T(8,128)}, f32[4,264,128]{2,1,0:T(8,128)}) custom-call(s32[19]{0:T(128)} %concatenate.26.scal, f32[1,2,4,512,128]{4,3,2,1,0:T(8,128)} %store.1, f32[4,512,128]{2,1,0:T(8,128)} %rate.1), custom_call_target="tpu_custom_call" | custom-call | bytes 6291456 | tf_op jit(solution)/shard_map/arrange/pallas_call | solution.py:396
  12.5 2.9 %collective-permute-start.12 = (f32[2,2,264,128]{3,2,1,0:T(8,128)S(1)}, f32[2,2,264,128]{3,2,1,0:T(8,128)}, u32[]{:S(2)}, u32[]{:S(2)}) collective-permute-start(f32[2,2,264,128]{3,2,1,0:T(8,128)S(1)} %get-tuple-element.25), channel_id=1, source_target_pairs={{0,16},{8,24},{16,0},{24,8},{1,17},{9,25},{17,1},{25,9},{2,18},{10... | collective-permute-start | bytes 1622024 | tf_op jit(solution)/shard_map/ppermute | solution.py:414
  17.5 2.2 %collective-permute-done.8 = f32[1,2,2,32,128]{4,3,2,1,0:T(8,128)S(1)} collective-permute-done((f32[1,2,2,32,128]{4,3,2,1,0:T(8,128)S(1)}, f32[1,2,2,32,128]{4,3,2,1,0:T(8,128)S(1)}, u32[]{:S(2)}, u32[]{:S(2)}) %collective-permute-start.8) | collective-permute-done | bytes 65568 | tf_op jit(solution)/shard_map/ppermute | solution.py:382
  29.2 2.7 %collective-permute-start.10 = (f32[4,2,2,32,128]{4,3,2,1,0:T(8,128)S(1)}, f32[4,2,2,32,128]{4,3,2,1,0:T(8,128)S(1)}, u32[]{:S(2)}, u32[]{:S(2)}) collective-permute-start(f32[4,2,2,32,128]{4,3,2,1,0:T(8,128)S(1)} %pad_maximum_fusion.1), channel_id=1, source_target_pairs={{0,4},{1,5},{2,6},{3,7},{4,0},{5,1},{6,2},{7,3},{8,12},{9,13},{10,... | collective-permute-start | bytes 786440 | tf_op jit(solution)/shard_map/ppermute | solution.py:382
  33.5 6.8 %collective-permute-done.13 = f32[2,2,264,128]{3,2,1,0:T(8,128)} collective-permute-done((f32[2,2,264,128]{3,2,1,0:T(8,128)S(1)}, f32[2,2,264,128]{3,2,1,0:T(8,128)}, u32[]{:S(2)}, u32[]{:S(2)}) %collective-permute-start.13) | collective-permute-done | bytes 540704 | tf_op jit(solution)/shard_map/ppermute | solution.py:414
  40.2 2.1 %collective-permute-start.14 = (f32[2,2,264,128]{3,2,1,0:T(8,128)S(1)}, f32[2,2,264,128]{3,2,1,0:T(8,128)S(1)}, u32[]{:S(2)}, u32[]{:S(2)}) collective-permute-start(f32[2,2,264,128]{3,2,1,0:T(8,128)S(1)} %broadcast_select_fusion.1.s_a), channel_id=1, source_target_pairs={{0,1},{1,0},{2,3},{3,2},{4,5},{5,4},{6,7},{7,6},{8,9},{9,8},{10,11... | collective-permute-start | bytes 1622024 | tf_op jit(solution)/shard_map/ppermute | solution.py:419
  42.4 9.3 %collective-permute-done.3 = f32[2,2,264,128]{3,2,1,0:T(8,128)S(1)} collective-permute-done((f32[2,2,264,128]{3,2,1,0:T(8,128)S(1)}, f32[2,2,264,128]{3,2,1,0:T(8,128)S(1)}, u32[]{:S(2)}, u32[]{:S(2)}) %collective-permute-start.3) | collective-permute-done | bytes 540704 | tf_op jit(solution)/shard_map/ppermute | solution.py:414
  51.7 2.1 %collective-permute-start.15 = (f32[2,2,264,128]{3,2,1,0:T(8,128)S(1)}, f32[2,2,264,128]{3,2,1,0:T(8,128)S(1)}, u32[]{:S(2)}, u32[]{:S(2)}) collective-permute-start(f32[2,2,264,128]{3,2,1,0:T(8,128)S(1)} %broadcast_select_fusion.s_b), channel_id=1, source_target_pairs={{0,1},{1,0},{2,3},{3,2},{4,5},{5,4},{6,7},{7,6},{8,9},{9,8},{10,11... | collective-permute-start | bytes 1622024 | tf_op jit(solution)/shard_map/ppermute | solution.py:420
  54.1 8.7 %collective-permute-done.4 = f32[2,2,264,128]{3,2,1,0:T(8,128)S(1)} collective-permute-done((f32[2,2,264,128]{3,2,1,0:T(8,128)S(1)}, f32[2,2,264,128]{3,2,1,0:T(8,128)S(1)}, u32[]{:S(2)}, u32[]{:S(2)}) %collective-permute-start.4) | collective-permute-done | bytes 540704 | tf_op jit(solution)/shard_map/ppermute | solution.py:414
  62.8 3.8 %collective-permute-start.1 = (f32[4,264,128]{2,1,0:T(8,128)S(1)}, f32[4,264,128]{2,1,0:T(8,128)S(1)}, u32[]{:S(2)}, u32[]{:S(2)}) collective-permute-start(f32[4,264,128]{2,1,0:T(8,128)S(1)} %collective-permute-done.rate_e), channel_id=1, source_target_pairs={{0,2},{2,4},{4,6},{3,1},{5,3},{7,5},{8,10},{10,12},{12,14},{11,9},... | collective-permute-start | bytes 1622024 | tf_op jit(solution)/shard_map/ppermute | solution.py:407
  66.6 3.5 %collective-permute-start.16 = (f32[2,2,264,128]{3,2,1,0:T(8,128)S(1)}, f32[2,2,264,128]{3,2,1,0:T(8,128)S(1)}, u32[]{:S(2)}, u32[]{:S(2)}) collective-permute-start(f32[2,2,264,128]{3,2,1,0:T(8,128)S(1)} %collective-permute-done.14.e_a), channel_id=1, source_target_pairs={{0,2},{2,4},{4,6},{3,1},{5,3},{7,5},{8,10},{10,12},{12,14},{11,9},... | collective-permute-start | bytes 1622024 | tf_op jit(solution)/shard_map/ppermute | solution.py:421
  70.1 3.5 %collective-permute-start.17 = (f32[2,2,264,128]{3,2,1,0:T(8,128)S(1)}, f32[2,2,264,128]{3,2,1,0:T(8,128)S(1)}, u32[]{:S(2)}, u32[]{:S(2)}) collective-permute-start(f32[2,2,264,128]{3,2,1,0:T(8,128)S(1)} %collective-permute-done.15.e_b), channel_id=1, source_target_pairs={{0,2},{2,4},{4,6},{3,1},{5,3},{7,5},{8,10},{10,12},{12,14},{11,9},... | collective-permute-start | bytes 1622024 | tf_op jit(solution)/shard_map/ppermute | solution.py:422
  73.7 4.8 %collective-permute-done.6 = f32[2,2,264,128]{3,2,1,0:T(8,128)S(1)} collective-permute-done((f32[2,2,264,128]{3,2,1,0:T(8,128)S(1)}, f32[2,2,264,128]{3,2,1,0:T(8,128)S(1)}, u32[]{:S(2)}, u32[]{:S(2)}) %collective-permute-start.6) | collective-permute-done | bytes 540704 | tf_op jit(solution)/shard_map/ppermute | solution.py:428
  78.6 4.0 %collective-permute-start.7 = (f32[2,2,264,128]{3,2,1,0:T(8,128)S(1)}, f32[2,2,264,128]{3,2,1,0:T(8,128)S(1)}, u32[]{:S(2)}, u32[]{:S(2)}) collective-permute-start(f32[2,2,264,128]{3,2,1,0:T(8,128)S(1)} %collective-permute-done.6), channel_id=1, source_target_pairs={{0,2},{2,4},{4,6},{3,1},{5,3},{7,5},{8,10},{10,12},{12,14},{11,9},... | collective-permute-start | bytes 1622024 | tf_op jit(solution)/shard_map/ppermute | solution.py:429
  83.9 5.6 %collective-permute-done.18.far_e = f32[264,128]{1,0:T(8,128)S(1)} collective-permute-done((f32[264,128]{1,0:T(8,128)S(1)}, f32[264,128]{1,0:T(8,128)S(1)}, u32[]{:S(2)}, u32[]{:S(2)}) %collective-permute-start.18) | collective-permute-done | bytes 135200 | tf_op jit(solution)/shard_map/ppermute | solution.py:425
  89.5 3.6 %collective-permute-start.19 = (f32[264,128]{1,0:T(8,128)S(1)}, f32[264,128]{1,0:T(8,128)S(1)}, u32[]{:S(2)}, u32[]{:S(2)}) collective-permute-start(f32[264,128]{1,0:T(8,128)S(1)} %get-tuple-element.28), channel_id=1, source_target_pairs={{0,2},{2,4},{4,6},{3,1},{5,3},{7,5},{8,10},{10,12},{12,14},{11,9},... | collective-permute-start | bytes 405512 | tf_op jit(solution)/shard_map/ppermute | solution.py:426
  93.2 6.7 %expand.1.vfine = f32[4,8,264,128]{3,2,1,0:T(8,128)S(1)} custom-call(s32[19]{0:T(128)S(1)} %copy-done.4, f32[8,2,2,32,128]{4,3,2,1,0:T(8,128)S(1)} %pad_maximum_fusion.own, f32[8,2,2,32,128]{4,3,2,1,0:T(8,128)S(1)} %collective-permute-done.11.sib), custom_call_target="tpu_custom_call" | custom-call | bytes 26214400 | tf_op jit(solution)/shard_map/expand/pallas_call | solution.py:432
  100.0 2.0 %copy-done = f32[4,8,264,128]{3,2,1,0:T(8,128)} copy-done((f32[4,8,264,128]{3,2,1,0:T(8,128)}, f32[4,8,264,128]{3,2,1,0:T(8,128)S(1)}, u32[]{:S(2)}) %copy-start) | copy-done | bytes 4325400
  101.9 13.2 %collective-permute-done.19.far_l = f32[264,128]{1,0:T(8,128)S(1)} collective-permute-done((f32[264,128]{1,0:T(8,128)S(1)}, f32[264,128]{1,0:T(8,128)S(1)}, u32[]{:S(2)}, u32[]{:S(2)}) %collective-permute-start.19) | collective-permute-done | bytes 135200 | tf_op jit(solution)/shard_map/ppermute | solution.py:426
  116.8 18.4 %first_step.1 = (f32[4,10,280,128]{3,2,1,0:T(8,128)}, f32[4,10,280,128]{3,2,1,0:T(8,128)}) custom-call(s32[19]{0:T(128)S(1)} %copy-done.4, f32[4,264,128]{2,1,0:T(8,128)S(1)} %copy-done.1, f32[4,264,128]{2,1,0:T(8,128)S(1)} %collective-permute-done.rate_e, f32[4,264,128]{2,1,0:T(8,128)S(1)} %collective-permute-done.1.rate_l, ...), custom_call_target="tpu_custom_call" | custom-call | bytes 52428800 | tf_op jit(solution)/shard_map/first_step/pallas_call | solution.py:447
  136.2 19.8 %second_step.1 = (f32[2,2,4,512,128]{4,3,2,1,0:T(8,128)}, f32[2,2,4,256,128]{4,3,2,1,0:T(8,128)}, f32[4,2,16,128]{3,2,1,0:T(8,128)}) custom-call(s32[19]{0:T(128)} %concatenate.26.scal, f32[4,264,128]{2,1,0:T(8,128)} %get-tuple-element.11.rate_m, f32[4,264,128]{2,1,0:T(8,128)} %copy-done.2, f32[4,264,128]{2,1,0:T(8,128)} %copy-done.3, ...), custom_call_target="tpu_custom_call" | custom-call | bytes 57671680 | tf_op jit(solution)/shard_map/second_step/pallas_call | solution.py:467
  157.4 9.4 %collective-permute-start.22 = (f32[2,2,16,128]{3,2,1,0:T(8,128)S(1)}, f32[2,2,16,128]{3,2,1,0:T(8,128)S(1)}, u32[]{:S(2)}, u32[]{:S(2)}) collective-permute-start(f32[2,2,16,128]{3,2,1,0:T(8,128)S(1)} %get-tuple-element.33), channel_id=1, source_target_pairs={{0,1},{1,0},{2,3},{3,2},{4,5},{5,4},{6,7},{7,6},{8,9},{9,8},{10,11... | collective-permute-start | bytes 98312 | tf_op jit(solution)/shard_map/ppermute | solution.py:504
  170.5 2.7 %collective-permute-start.25 = (f32[2,2,32,128]{3,2,1,0:T(8,128)S(1)}, f32[2,2,32,128]{3,2,1,0:T(8,128)S(1)}, u32[]{:S(2)}, u32[]{:S(2)}) collective-permute-start(f32[2,2,32,128]{3,2,1,0:T(8,128)S(1)} %get-tuple-element.31), channel_id=1, source_target_pairs={{0,4},{1,5},{2,6},{3,7},{4,0},{5,1},{6,2},{7,3},{8,12},{9,13},{10,... | collective-permute-start | bytes 196616 | tf_op jit(solution)/shard_map/ppermute | solution.py:512
  181.4 3.1 %finish.1 = f32[2,2,4,512,128]{4,3,2,1,0:T(8,128)} custom-call(s32[19]{0:T(128)} %concatenate.26.scal, f32[2,2,4,512,128]{4,3,2,1,0:T(8,128)} %get-tuple-element.16.held, f32[2,2,4,256,128]{4,3,2,1,0:T(8,128)} %copy-done.8), custom_call_target="tpu_custom_call", output_to_operand_aliasing={{}: (1, {})} | custom-call | bytes 8388608 | tf_op jit(solution)/shard_map/finish/pallas_call | solution.py:515
  (88 shorter events, 27.3 us)
Async XLA Ops:
  12.5 19.4 %collective-permute-start.12 = (f32[2,2,264,128]{3,2,1,0:T(8,128)S(1)}, f32[2,2,264,128]{3,2,1,0:T(8,128)}, u32[]{:S(2)}, u32[]{:S(2)}) collective-permute-start(f32[2,2,264,128]{3,2,1,0:T(8,128)S(1)} %get-tuple-element.25), channel_id=1, source_target_pairs={{0,16},{8,24},{16,0},{24,8},{1,17},{9,25},{17,1},{25,9},{2,18},{10... | collective-permute-start | bytes 1622024 | tf_op jit(solution)/shard_map/ppermute | solution.py:414
  17.0 23.2 %collective-permute-start.13 = (f32[2,2,264,128]{3,2,1,0:T(8,128)S(1)}, f32[2,2,264,128]{3,2,1,0:T(8,128)}, u32[]{:S(2)}, u32[]{:S(2)}) collective-permute-start(f32[2,2,264,128]{3,2,1,0:T(8,128)S(1)} %get-tuple-element.24), channel_id=1, source_target_pairs={{0,16},{8,24},{16,0},{24,8},{1,17},{9,25},{17,1},{25,9},{2,18},{10... | collective-permute-start | bytes 1622024 | tf_op jit(solution)/shard_map/ppermute | solution.py:414
  20.4 8.8 %collective-permute-start.9 = (f32[2,2,2,32,128]{4,3,2,1,0:T(8,128)}, f32[2,2,2,32,128]{4,3,2,1,0:T(8,128)S(1)}, u32[]{:S(2)}, u32[]{:S(2)}) collective-permute-start(f32[2,2,2,32,128]{4,3,2,1,0:T(8,128)} %pad_maximum_fusion.2), channel_id=1, source_target_pairs={{0,2},{1,3},{2,0},{3,1},{4,6},{5,7},{6,4},{7,5},{8,10},{9,11},{10,... | collective-permute-start | bytes 393224 | tf_op jit(solution)/shard_map/ppermute | solution.py:382
  22.0 32.0 %collective-permute-start = (f32[4,264,128]{2,1,0:T(8,128)S(1)}, f32[4,264,128]{2,1,0:T(8,128)S(1)}, u32[]{:S(2)}, u32[]{:S(2)}) collective-permute-start(f32[4,264,128]{2,1,0:T(8,128)S(1)} %copy-done.1), channel_id=1, source_target_pairs={{0,1},{1,0},{2,3},{3,2},{4,5},{5,4},{6,7},{7,6},{8,9},{9,8},{10,11... | collective-permute-start | bytes 1622024 | tf_op jit(solution)/shard_map/ppermute | solution.py:406
  28.6 23.1 %collective-permute-start.3 = (f32[2,2,264,128]{3,2,1,0:T(8,128)S(1)}, f32[2,2,264,128]{3,2,1,0:T(8,128)S(1)}, u32[]{:S(2)}, u32[]{:S(2)}) collective-permute-start(f32[2,2,264,128]{3,2,1,0:T(8,128)S(1)} %get-tuple-element.27), channel_id=1, source_target_pairs={{0,16},{8,24},{16,0},{24,8},{1,17},{9,25},{17,1},{25,9},{2,18},{10... | collective-permute-start | bytes 1622024 | tf_op jit(solution)/shard_map/ppermute | solution.py:414
  29.2 24.6 %collective-permute-start.10 = (f32[4,2,2,32,128]{4,3,2,1,0:T(8,128)S(1)}, f32[4,2,2,32,128]{4,3,2,1,0:T(8,128)S(1)}, u32[]{:S(2)}, u32[]{:S(2)}) collective-permute-start(f32[4,2,2,32,128]{4,3,2,1,0:T(8,128)S(1)} %pad_maximum_fusion.1), channel_id=1, source_target_pairs={{0,4},{1,5},{2,6},{3,7},{4,0},{5,1},{6,2},{7,3},{8,12},{9,13},{10,... | collective-permute-start | bytes 786440 | tf_op jit(solution)/shard_map/ppermute | solution.py:382
  31.9 30.9 %collective-permute-start.4 = (f32[2,2,264,128]{3,2,1,0:T(8,128)S(1)}, f32[2,2,264,128]{3,2,1,0:T(8,128)S(1)}, u32[]{:S(2)}, u32[]{:S(2)}) collective-permute-start(f32[2,2,264,128]{3,2,1,0:T(8,128)S(1)} %get-tuple-element.26), channel_id=1, source_target_pairs={{0,16},{8,24},{16,0},{24,8},{1,17},{9,25},{17,1},{25,9},{2,18},{10... | collective-permute-start | bytes 1622024 | tf_op jit(solution)/shard_map/ppermute | solution.py:414
  40.2 26.4 %collective-permute-start.14 = (f32[2,2,264,128]{3,2,1,0:T(8,128)S(1)}, f32[2,2,264,128]{3,2,1,0:T(8,128)S(1)}, u32[]{:S(2)}, u32[]{:S(2)}) collective-permute-start(f32[2,2,264,128]{3,2,1,0:T(8,128)S(1)} %broadcast_select_fusion.1.s_a), channel_id=1, source_target_pairs={{0,1},{1,0},{2,3},{3,2},{4,5},{5,4},{6,7},{7,6},{8,9},{9,8},{10,11... | collective-permute-start | bytes 1622024 | tf_op jit(solution)/shard_map/ppermute | solution.py:419
  51.7 18.5 %collective-permute-start.15 = (f32[2,2,264,128]{3,2,1,0:T(8,128)S(1)}, f32[2,2,264,128]{3,2,1,0:T(8,128)S(1)}, u32[]{:S(2)}, u32[]{:S(2)}) collective-permute-start(f32[2,2,264,128]{3,2,1,0:T(8,128)S(1)} %broadcast_select_fusion.s_b), channel_id=1, source_target_pairs={{0,1},{1,0},{2,3},{3,2},{4,5},{5,4},{6,7},{7,6},{8,9},{9,8},{10,11... | collective-permute-start | bytes 1622024 | tf_op jit(solution)/shard_map/ppermute | solution.py:420
  53.9 24.7 %collective-permute-start.6 = (f32[2,2,264,128]{3,2,1,0:T(8,128)S(1)}, f32[2,2,264,128]{3,2,1,0:T(8,128)S(1)}, u32[]{:S(2)}, u32[]{:S(2)}) collective-permute-start(f32[2,2,264,128]{3,2,1,0:T(8,128)S(1)} %broadcast_select_fusion.3.s_a), channel_id=1, source_target_pairs={{0,1},{1,0},{2,3},{3,2},{4,5},{5,4},{6,7},{7,6},{8,9},{9,8},{10,11... | collective-permute-start | bytes 1622024 | tf_op jit(solution)/shard_map/ppermute | solution.py:428
  54.0 19.6 %collective-permute-start.11 = (f32[8,2,2,32,128]{4,3,2,1,0:T(8,128)S(1)}, f32[8,2,2,32,128]{4,3,2,1,0:T(8,128)S(1)}, u32[]{:S(2)}, u32[]{:S(2)}) collective-permute-start(f32[8,2,2,32,128]{4,3,2,1,0:T(8,128)S(1)} %pad_maximum_fusion.own), channel_id=1, source_target_pairs={{0,8},{8,0},{16,24},{24,16},{1,9},{9,1},{17,25},{25,17},{2,10},{10... | collective-permute-start | bytes 1572872 | tf_op jit(solution)/shard_map/ppermute | solution.py:384
  62.8 19.8 %collective-permute-start.1 = (f32[4,264,128]{2,1,0:T(8,128)S(1)}, f32[4,264,128]{2,1,0:T(8,128)S(1)}, u32[]{:S(2)}, u32[]{:S(2)}) collective-permute-start(f32[4,264,128]{2,1,0:T(8,128)S(1)} %collective-permute-done.rate_e), channel_id=1, source_target_pairs={{0,2},{2,4},{4,6},{3,1},{5,3},{7,5},{8,10},{10,12},{12,14},{11,9},... | collective-permute-start | bytes 1622024 | tf_op jit(solution)/shard_map/ppermute | solution.py:407
  66.6 48.5 %collective-permute-start.16 = (f32[2,2,264,128]{3,2,1,0:T(8,128)S(1)}, f32[2,2,264,128]{3,2,1,0:T(8,128)S(1)}, u32[]{:S(2)}, u32[]{:S(2)}) collective-permute-start(f32[2,2,264,128]{3,2,1,0:T(8,128)S(1)} %collective-permute-done.14.e_a), channel_id=1, source_target_pairs={{0,2},{2,4},{4,6},{3,1},{5,3},{7,5},{8,10},{10,12},{12,14},{11,9},... | collective-permute-start | bytes 1622024 | tf_op jit(solution)/shard_map/ppermute | solution.py:421
  70.1 45.0 %collective-permute-start.17 = (f32[2,2,264,128]{3,2,1,0:T(8,128)S(1)}, f32[2,2,264,128]{3,2,1,0:T(8,128)S(1)}, u32[]{:S(2)}, u32[]{:S(2)}) collective-permute-start(f32[2,2,264,128]{3,2,1,0:T(8,128)S(1)} %collective-permute-done.15.e_b), channel_id=1, source_target_pairs={{0,2},{2,4},{4,6},{3,1},{5,3},{7,5},{8,10},{10,12},{12,14},{11,9},... | collective-permute-start | bytes 1622024 | tf_op jit(solution)/shard_map/ppermute | solution.py:422
  73.7 61.6 %collective-permute-start.5 = (f32[2,2,264,128]{3,2,1,0:T(8,128)S(1)}, f32[2,2,264,128]{3,2,1,0:T(8,128)S(1)}, u32[]{:S(2)}, u32[]{:S(2)}) collective-permute-start(f32[2,2,264,128]{3,2,1,0:T(8,128)S(1)} %broadcast_select_fusion.2.s_b), channel_id=1, source_target_pairs={{0,1},{1,0},{2,3},{3,2},{4,5},{5,4},{6,7},{7,6},{8,9},{9,8},{10,11... | collective-permute-start | bytes 1622024 | tf_op jit(solution)/shard_map/ppermute | solution.py:430
  78.6 56.7 %collective-permute-start.7 = (f32[2,2,264,128]{3,2,1,0:T(8,128)S(1)}, f32[2,2,264,128]{3,2,1,0:T(8,128)S(1)}, u32[]{:S(2)}, u32[]{:S(2)}) collective-permute-start(f32[2,2,264,128]{3,2,1,0:T(8,128)S(1)} %collective-permute-done.6), channel_id=1, source_target_pairs={{0,2},{2,4},{4,6},{3,1},{5,3},{7,5},{8,10},{10,12},{12,14},{11,9},... | collective-permute-start | bytes 1622024 | tf_op jit(solution)/shard_map/ppermute | solution.py:429
  82.6 6.9 %collective-permute-start.18 = (f32[264,128]{1,0:T(8,128)S(1)}, f32[264,128]{1,0:T(8,128)S(1)}, u32[]{:S(2)}, u32[]{:S(2)}) collective-permute-start(f32[264,128]{1,0:T(8,128)S(1)} %get-tuple-element.29), channel_id=1, source_target_pairs={{2,0},{4,2},{6,4},{1,3},{3,5},{5,7},{10,8},{12,10},{14,12},{9,11},... | collective-permute-start | bytes 405512 | tf_op jit(solution)/shard_map/ppermute | solution.py:425
  89.5 25.6 %collective-permute-start.19 = (f32[264,128]{1,0:T(8,128)S(1)}, f32[264,128]{1,0:T(8,128)S(1)}, u32[]{:S(2)}, u32[]{:S(2)}) collective-permute-start(f32[264,128]{1,0:T(8,128)S(1)} %get-tuple-element.28), channel_id=1, source_target_pairs={{0,2},{2,4},{4,6},{3,1},{5,3},{7,5},{8,10},{10,12},{12,14},{11,9},... | collective-permute-start | bytes 405512 | tf_op jit(solution)/shard_map/ppermute | solution.py:426
  156.1 24.0 %collective-permute-start.20 = (f32[2,2,4,256,128]{4,3,2,1,0:T(8,128)}, f32[2,2,4,256,128]{4,3,2,1,0:T(8,128)S(1)}, u32[]{:S(2)}, u32[]{:S(2)}) collective-permute-start(f32[2,2,4,256,128]{4,3,2,1,0:T(8,128)} %get-tuple-element.17), channel_id=1, source_target_pairs={{0,8},{8,0},{16,24},{24,16},{1,9},{9,1},{17,25},{25,17},{2,10},{10... | collective-permute-start | bytes 6291464 | tf_op jit(solution)/shard_map/ppermute | solution.py:524
  156.9 12.4 %collective-permute-start.21 = (f32[2,2,16,128]{3,2,1,0:T(8,128)S(1)}, f32[2,2,16,128]{3,2,1,0:T(8,128)S(1)}, u32[]{:S(2)}, u32[]{:S(2)}) collective-permute-start(f32[2,2,16,128]{3,2,1,0:T(8,128)S(1)} %get-tuple-element.32), channel_id=1, source_target_pairs={{0,8},{8,0},{16,24},{24,16},{1,9},{9,1},{17,25},{25,17},{2,10},{10... | collective-permute-start | bytes 98312 | tf_op jit(solution)/shard_map/ppermute | solution.py:503
  157.4 11.9 %collective-permute-start.22 = (f32[2,2,16,128]{3,2,1,0:T(8,128)S(1)}, f32[2,2,16,128]{3,2,1,0:T(8,128)S(1)}, u32[]{:S(2)}, u32[]{:S(2)}) collective-permute-start(f32[2,2,16,128]{3,2,1,0:T(8,128)S(1)} %get-tuple-element.33), channel_id=1, source_target_pairs={{0,1},{1,0},{2,3},{3,2},{4,5},{5,4},{6,7},{7,6},{8,9},{9,8},{10,11... | collective-permute-start | bytes 98312 | tf_op jit(solution)/shard_map/ppermute | solution.py:504
  170.5 8.1 %collective-permute-start.25 = (f32[2,2,32,128]{3,2,1,0:T(8,128)S(1)}, f32[2,2,32,128]{3,2,1,0:T(8,128)S(1)}, u32[]{:S(2)}, u32[]{:S(2)}) collective-permute-start(f32[2,2,32,128]{3,2,1,0:T(8,128)S(1)} %get-tuple-element.31), channel_id=1, source_target_pairs={{0,4},{1,5},{2,6},{3,7},{4,0},{5,1},{6,2},{7,3},{8,12},{9,13},{10,... | collective-permute-start | bytes 196616 | tf_op jit(solution)/shard_map/ppermute | solution.py:512
  173.1 5.5 %collective-permute-start.26 = (f32[2,2,32,128]{3,2,1,0:T(8,128)S(1)}, f32[2,2,32,128]{3,2,1,0:T(8,128)S(1)}, u32[]{:S(2)}, u32[]{:S(2)}) collective-permute-start(f32[2,2,32,128]{3,2,1,0:T(8,128)S(1)} %get-tuple-element.30), channel_id=1, source_target_pairs={{0,2},{1,3},{2,0},{3,1},{4,6},{5,7},{6,4},{7,5},{8,10},{9,11},{10,... | collective-permute-start | bytes 196616 | tf_op jit(solution)/shard_map/ppermute | solution.py:512
  173.1 6.3 %collective-permute-start.24 = (f32[2,2,32,128]{3,2,1,0:T(8,128)S(1)}, f32[2,2,32,128]{3,2,1,0:T(8,128)S(1)}, u32[]{:S(2)}, u32[]{:S(2)}) collective-permute-start(f32[2,2,32,128]{3,2,1,0:T(8,128)S(1)} %broadcast_select_fusion.6), channel_id=1, source_target_pairs={{0,6},{1,7},{2,4},{3,5},{4,2},{5,3},{6,0},{7,1},{8,14},{9,15},{10,... | collective-permute-start | bytes 196616 | tf_op jit(solution)/shard_map/ppermute | solution.py:512
  (19 other events, 284.3 us)

commit v2 on v1

--- a/solution.py
+++ b/solution.py
@@ -135,11 +135,12 @@
 
 
 def first_step(
-    scal, rate_m, rate_e, rate_l, s_a, s_b, e_a, e_b, l_a, l_b, far_e, far_l, vfine,
-    p3, q3, rate, slab, far, v, q1, p2, q2, sems,
+    scal, rate_m, rate_e, rate_l, s_a, s_b, e_a, e_b, l_a, l_b, far_e, far_l, v,
+    state, rate, slab, far, q1, p2, q2, sems,
 ):
     sigma = 1 - 2 * scal[1]
     has_late = scal[2]
+    p3, q3 = state.at[0], state.at[1]
     rows = rate.shape[1]
     moves = [(rate_m, rate.at[pl.ds(4, 4)])]
     moves += [(s_a, slab.at[:, pl.ds(4, 2)]), (s_b, slab.at[:, pl.ds(6, 2)])]
@@ -151,7 +152,7 @@
         moves.append((e_b.at[:, j], slab.at[:, 9 - j]))
         moves.append((l_a.at[:, j], slab.at[:, 3 - j]))
         moves.append((l_b.at[:, j], slab.at[:, 1 - j]))
-    moves += [(far_l, far.at[0]), (far_e, far.at[1]), (vfine, v)]
+    moves += [(far_l, far.at[0]), (far_e, far.at[1])]
     copies = [pltpu.make_async_copy(a, b, sems.at[i]) for i, (a, b) in enumerate(moves)]
     for copy in copies:
         copy.start()
@@ -214,21 +215,21 @@
 
 
 def second_step(
-    scal, rate_m, rate_e, rate_l, s_a, s_b, e_b, l_a, vfine, p3_in, q3_in,
-    tangent, sent, means, rate, slab, v, p3, q3, weight, p4, q4, p5, q5, p6, q6, sems, out_sems,
+    scal, rate_m, rate_e, rate_l, s_a, s_b, e_b, l_a, v, state,
+    tangent, sent, means, rate, slab, weight, p4, q4, p5, q5, p6, q6, sems, out_sems,
 ):
     core, odd, has_late = scal[0], scal[1], scal[2]
     sigma = 1 - 2 * odd
     rows = rate.shape[1]
     half = rows - EDGE
-    moves = [(p3_in, p3), (q3_in, q3), (rate_m, rate.at[pl.ds(2, 4)])]
+    p3, q3 = state.at[0], state.at[1]
+    moves = [(rate_m, rate.at[pl.ds(2, 4)])]
     moves += [(s_a, slab.at[:, pl.ds(2, 2)]), (s_b, slab.at[:, pl.ds(4, 2)])]
     for j in range(2):
         moves.append((rate_e.at[3 - j], rate.at[6 + j]))
         moves.append((rate_l.at[j], rate.at[1 - j]))
         moves.append((e_b.at[:, 1 - j], slab.at[:, 6 + j]))
         moves.append((l_a.at[:, j], slab.at[:, 1 - j]))
-    moves.append((vfine.at[:, pl.ds(2, 4)], v))
     copies = [pltpu.make_async_copy(a, b, sems.at[i]) for i, (a, b) in enumerate(moves)]
     for copy in copies:
         copy.start()
@@ -243,7 +244,7 @@
 
     @pl.loop(0, 8)
     def _(i):
-        coarse = i // 2
+        coarse = i // 2 + 2
         for at, n in chunks(rows):
             scaled = rate_scale * rate[i, pl.ds(at, n)]
             b = slab[1, i, pl.ds(at, n)]
@@ -319,34 +320,38 @@
             copy.wait()
 
 
-def finish(scal, held, received, tangent, stage, sems):
+def finish(scal, held, received, tangent, sems):
     half = received.shape[3]
     place = pl.multiple_of((1 - scal[0]) * half, 8)
-    parts = [(i, j) for i in range(2) for j in range(2)]
-    loads = [
-        pltpu.make_async_copy(received.at[i, j], stage.at[i, j], sems.at[0, 2 * i + j]) for i, j in parts
-    ]
-    stores = [
-        pltpu.make_async_copy(
-            stage.at[i, j], tangent.at[i, j, :, pl.ds(place, half)], sems.at[1, 2 * i + j]
-        )
-        for i, j in parts
-    ]
-    for copy in loads:
-        copy.start()
-    for load, store in zip(loads, stores):
-        load.wait()
-        store.start()
-    for copy in stores:
-        copy.wait()
+    run_all(
+        [
+            pltpu.make_async_copy(
+                received.at[i, j], tangent.at[i, j, :, pl.ds(place, half)], sems.at[i, j]
+            )
+            for i in range(2)
+            for j in range(2)
+        ]
+    )
 
 
 def cost(flops, moved):
     return pl.CostEstimate(flops=flops, bytes_accessed=moved, transcendentals=0)
 
 
+def after(value, *others):
+    return lax.optimization_barrier((value, *others))[0]
+
+
 def params(megabytes):
     return pltpu.CompilerParams(vmem_limit_bytes=megabytes << 20)
+
+
+def stay(value):
+    return pltpu.with_memory_space_constraint(value, pltpu.VMEM)
+
+
+def vmem(*dims):
+    return pltpu.VMEM(dims, jnp.float32)
 
 
 def shape(*dims):
@@ -363,6 +368,7 @@
     core, column = group % 2, group // 2
     odd = mine % 2
     has_late = ((mine > 0) & (mine < n_space - 1)).astype(jnp.int32)
+    scal = jnp.stack([core, odd, has_late]).astype(jnp.int32)
 
     across_core = [(i, i ^ 1) for i in range(4)]
     across_column = [(i, i ^ 2) for i in range(4)]
@@ -375,24 +381,6 @@
     to_ahead = functools.partial(lax.ppermute, axis_name="space", perm=ahead)
     to_behind = functools.partial(lax.ppermute, axis_name="space", perm=behind)
 
-    gathered = directions.reshape(1, 2, 2, 32, 128)
-    reach = 1
-    while reach < n_space:
-        pairs = [(i, i ^ reach) for i in range(n_space)]
-        gathered = jnp.concatenate([gathered, lax.ppermute(gathered, "space", pairs)], 0)
-        reach *= 2
-    gathered_sib = to_core(gathered)
-    local_coarse = jnp.arange(8, dtype=jnp.int32) - 3
-    coarse_at = 2 * mine + jnp.where(odd == 1, 1 - local_coarse, local_coarse)
-    block = jnp.clip(coarse_at // 2, 0, n_space - 1)
-    scal = jnp.concatenate(
-        [
-            jnp.stack([core, odd, has_late]).astype(jnp.int32),
-            (block_map[block] ^ mine).astype(jnp.int32),
-            (coarse_at % 2).astype(jnp.int32),
-        ]
-    )
-
     own, other, rate_m = pl.pallas_call(
         arrange,
         out_shape=(shape(2, 4, rows, width_z), shape(2, 4, rows, width_z), shape(4, rows, width_z)),
@@ -402,67 +390,98 @@
         scratch_shapes=[pltpu.SemaphoreType.DMA((12,))],
         name="arrange",
     )(scal, store, rate)
-    received = to_core(other)
-    rate_e = to_pair(rate_m)
-    rate_l = to_ahead(rate_e)
-
-    def slab(step):
-        owner = owner_map[step]
-        parts = []
-        for at in (0, 2):
-            have = jnp.where(group == owner, own[:, at : at + 2], received[:, at : at + 2])
-            came = to_column(have)
-            parts.append(jnp.where(column == owner // 2, have, came))
-        return parts
-
-    s0_a, s0_b = slab(0)
-    e0_a = to_pair(s0_a)
-    e0_b = to_pair(s0_b)
-    l0_a = to_ahead(e0_a)
-    l0_b = to_ahead(e0_b)
-    w_near = rate_scale * rate_m[0] * s0_a[0, 0] * s0_a[1, 0]
-    w_late = rate_scale * rate_m[3] * s0_b[0, 1] * s0_b[1, 1]
-    far_e = to_behind(w_near)
-    far_l = to_ahead(w_late)
-    s1_a, s1_b = slab(1)
-    e1_a = to_pair(s1_a)
-    l1_a = to_ahead(e1_a)
-    e1_b = to_pair(s1_b)
+    with jax.named_scope("store_core"):
+        received = to_core(other)
+    gathered = after(directions, rate_m).reshape(1, 2, 2, 32, 128)
+    reach = 1
+    while reach < n_space:
+        pairs = [(i, i ^ reach) for i in range(n_space)]
+        with jax.named_scope("directions_space"):
+            gathered = jnp.concatenate([gathered, lax.ppermute(gathered, "space", pairs)], 0)
+        if reach == 1:
+            near = gathered
+        reach *= 2
+    with jax.named_scope("directions_core"):
+        gathered_sib = to_core(gathered)
+    local_coarse = jnp.arange(8, dtype=jnp.int32) - 3
+    coarse_at = 2 * mine + jnp.where(odd == 1, 1 - local_coarse, local_coarse)
+    block = jnp.clip(coarse_at // 2, 0, n_space - 1)
+    coarse_scal = jnp.concatenate(
+        [scal, (block_map[block] ^ mine).astype(jnp.int32), (coarse_at % 2).astype(jnp.int32)]
+    )
 
     vfine = pl.pallas_call(
         expand,
-        out_shape=shape(4, 8, rows, width_z),
+        out_shape=vmem(4, 8, rows, width_z),
         in_specs=[SMEM, VMEM, VMEM],
         out_specs=VMEM,
         name="expand",
         cost_estimate=cost(0, 25 << 20),
-        compiler_params=params(32),
-    )(scal, gathered, gathered_sib)
+        compiler_params=params(16),
+    )(coarse_scal, gathered, gathered_sib)
+    with jax.named_scope("rate_pair"):
+        rate_e = to_pair(after(rate_m, near))
+    with jax.named_scope("rate_ahead"):
+        rate_l = to_ahead(after(rate_e, gathered))
+
+    def candidates(step, received):
+        owner = owner_map[step]
+        return [jnp.where(group == owner, own[:, at : at + 2], received[:, at : at + 2]) for at in (0, 2)]
+
+    def settled(step, have, came):
+        return jnp.where(column == owner_map[step] // 2, have, came)
+
+    have0_a, have0_b = candidates(0, received)
+    with jax.named_scope("slab0_column"):
+        came0_a = to_column(have0_a)
+        came0_b = to_column(after(have0_b, came0_a))
+    have1_a, have1_b = candidates(1, after(received, have0_a, rate_e))
+    s0_a = settled(0, have0_a, came0_a)
+    with jax.named_scope("slab0_pair"):
+        e0_a = to_pair(after(s0_a, rate_e))
+    s0_b = settled(0, have0_b, came0_b)
+    w_near = rate_scale * rate_m[0] * s0_a[0, 0] * s0_a[1, 0]
+    w_late = rate_scale * rate_m[3] * s0_b[0, 1] * s0_b[1, 1]
+    with jax.named_scope("far_layers"):
+        far_e = to_behind(w_near)
+        far_l = to_ahead(w_late)
+    with jax.named_scope("slab1_column"):
+        came1_a = to_column(after(have1_a, came0_b, vfine))
+        came1_b = to_column(after(have1_b, came1_a, far_e, far_l))
+    with jax.named_scope("slab0_pair"):
+        e0_b = to_pair(after(s0_b, e0_a))
+    with jax.named_scope("slab0_ahead"):
+        l0_a = to_ahead(after(e0_a, rate_l))
+        l0_b = to_ahead(after(e0_b, l0_a))
+    s1_a = settled(1, have1_a, came1_a)
+    with jax.named_scope("slab1_pair"):
+        e1_a = to_pair(after(s1_a, e0_b))
+    with jax.named_scope("slab1_ahead"):
+        l1_a = to_ahead(after(e1_a, l0_b))
+    s1_b = settled(1, have1_b, came1_b)
+    with jax.named_scope("slab1_pair"):
+        e1_b = to_pair(after(s1_b, e1_a))
+    l0_b = after(l0_b, s1_b, e1_a)
 
     tall = rows + 2 * PAD
-
-    def vmem(*dims):
-        return pltpu.VMEM(dims, jnp.float32)
-
-    p3, q3 = pl.pallas_call(
+    state = pl.pallas_call(
         first_step,
-        out_shape=(shape(4, 10, tall, width_z),) * 2,
-        in_specs=[SMEM] + [ANY] * 12,
-        out_specs=[VMEM] * 2,
+        out_shape=vmem(2, 4, 10, tall, width_z),
+        in_specs=[SMEM] + [ANY] * 11 + [VMEM],
+        out_specs=VMEM,
         scratch_shapes=[
             vmem(12, rows, width_z),
             vmem(2, 12, rows, width_z),
             vmem(2, rows, width_z),
-            vmem(4, 8, rows, width_z),
             vmem(4, 14, tall, width_z),
             vmem(4, 12, tall, width_z),
             vmem(4, 12, tall, width_z),
-            pltpu.SemaphoreType.DMA((22,)),
+            pltpu.SemaphoreType.DMA((21,)),
         ],
         name="first_step",
         cost_estimate=cost(0, 50 << 20),
-        compiler_params=params(50),
-    )(scal, rate_m, rate_e, rate_l, s0_a, s0_b, e0_a, e0_b, l0_a, l0_b, far_e, far_l, vfine)
+        compiler_params=params(31),
+    )(scal, rate_m, rate_e, rate_l, s0_a, s0_b, e0_a, e0_b, l0_a, l0_b, far_e, far_l, stay(vfine))
 
     tangent, sent, means = pl.pallas_call(
         second_step,
@@ -471,14 +490,11 @@
             shape(2, 2, 4, half, width_z),
             shape(4, 2, half // 16, 128),
         ),
-        in_specs=[SMEM] + [ANY] * 10,
+        in_specs=[SMEM] + [ANY] * 7 + [VMEM] * 2,
         out_specs=[ANY, ANY, VMEM],
         scratch_shapes=[
             vmem(8, rows, width_z),
             vmem(2, 8, rows, width_z),
-            vmem(4, 4, rows, width_z),
-            vmem(4, 10, tall, width_z),
-            vmem(4, 10, tall, width_z),
             vmem(4, 8, rows, width_z),
             vmem(4, 8, tall, width_z),
             vmem(4, 8, tall, width_z),
@@ -486,15 +502,17 @@
             vmem(4, 6, tall, width_z),
             vmem(4, 4, rows, width_z),
             vmem(4, 4, rows, width_z),
-            pltpu.SemaphoreType.DMA((14,)),
+            pltpu.SemaphoreType.DMA((11,)),
             pltpu.SemaphoreType.DMA((4, 4)),
         ],
         name="second_step",
         cost_estimate=cost(0, 55 << 20),
-        compiler_params=params(56),
-    )(scal, rate_m, rate_e, rate_l, s1_a, s1_b, e1_b, l1_a, vfine, p3, q3)
+        compiler_params=params(36),
+    )(scal, rate_m, rate_e, rate_l, s1_a, s1_b, e1_b, l1_a, stay(vfine), stay(state))
 
     first, second = means[:2], means[2:]
+    with jax.named_scope("tangent_core"):
+        rest = to_core(sent)
 
     def joined(a, b):
         return jnp.where(core == 0, jnp.concatenate([a, b], 2), jnp.concatenate([b, a], 2))
@@ -502,26 +520,27 @@
     both = [(i * n_space + j, (i ^ 1) * n_space + (j ^ 1)) for i in range(4) for j in range(n_space)]
     here = joined(first, to_core(second))
     there = joined(to_pair(first), lax.ppermute(second, ("dir", "space"), both))
-    partner = mine ^ 1
     source = jnp.argmax(block_map == mine).astype(jnp.int32)
     sens = jnp.where(source == mine, here, there)
+    came = []
     for j in range(2, n_space, 2):
-        target = mine ^ j
-        row = jnp.where(block_map[mine] == target, here, there)
+        row = jnp.where(block_map[mine] == mine ^ j, here, there)
         pairs = [(i, i ^ j) for i in range(n_space)]
-        came = lax.ppermute(row, "space", pairs)
-        sens = jnp.where(source // 2 == target // 2, came, sens)
-
+        with jax.named_scope("means_space"):
+            came.append(lax.ppermute(row, "space", pairs))
     tangent = pl.pallas_call(
         finish,
         out_shape=shape(2, 2, 4, width_y, width_z),
-        in_specs=[SMEM, ANY, ANY],
+        in_specs=[SMEM, ANY, VMEM],
         out_specs=ANY,
-        scratch_shapes=[vmem(2, 2, 4, half, width_z), pltpu.SemaphoreType.DMA((2, 4))],
+        scratch_shapes=[pltpu.SemaphoreType.DMA((2, 2))],
         input_output_aliases={1: 0},
         cost_estimate=cost(0, 2 << 22),
         name="finish",
-    )(scal, tangent, to_core(sent))
+    )(scal, tangent, rest)
+    came[0] = after(came[0], tangent)
+    for j, row in zip(range(2, n_space, 2), came):
+        sens = jnp.where(source // 2 == (mine ^ j) // 2, row, sens)
     return tangent, sens.reshape(2, 1, -1)
 
 

time: 185 us -> 145 us (0.78)
  waiting for transfers between devices: 53.2 us -> 33.5 us
  Pallas kernels: 52 us -> 41.4 us
  starting transfers between devices: 51.8 us -> 43.3 us
  local copies, waits for them, and re-layouts: 10.9 us -> 4.88 us
  other arithmetic: 4.16 us -> 9.31 us
    ppermute x1, waiting for transfers between devices: 13.2 us -> 0.01 us  [local(): far_l = to_ahead(w_late)]
    ppermute x17, starting transfers between devices: 30.7 us -> 19.9 us  [the longest x3 4.52 us: local(): came.append(lax.ppermute(row, 'space', pairs))]
    ppermute x17, waiting for transfers between devices: 30.4 us -> 22.3 us  [the longest x1 8.93 us: local(): l0_b = to_ahead(after(e0_b, l0_a))]
    ppermute x3, waiting for transfers between devices: 2.22 us -> 10 us  [local(): lax.ppermute(gathered, 'space', pairs)]
    pallas_call x2, Pallas kernels: 25.2 us -> 19.4 us  [the longest x1 12.6 us: local(): pl.pallas_call(first_step, out_shape=vmem(2, 4, 10, tall, width_z), in_sp...]
    ppermute x1, waiting for transfers between devices: 5.61 us -> 0.01 us  [local(): far_e = to_behind(w_near)]
    select_n x8 -> x9, other arithmetic: 2.7 us -> 7.79 us  [the longest x2 3.65 us: candidates(): jnp.where(group == owner, own[:, at:at + 2], received[:, at:at + 2])]
    pallas_call x1, Pallas kernels: 19.8 us -> 15.1 us  [local(): pl.pallas_call(second_step, out_shape=(shape(2, 2, 4, width_y, width_z),...]
  transfers between devices with their start and end apart: 27 -> 27, of which waited for: 10 -> 9; matrix products, arithmetic and copies ran while one was open for 2% -> 7% of each run, Pallas kernels for 14% -> 15%
where the time goes in v2:
time: 145 us
  starting transfers between devices  43.3 us (30%)
  Pallas kernels  41.4 us (29%)
  waiting for transfers between devices  33.5 us (23%)
  between operations  12.3 us (8%)
  other arithmetic  9.31 us (6%)
  local copies, waits for them, and re-layouts  4.88 us (3%)
    pallas_call x1, Pallas kernels, local(): pl.pallas_call(second_step, out_shape=(shape(2, 2, 4, width_y, width_z),...  15.1 us
    pallas_call x1, Pallas kernels, local(): pl.pallas_call(first_step, out_shape=vmem(2, 4, 10, tall, width_z), in_sp...  12.6 us
    ppermute x3, waiting for transfers between devices, local(): lax.ppermute(gathered, 'space', pairs)  10 us
    ppermute x1, waiting for transfers between devices, local(): l0_b = to_ahead(after(e0_b, l0_a))  8.93 us
    ppermute x2, starting transfers between devices, local(): there = joined(to_pair(first), lax.ppermute(second, ('dir', 'space'), both))  8.92 us
    ppermute x3, starting transfers between devices, local(): lax.ppermute(gathered, 'space', pairs)  7.13 us
    pallas_call x1, Pallas kernels, local(): pl.pallas_call(expand, out_shape=vmem(4, 8, rows, width_z), in_specs=[SME...  6.74 us
    ppermute x1, starting transfers between devices, local(): far_l = to_ahead(w_late)  4.67 us
  transfers between devices with their start and end apart: 27, of which 9 were waited for; matrix products, arithmetic and copies ran while one was open for 7% of the time, Pallas kernels for 15%

profile of v2, /device:TPU:0, one launch (start us, length us, event | category | flops | bytes accessed | tf_op | source)
XLA Modules:
  0.0 144.6 jit_solution(13240526921073605438)
XLA Ops:
  1.3 4.0 %arrange.1 = (f32[2,4,264,128]{3,2,1,0:T(8,128)}, f32[2,4,264,128]{3,2,1,0:T(8,128)}, f32[4,264,128]{2,1,0:T(8,128)}) custom-call(s32[3]{0:T(128)} %pad_add_fusion.scal, f32[1,2,4,512,128]{4,3,2,1,0:T(8,128)} %store.1, f32[4,512,128]{2,1,0:T(8,128)} %rate.1), custom_call_target="tpu_custom_call" | custom-call | bytes 6291456 | tf_op jit(solution)/shard_map/arrange/pallas_call | solution.py:384
  5.8 2.6 %collective-permute-start = (f32[1,2,2,32,128]{4,3,2,1,0:T(8,128)S(1)}, f32[1,2,2,32,128]{4,3,2,1,0:T(8,128)S(1)}, u32[]{:S(2)}, u32[]{:S(2)}) collective-permute-start(f32[1,2,2,32,128]{4,3,2,1,0:T(8,128)S(1)} %bitcast.34), channel_id=1, source_target_pairs={{0,1},{1,0},{2,3},{3,2},{4,5},{5,4},{6,7},{7,6},{8,9},{9,8},{10,11... | collective-permute-start | bytes 196616 | tf_op jit(solution)/shard_map/directions_space/ppermute | solution.py:400
  11.1 1.9 %collective-permute-start.2 = (f32[2,2,2,32,128]{4,3,2,1,0:T(8,128)S(1)}, f32[2,2,2,32,128]{4,3,2,1,0:T(8,128)S(1)}, u32[]{:S(2)}, u32[]{:S(2)}) collective-permute-start(f32[2,2,2,32,128]{4,3,2,1,0:T(8,128)S(1)} %pad_maximum_fusion.2), channel_id=1, source_target_pairs={{0,2},{1,3},{2,0},{3,1},{4,6},{5,7},{6,4},{7,5},{8,10},{9,11},{10,... | collective-permute-start | bytes 393224 | tf_op jit(solution)/shard_map/directions_space/ppermute | solution.py:400
  14.5 2.6 %slice_select_fusion = (f32[2,2,264,128]{3,2,1,0:T(8,128)}, f32[2,2,264,128]{3,2,1,0:T(8,128)S(1)}) fusion(f32[2,4,264,128]{3,2,1,0:T(8,128)S(1)} %collective-permute-done.5, f32[2,4,264,128]{3,2,1,0:T(8,128)} %get-tuple-element.29, pred[]{:T(512)S(6)} %eq.57), kind=kLoop, calls=%fused_computation.1 | loop fusion | flops 270336 | bytes 3244033 | tf_op jit(solution)/shard_map/jit(_where)/select_n | solution.py:429
  18.6 2.7 %collective-permute-start.3 = (f32[4,2,2,32,128]{4,3,2,1,0:T(8,128)S(1)}, f32[4,2,2,32,128]{4,3,2,1,0:T(8,128)S(1)}, u32[]{:S(2)}, u32[]{:S(2)}) collective-permute-start(f32[4,2,2,32,128]{4,3,2,1,0:T(8,128)S(1)} %pad_maximum_fusion.1), channel_id=1, source_target_pairs={{0,4},{1,5},{2,6},{3,7},{4,0},{5,1},{6,2},{7,3},{8,12},{9,13},{10,... | collective-permute-start | bytes 786440 | tf_op jit(solution)/shard_map/directions_space/ppermute | solution.py:400
  23.6 8.5 %collective-permute-done.3 = f32[4,2,2,32,128]{4,3,2,1,0:T(8,128)S(1)} collective-permute-done((f32[4,2,2,32,128]{4,3,2,1,0:T(8,128)S(1)}, f32[4,2,2,32,128]{4,3,2,1,0:T(8,128)S(1)}, u32[]{:S(2)}, u32[]{:S(2)}) %collective-permute-start.3) | collective-permute-done | bytes 262176 | tf_op jit(solution)/shard_map/directions_space/ppermute | solution.py:400
  32.2 1.7 %collective-permute-start.4 = (f32[4,264,128]{2,1,0:T(8,128)S(1)}, f32[4,264,128]{2,1,0:T(8,128)S(1)}, u32[]{:S(2)}, u32[]{:S(2)}) collective-permute-start(f32[4,264,128]{2,1,0:T(8,128)S(1)} %collective-permute-done.1.rate_e), channel_id=1, source_target_pairs={{0,2},{2,4},{4,6},{3,1},{5,3},{7,5},{8,10},{10,12},{12,14},{11,9},... | collective-permute-start | bytes 1622024 | tf_op jit(solution)/shard_map/rate_ahead/ppermute | solution.py:425
  36.6 6.7 %expand.1.v = f32[4,8,264,128]{3,2,1,0:T(8,128)S(1)} custom-call(s32[19]{0:T(128)S(1)} %concatenate.30.scal, f32[8,2,2,32,128]{4,3,2,1,0:T(8,128)S(1)} %pad_maximum_fusion.own, f32[8,2,2,32,128]{4,3,2,1,0:T(8,128)S(1)} %collective-permute-done.8.sib), custom_call_target="tpu_custom_call" | custom-call | bytes 26214400 | tf_op jit(solution)/shard_map/expand/pallas_call | solution.py:413
  44.5 1.6 %collective-permute-done.4.rate_l = f32[4,264,128]{2,1,0:T(8,128)S(1)} collective-permute-done((f32[4,264,128]{2,1,0:T(8,128)S(1)}, f32[4,264,128]{2,1,0:T(8,128)S(1)}, u32[]{:S(2)}, u32[]{:S(2)}) %collective-permute-start.4) | collective-permute-done | bytes 540704 | tf_op jit(solution)/shard_map/rate_ahead/ppermute | solution.py:425
  46.1 3.5 %collective-permute-done.13.e_a = f32[2,2,264,128]{3,2,1,0:T(8,128)S(1)} collective-permute-done((f32[2,2,264,128]{3,2,1,0:T(8,128)S(1)}, f32[2,2,264,128]{3,2,1,0:T(8,128)S(1)}, u32[]{:S(2)}, u32[]{:S(2)}) %collective-permute-start.13) | collective-permute-done | bytes 540704 | tf_op jit(solution)/shard_map/slab0_pair/ppermute | solution.py:441
  49.5 3.7 %collective-permute-start.17 = (f32[2,2,264,128]{3,2,1,0:T(8,128)S(1)}, f32[2,2,264,128]{3,2,1,0:T(8,128)}, u32[]{:S(2)}, u32[]{:S(2)}) collective-permute-start(f32[2,2,264,128]{3,2,1,0:T(8,128)S(1)} %collective-permute-done.13.e_a), channel_id=1, source_target_pairs={{0,2},{2,4},{4,6},{3,1},{5,3},{7,5},{8,10},{10,12},{12,14},{11,9},... | collective-permute-start | bytes 1622024 | tf_op jit(solution)/shard_map/slab0_ahead/ppermute | solution.py:454
  58.4 4.7 %collective-permute-start.11 = (f32[264,128]{1,0:T(8,128)S(1)}, f32[264,128]{1,0:T(8,128)S(1)}, u32[]{:S(2)}, u32[]{:S(2)}) collective-permute-start(f32[264,128]{1,0:T(8,128)S(1)} %get-tuple-element.56), channel_id=1, source_target_pairs={{0,2},{2,4},{4,6},{3,1},{5,3},{7,5},{8,10},{10,12},{12,14},{11,9},... | collective-permute-start | bytes 405512 | tf_op jit(solution)/shard_map/far_layers/ppermute | solution.py:447
  63.1 2.0 %collective-permute-done.17.l_a = f32[2,2,264,128]{3,2,1,0:T(8,128)} collective-permute-done((f32[2,2,264,128]{3,2,1,0:T(8,128)S(1)}, f32[2,2,264,128]{3,2,1,0:T(8,128)}, u32[]{:S(2)}, u32[]{:S(2)}) %collective-permute-start.17) | collective-permute-done | bytes 540704 | tf_op jit(solution)/shard_map/slab0_ahead/ppermute | solution.py:454
  65.1 3.1 %collective-permute-done.14.e_b = f32[2,2,264,128]{3,2,1,0:T(8,128)} collective-permute-done((f32[2,2,264,128]{3,2,1,0:T(8,128)S(1)}, f32[2,2,264,128]{3,2,1,0:T(8,128)}, u32[]{:S(2)}, u32[]{:S(2)}) %collective-permute-start.14) | collective-permute-done | bytes 540704 | tf_op jit(solution)/shard_map/slab0_pair/ppermute | solution.py:452
  68.2 3.7 %collective-permute-start.18 = (f32[2,2,264,128]{3,2,1,0:T(8,128)}, f32[2,2,264,128]{3,2,1,0:T(8,128)S(1)}, u32[]{:S(2)}, u32[]{:S(2)}) collective-permute-start(f32[2,2,264,128]{3,2,1,0:T(8,128)} %collective-permute-done.14.e_b), channel_id=1, source_target_pairs={{0,2},{2,4},{4,6},{3,1},{5,3},{7,5},{8,10},{10,12},{12,14},{11,9},... | collective-permute-start | bytes 1622024 | tf_op jit(solution)/shard_map/slab0_ahead/ppermute | solution.py:455
  73.3 8.9 %collective-permute-done.18.l_b = f32[2,2,264,128]{3,2,1,0:T(8,128)S(1)} collective-permute-done((f32[2,2,264,128]{3,2,1,0:T(8,128)}, f32[2,2,264,128]{3,2,1,0:T(8,128)S(1)}, u32[]{:S(2)}, u32[]{:S(2)}) %collective-permute-start.18) | collective-permute-done | bytes 540704 | tf_op jit(solution)/shard_map/slab0_ahead/ppermute | solution.py:455
  82.2 3.1 %collective-permute-done.15 = f32[2,2,264,128]{3,2,1,0:T(8,128)S(1)} collective-permute-done((f32[2,2,264,128]{3,2,1,0:T(8,128)S(1)}, f32[2,2,264,128]{3,2,1,0:T(8,128)S(1)}, u32[]{:S(2)}, u32[]{:S(2)}) %collective-permute-start.15) | collective-permute-done | bytes 540704 | tf_op jit(solution)/shard_map/slab1_pair/ppermute | solution.py:458
  85.4 2.6 %collective-permute-start.19 = (f32[2,2,264,128]{3,2,1,0:T(8,128)S(1)}, f32[2,2,264,128]{3,2,1,0:T(8,128)S(1)}, u32[]{:S(2)}, u32[]{:S(2)}) collective-permute-start(f32[2,2,264,128]{3,2,1,0:T(8,128)S(1)} %collective-permute-done.15), channel_id=1, source_target_pairs={{0,2},{2,4},{4,6},{3,1},{5,3},{7,5},{8,10},{10,12},{12,14},{11,9},... | collective-permute-start | bytes 1622024 | tf_op jit(solution)/shard_map/slab1_ahead/ppermute | solution.py:460
  88.2 12.6 %first_step.1.state = f32[2,4,10,280,128]{4,3,2,1,0:T(8,128)S(1)} custom-call(s32[3]{0:T(128)S(1)} %copy-done.3, f32[4,264,128]{2,1,0:T(8,128)S(1)} %copy-done.2, f32[4,264,128]{2,1,0:T(8,128)S(1)} %collective-permute-done.1.rate_e, f32[4,264,128]{2,1,0:T(8,128)S(1)} %collective-permute-done.4.rate_l, f32[2,2,264,128]{3,2,1,0:T(8,128)S(1)} %broadcast_select_fusion.1.s_a, ...), custom_call_target="tpu_custom_call" | custom-call | bytes 52428800 | tf_op jit(solution)/shard_map/first_step/pallas_call | solution.py:467
  102.5 15.1 %second_step.1 = (f32[2,2,4,512,128]{4,3,2,1,0:T(8,128)}, f32[2,2,4,256,128]{4,3,2,1,0:T(8,128)}, f32[4,2,16,128]{3,2,1,0:T(8,128)S(1)}) custom-call(s32[3]{0:T(128)S(1)} %copy-done.3, f32[4,264,128]{2,1,0:T(8,128)S(1)} %copy-done.2, f32[4,264,128]{2,1,0:T(8,128)S(1)} %collective-permute-done.1.rate_e, f32[4,264,128]{2,1,0:T(8,128)S(1)} %collective-permute-done.4.rate_l, ...), custom_call_target="tpu_custom_call" | custom-call | bytes 57671680 | tf_op jit(solution)/shard_map/second_step/pallas_call | solution.py:486
  118.2 8.9 %collective-permute-start.22 = (f32[2,2,16,128]{3,2,1,0:T(8,128)S(1)}, f32[2,2,16,128]{3,2,1,0:T(8,128)S(1)}, u32[]{:S(2)}, u32[]{:S(2)}) collective-permute-start(f32[2,2,16,128]{3,2,1,0:T(8,128)S(1)} %get-tuple-element.61), channel_id=1, source_target_pairs={{0,1},{1,0},{2,3},{3,2},{4,5},{5,4},{6,7},{7,6},{8,9},{9,8},{10,11... | collective-permute-start | bytes 98312 | tf_op jit(solution)/shard_map/ppermute | solution.py:522
  130.8 1.8 %collective-permute-start.26 = (f32[2,2,32,128]{3,2,1,0:T(8,128)S(1)}, f32[2,2,32,128]{3,2,1,0:T(8,128)S(1)}, u32[]{:S(2)}, u32[]{:S(2)}) collective-permute-start(f32[2,2,32,128]{3,2,1,0:T(8,128)S(1)} %get-tuple-element.58), channel_id=1, source_target_pairs={{0,2},{1,3},{2,0},{3,1},{4,6},{5,7},{6,4},{7,5},{8,10},{9,11},{10,... | collective-permute-start | bytes 196616 | tf_op jit(solution)/shard_map/means_space/ppermute | solution.py:530
  132.6 2.7 %collective-permute-start.24 = (f32[2,2,32,128]{3,2,1,0:T(8,128)S(1)}, f32[2,2,32,128]{3,2,1,0:T(8,128)S(1)}, u32[]{:S(2)}, u32[]{:S(2)}) collective-permute-start(f32[2,2,32,128]{3,2,1,0:T(8,128)S(1)} %broadcast_select_fusion.6), channel_id=1, source_target_pairs={{0,6},{1,7},{2,4},{3,5},{4,2},{5,3},{6,0},{7,1},{8,14},{9,15},{10,... | collective-permute-start | bytes 196616 | tf_op jit(solution)/shard_map/means_space/ppermute | solution.py:530
  141.0 2.9 %finish.1 = f32[2,2,4,512,128]{4,3,2,1,0:T(8,128)} custom-call(s32[3]{0:T(128)} %pad_add_fusion.scal, f32[2,2,4,512,128]{4,3,2,1,0:T(8,128)} %get-tuple-element.43.held, f32[2,2,4,256,128]{4,3,2,1,0:T(8,128)} %copy-done.8), custom_call_target="tpu_custom_call", output_to_operand_aliasing={{}: (1, {})} | custom-call | bytes 8388608 | tf_op jit(solution)/shard_map/finish/pallas_call | solution.py:531
  (84 shorter events, 20.6 us)
Async XLA Ops:
  5.3 9.2 %collective-permute-start.5 = (f32[2,4,264,128]{3,2,1,0:T(8,128)}, f32[2,4,264,128]{3,2,1,0:T(8,128)S(1)}, u32[]{:S(2)}, u32[]{:S(2)}) collective-permute-start(f32[2,4,264,128]{3,2,1,0:T(8,128)} %get-tuple-element.30), channel_id=1, source_target_pairs={{0,8},{8,0},{16,24},{24,16},{1,9},{9,1},{17,25},{25,17},{2,10},{10... | collective-permute-start | bytes 3244040 | tf_op jit(solution)/shard_map/store_core/ppermute | solution.py:394
  11.1 7.5 %collective-permute-start.2 = (f32[2,2,2,32,128]{4,3,2,1,0:T(8,128)S(1)}, f32[2,2,2,32,128]{4,3,2,1,0:T(8,128)S(1)}, u32[]{:S(2)}, u32[]{:S(2)}) collective-permute-start(f32[2,2,2,32,128]{4,3,2,1,0:T(8,128)S(1)} %pad_maximum_fusion.2), channel_id=1, source_target_pairs={{0,2},{1,3},{2,0},{3,1},{4,6},{5,7},{6,4},{7,5},{8,10},{9,11},{10,... | collective-permute-start | bytes 393224 | tf_op jit(solution)/shard_map/directions_space/ppermute | solution.py:400
  13.0 19.2 %collective-permute-start.1 = (f32[4,264,128]{2,1,0:T(8,128)}, f32[4,264,128]{2,1,0:T(8,128)S(1)}, u32[]{:S(2)}, u32[]{:S(2)}) collective-permute-start(f32[4,264,128]{2,1,0:T(8,128)} %get-tuple-element.27.rate_m), channel_id=1, source_target_pairs={{0,1},{1,0},{2,3},{3,2},{4,5},{5,4},{6,7},{7,6},{8,9},{9,8},{10,11... | collective-permute-start | bytes 1622024 | tf_op jit(solution)/shard_map/rate_pair/ppermute | solution.py:423
  17.1 16.9 %collective-permute-start.6 = (f32[2,2,264,128]{3,2,1,0:T(8,128)S(1)}, f32[2,2,264,128]{3,2,1,0:T(8,128)}, u32[]{:S(2)}, u32[]{:S(2)}) collective-permute-start(f32[2,2,264,128]{3,2,1,0:T(8,128)S(1)} %get-tuple-element.55), channel_id=1, source_target_pairs={{0,16},{8,24},{16,0},{24,8},{1,17},{9,25},{17,1},{25,9},{2,18},{10... | collective-permute-start | bytes 1622024 | tf_op jit(solution)/shard_map/slab0_column/ppermute | solution.py:436
  18.6 13.5 %collective-permute-start.3 = (f32[4,2,2,32,128]{4,3,2,1,0:T(8,128)S(1)}, f32[4,2,2,32,128]{4,3,2,1,0:T(8,128)S(1)}, u32[]{:S(2)}, u32[]{:S(2)}) collective-permute-start(f32[4,2,2,32,128]{4,3,2,1,0:T(8,128)S(1)} %pad_maximum_fusion.1), channel_id=1, source_target_pairs={{0,4},{1,5},{2,6},{3,7},{4,0},{5,1},{6,2},{7,3},{8,12},{9,13},{10,... | collective-permute-start | bytes 786440 | tf_op jit(solution)/shard_map/directions_space/ppermute | solution.py:400
  32.2 13.8 %collective-permute-start.4 = (f32[4,264,128]{2,1,0:T(8,128)S(1)}, f32[4,264,128]{2,1,0:T(8,128)S(1)}, u32[]{:S(2)}, u32[]{:S(2)}) collective-permute-start(f32[4,264,128]{2,1,0:T(8,128)S(1)} %collective-permute-done.1.rate_e), channel_id=1, source_target_pairs={{0,2},{2,4},{4,6},{3,1},{5,3},{7,5},{8,10},{10,12},{12,14},{11,9},... | collective-permute-start | bytes 1622024 | tf_op jit(solution)/shard_map/rate_ahead/ppermute | solution.py:425
  35.1 14.4 %collective-permute-start.13 = (f32[2,2,264,128]{3,2,1,0:T(8,128)S(1)}, f32[2,2,264,128]{3,2,1,0:T(8,128)S(1)}, u32[]{:S(2)}, u32[]{:S(2)}) collective-permute-start(f32[2,2,264,128]{3,2,1,0:T(8,128)S(1)} %broadcast_select_fusion.1.s_a), channel_id=1, source_target_pairs={{0,1},{1,0},{2,3},{3,2},{4,5},{5,4},{6,7},{7,6},{8,9},{9,8},{10,11... | collective-permute-start | bytes 1622024 | tf_op jit(solution)/shard_map/slab0_pair/ppermute | solution.py:441
  35.2 18.0 %collective-permute-start.7 = (f32[2,2,264,128]{3,2,1,0:T(8,128)}, f32[2,2,264,128]{3,2,1,0:T(8,128)}, u32[]{:S(2)}, u32[]{:S(2)}) collective-permute-start(f32[2,2,264,128]{3,2,1,0:T(8,128)} %get-tuple-element.32), channel_id=1, source_target_pairs={{0,16},{8,24},{16,0},{24,8},{1,17},{9,25},{17,1},{25,9},{2,18},{10... | collective-permute-start | bytes 1622024 | tf_op jit(solution)/shard_map/slab0_column/ppermute | solution.py:437
  49.5 15.6 %collective-permute-start.17 = (f32[2,2,264,128]{3,2,1,0:T(8,128)S(1)}, f32[2,2,264,128]{3,2,1,0:T(8,128)}, u32[]{:S(2)}, u32[]{:S(2)}) collective-permute-start(f32[2,2,264,128]{3,2,1,0:T(8,128)S(1)} %collective-permute-done.13.e_a), channel_id=1, source_target_pairs={{0,2},{2,4},{4,6},{3,1},{5,3},{7,5},{8,10},{10,12},{12,14},{11,9},... | collective-permute-start | bytes 1622024 | tf_op jit(solution)/shard_map/slab0_ahead/ppermute | solution.py:454
  54.4 13.9 %collective-permute-start.14 = (f32[2,2,264,128]{3,2,1,0:T(8,128)S(1)}, f32[2,2,264,128]{3,2,1,0:T(8,128)}, u32[]{:S(2)}, u32[]{:S(2)}) collective-permute-start(f32[2,2,264,128]{3,2,1,0:T(8,128)S(1)} %broadcast_select_fusion.s_b), channel_id=1, source_target_pairs={{0,1},{1,0},{2,3},{3,2},{4,5},{5,4},{6,7},{7,6},{8,9},{9,8},{10,11... | collective-permute-start | bytes 1622024 | tf_op jit(solution)/shard_map/slab0_pair/ppermute | solution.py:452
  54.4 17.5 %collective-permute-start.9 = (f32[2,2,264,128]{3,2,1,0:T(8,128)}, f32[2,2,264,128]{3,2,1,0:T(8,128)}, u32[]{:S(2)}, u32[]{:S(2)}) collective-permute-start(f32[2,2,264,128]{3,2,1,0:T(8,128)} %get-tuple-element.33), channel_id=1, source_target_pairs={{0,16},{8,24},{16,0},{24,8},{1,17},{9,25},{17,1},{25,9},{2,18},{10... | collective-permute-start | bytes 1622024 | tf_op jit(solution)/shard_map/slab1_column/ppermute | solution.py:449
  56.9 16.3 %collective-permute-start.10 = (f32[264,128]{1,0:T(8,128)S(1)}, f32[264,128]{1,0:T(8,128)S(1)}, u32[]{:S(2)}, u32[]{:S(2)}) collective-permute-start(f32[264,128]{1,0:T(8,128)S(1)} %get-tuple-element.57), channel_id=1, source_target_pairs={{2,0},{4,2},{6,4},{1,3},{3,5},{5,7},{10,8},{12,10},{14,12},{9,11},... | collective-permute-start | bytes 405512 | tf_op jit(solution)/shard_map/far_layers/ppermute | solution.py:446
  58.4 14.8 %collective-permute-start.11 = (f32[264,128]{1,0:T(8,128)S(1)}, f32[264,128]{1,0:T(8,128)S(1)}, u32[]{:S(2)}, u32[]{:S(2)}) collective-permute-start(f32[264,128]{1,0:T(8,128)S(1)} %get-tuple-element.56), channel_id=1, source_target_pairs={{0,2},{2,4},{4,6},{3,1},{5,3},{7,5},{8,10},{10,12},{12,14},{11,9},... | collective-permute-start | bytes 405512 | tf_op jit(solution)/shard_map/far_layers/ppermute | solution.py:447
  68.2 14.0 %collective-permute-start.18 = (f32[2,2,264,128]{3,2,1,0:T(8,128)}, f32[2,2,264,128]{3,2,1,0:T(8,128)S(1)}, u32[]{:S(2)}, u32[]{:S(2)}) collective-permute-start(f32[2,2,264,128]{3,2,1,0:T(8,128)} %collective-permute-done.14.e_b), channel_id=1, source_target_pairs={{0,2},{2,4},{4,6},{3,1},{5,3},{7,5},{8,10},{10,12},{12,14},{11,9},... | collective-permute-start | bytes 1622024 | tf_op jit(solution)/shard_map/slab0_ahead/ppermute | solution.py:455
  73.1 12.2 %collective-permute-start.15 = (f32[2,2,264,128]{3,2,1,0:T(8,128)S(1)}, f32[2,2,264,128]{3,2,1,0:T(8,128)S(1)}, u32[]{:S(2)}, u32[]{:S(2)}) collective-permute-start(f32[2,2,264,128]{3,2,1,0:T(8,128)S(1)} %broadcast_select_fusion.3.s_a), channel_id=1, source_target_pairs={{0,1},{1,0},{2,3},{3,2},{4,5},{5,4},{6,7},{7,6},{8,9},{9,8},{10,11... | collective-permute-start | bytes 1622024 | tf_op jit(solution)/shard_map/slab1_pair/ppermute | solution.py:458
  73.2 14.8 %collective-permute-start.12 = (f32[2,2,264,128]{3,2,1,0:T(8,128)}, f32[2,2,264,128]{3,2,1,0:T(8,128)S(1)}, u32[]{:S(2)}, u32[]{:S(2)}) collective-permute-start(f32[2,2,264,128]{3,2,1,0:T(8,128)} %get-tuple-element.34), channel_id=1, source_target_pairs={{0,16},{8,24},{16,0},{24,8},{1,17},{9,25},{17,1},{25,9},{2,18},{10... | collective-permute-start | bytes 1622024 | tf_op jit(solution)/shard_map/slab1_column/ppermute | solution.py:450
  85.4 15.5 %collective-permute-start.19 = (f32[2,2,264,128]{3,2,1,0:T(8,128)S(1)}, f32[2,2,264,128]{3,2,1,0:T(8,128)S(1)}, u32[]{:S(2)}, u32[]{:S(2)}) collective-permute-start(f32[2,2,264,128]{3,2,1,0:T(8,128)S(1)} %collective-permute-done.15), channel_id=1, source_target_pairs={{0,2},{2,4},{4,6},{3,1},{5,3},{7,5},{8,10},{10,12},{12,14},{11,9},... | collective-permute-start | bytes 1622024 | tf_op jit(solution)/shard_map/slab1_ahead/ppermute | solution.py:460
  88.1 12.8 %collective-permute-start.16 = (f32[2,2,264,128]{3,2,1,0:T(8,128)S(1)}, f32[2,2,264,128]{3,2,1,0:T(8,128)S(1)}, u32[]{:S(2)}, u32[]{:S(2)}) collective-permute-start(f32[2,2,264,128]{3,2,1,0:T(8,128)S(1)} %broadcast_select_fusion.2.s_b), channel_id=1, source_target_pairs={{0,1},{1,0},{2,3},{3,2},{4,5},{5,4},{6,7},{7,6},{8,9},{9,8},{10,11... | collective-permute-start | bytes 1622024 | tf_op jit(solution)/shard_map/slab1_pair/ppermute | solution.py:463
  117.6 22.0 %collective-permute-start.20 = (f32[2,2,4,256,128]{4,3,2,1,0:T(8,128)}, f32[2,2,4,256,128]{4,3,2,1,0:T(8,128)S(1)}, u32[]{:S(2)}, u32[]{:S(2)}) collective-permute-start(f32[2,2,4,256,128]{4,3,2,1,0:T(8,128)} %get-tuple-element.44), channel_id=1, source_target_pairs={{0,8},{8,0},{16,24},{24,16},{1,9},{9,1},{17,25},{25,17},{2,10},{10... | collective-permute-start | bytes 6291464 | tf_op jit(solution)/shard_map/tangent_core/ppermute | solution.py:515
  117.7 11.9 %collective-permute-start.21 = (f32[2,2,16,128]{3,2,1,0:T(8,128)S(1)}, f32[2,2,16,128]{3,2,1,0:T(8,128)S(1)}, u32[]{:S(2)}, u32[]{:S(2)}) collective-permute-start(f32[2,2,16,128]{3,2,1,0:T(8,128)S(1)} %get-tuple-element.60), channel_id=1, source_target_pairs={{0,8},{8,0},{16,24},{24,16},{1,9},{9,1},{17,25},{25,17},{2,10},{10... | collective-permute-start | bytes 98312 | tf_op jit(solution)/shard_map/ppermute | solution.py:521
  118.2 11.5 %collective-permute-start.22 = (f32[2,2,16,128]{3,2,1,0:T(8,128)S(1)}, f32[2,2,16,128]{3,2,1,0:T(8,128)S(1)}, u32[]{:S(2)}, u32[]{:S(2)}) collective-permute-start(f32[2,2,16,128]{3,2,1,0:T(8,128)S(1)} %get-tuple-element.61), channel_id=1, source_target_pairs={{0,1},{1,0},{2,3},{3,2},{4,5},{5,4},{6,7},{7,6},{8,9},{9,8},{10,11... | collective-permute-start | bytes 98312 | tf_op jit(solution)/shard_map/ppermute | solution.py:522
  130.8 13.1 %collective-permute-start.26 = (f32[2,2,32,128]{3,2,1,0:T(8,128)S(1)}, f32[2,2,32,128]{3,2,1,0:T(8,128)S(1)}, u32[]{:S(2)}, u32[]{:S(2)}) collective-permute-start(f32[2,2,32,128]{3,2,1,0:T(8,128)S(1)} %get-tuple-element.58), channel_id=1, source_target_pairs={{0,2},{1,3},{2,0},{3,1},{4,6},{5,7},{6,4},{7,5},{8,10},{9,11},{10,... | collective-permute-start | bytes 196616 | tf_op jit(solution)/shard_map/means_space/ppermute | solution.py:530
  132.6 11.4 %collective-permute-start.25 = (f32[2,2,32,128]{3,2,1,0:T(8,128)S(1)}, f32[2,2,32,128]{3,2,1,0:T(8,128)S(1)}, u32[]{:S(2)}, u32[]{:S(2)}) collective-permute-start(f32[2,2,32,128]{3,2,1,0:T(8,128)S(1)} %get-tuple-element.59), channel_id=1, source_target_pairs={{0,4},{1,5},{2,6},{3,7},{4,0},{5,1},{6,2},{7,3},{8,12},{9,13},{10,... | collective-permute-start | bytes 196616 | tf_op jit(solution)/shard_map/means_space/ppermute | solution.py:530
  132.6 11.4 %collective-permute-start.24 = (f32[2,2,32,128]{3,2,1,0:T(8,128)S(1)}, f32[2,2,32,128]{3,2,1,0:T(8,128)S(1)}, u32[]{:S(2)}, u32[]{:S(2)}) collective-permute-start(f32[2,2,32,128]{3,2,1,0:T(8,128)S(1)} %broadcast_select_fusion.6), channel_id=1, source_target_pairs={{0,6},{1,7},{2,4},{3,5},{4,2},{5,3},{6,0},{7,1},{8,14},{9,15},{10,... | collective-permute-start | bytes 196616 | tf_op jit(solution)/shard_map/means_space/ppermute | solution.py:530
  (16 other events, 158.0 us)

commit v3 on v2

--- a/solution.py
+++ b/solution.py
@@ -48,7 +48,7 @@
         layer = jnp.where(odd == 1, 3 - m, m)
         for start, target in ((second, other), (first, mine)):
             copies.append((store.at[0, :, layer, pl.ds(start, rows)], target.at[:, m]))
-        copies.append((rate.at[layer, pl.ds(first, rows)], rate_m.at[m]))
+        copies.append((rate.at[layer, pl.ds(first, rows)], rate_m.at[pl.ds(rows * m, rows)]))
     run_all([pltpu.make_async_copy(a, b, sems.at[i]) for i, (a, b) in enumerate(copies)])
 
 
@@ -56,25 +56,49 @@
     return jnp.dot(a, b, precision=lax.Precision.HIGHEST, preferred_element_type=jnp.float32)
 
 
-def expand(scal, own, sib, vfine):
+def window(scal, own, sib, out):
+    half = own.shape[2] // 2
+    for core in range(2):
+
+        @pl.when(scal[0] == core)
+        def _():
+            at = core * (half - 1)
+            for d in range(4):
+                for k in range(2):
+                    block = (own if d < 2 else sib)[d % 2, k, at : at + half + 1]
+                    out[pl.ds((2 * d + k) * (half + 1), half + 1)] = block
+
+
+def expand(scal, where, *refs):
+    held, vfine, blocks = refs[:-2], refs[-2], refs[-1]
     core = scal[0]
     rows = vfine.shape[2]
     shift = rows - 2 * EDGE
-    packed = own.shape[3]
-    row = lax.broadcasted_iota(jnp.int32, (rows, 4 * packed), 0) + core * shift
-    column = lax.broadcasted_iota(jnp.int32, (rows, 4 * packed), 1)
-    coarse = row // 4
-    pick_rows = (coarse == 4 * (column % packed) + column // packed).astype(jnp.float32)
+    count = held[0].shape[1] // 8
+    tall = blocks.shape[1]
+    row = lax.broadcasted_iota(jnp.int32, (rows, 4 * tall), 0) + core * shift
+    column = lax.broadcasted_iota(jnp.int32, (rows, 4 * tall), 1)
+    place = column % tall
+    there = 4 * (place + core * (count - 2)) + column // tall
+    pick_rows = ((row // 4 == there) & (place < count)).astype(jnp.float32)
     lane = lax.broadcasted_iota(jnp.int32, (128, 512), 0)
     z = lax.broadcasted_iota(jnp.int32, (128, 512), 1)
     pick_lanes = (lane == 32 * (z // 128) + (z % 128) // 4).astype(jnp.float32)
+    blocks[...] = jnp.zeros(blocks.shape, jnp.float32)
     for k in range(8):
-        blocks = [(own if d < 2 else sib)[scal[3 + k], d % 2, scal[11 + k]] for d in range(4)]
-        wide = exact_dot(jnp.concatenate(blocks, 0), pick_lanes)
+        for d in range(4):
+            block = jnp.zeros((count, 128), jnp.float32)
+            for i, ref in enumerate(held):
+                for j in range(2):
+                    for h in range(2):
+                        hit = (where[k] == 2 * i + j) & (where[8 + k] == h)
+                        block = jnp.where(hit, ref[j, pl.ds((2 * d + h) * count, count)], block)
+            blocks[d, pl.ds(0, count)] = block
+        wide = exact_dot(blocks[...].reshape(4 * tall, 128), pick_lanes)
         table = jnp.concatenate(
             [
                 jnp.concatenate(
-                    [wide[packed * d : packed * (d + 1), 128 * j : 128 * (j + 1)] for j in range(4)], 0
+                    [wide[tall * d : tall * (d + 1), 128 * j : 128 * (j + 1)] for j in range(4)], 0
                 )
                 for d in range(4)
             ],
@@ -142,11 +166,11 @@
     has_late = scal[2]
     p3, q3 = state.at[0], state.at[1]
     rows = rate.shape[1]
-    moves = [(rate_m, rate.at[pl.ds(4, 4)])]
+    moves = [(rate_m.at[pl.ds(rows * j, rows)], rate.at[4 + j]) for j in range(4)]
     moves += [(s_a, slab.at[:, pl.ds(4, 2)]), (s_b, slab.at[:, pl.ds(6, 2)])]
     for j in range(4):
-        moves.append((rate_e.at[j], rate.at[11 - j]))
-        moves.append((rate_l.at[j], rate.at[3 - j]))
+        moves.append((rate_e.at[pl.ds(rows * j, rows)], rate.at[11 - j]))
+        moves.append((rate_l.at[pl.ds(rows * j, rows)], rate.at[3 - j]))
     for j in range(2):
         moves.append((e_a.at[:, j], slab.at[:, 11 - j]))
         moves.append((e_b.at[:, j], slab.at[:, 9 - j]))
@@ -216,18 +240,18 @@
 
 def second_step(
     scal, rate_m, rate_e, rate_l, s_a, s_b, e_b, l_a, v, state,
-    tangent, sent, means, rate, slab, weight, p4, q4, p5, q5, p6, q6, sems, out_sems,
+    tangent, sent, means, means_sib, rate, slab, weight, p4, q4, p5, q5, p6, q6, sems, out_sems,
 ):
     core, odd, has_late = scal[0], scal[1], scal[2]
     sigma = 1 - 2 * odd
     rows = rate.shape[1]
     half = rows - EDGE
     p3, q3 = state.at[0], state.at[1]
-    moves = [(rate_m, rate.at[pl.ds(2, 4)])]
+    moves = [(rate_m.at[pl.ds(rows * j, rows)], rate.at[2 + j]) for j in range(4)]
     moves += [(s_a, slab.at[:, pl.ds(2, 2)]), (s_b, slab.at[:, pl.ds(4, 2)])]
     for j in range(2):
-        moves.append((rate_e.at[3 - j], rate.at[6 + j]))
-        moves.append((rate_l.at[j], rate.at[1 - j]))
+        moves.append((rate_e.at[pl.ds(rows * (3 - j), rows)], rate.at[6 + j]))
+        moves.append((rate_l.at[pl.ds(rows * j, rows)], rate.at[1 - j]))
         moves.append((e_b.at[:, 1 - j], slab.at[:, 6 + j]))
         moves.append((l_a.at[:, j], slab.at[:, 1 - j]))
     copies = [pltpu.make_async_copy(a, b, sems.at[i]) for i, (a, b) in enumerate(moves)]
@@ -312,7 +336,7 @@
     for d in range(4):
         for k in range(2):
             layer = jnp.where(odd == 1, 1 - k, k)
-            means[d, layer] = total[packed * (2 * d + k) : packed * (2 * d + k + 1)]
+            (means if d < 2 else means_sib)[d % 2, layer] = total[packed * (2 * d + k) : packed * (2 * d + k + 1)]
 
     @pl.loop(0, 4)
     def _(i):
@@ -365,8 +389,8 @@
     n_space = lax.axis_size("space")
     mine = lax.axis_index("space")
     group = lax.axis_index("dir")
-    core, column = group % 2, group // 2
-    odd = mine % 2
+    core, column = group & 1, group >> 1
+    odd = mine & 1
     has_late = ((mine > 0) & (mine < n_space - 1)).astype(jnp.int32)
     scal = jnp.stack([core, odd, has_late]).astype(jnp.int32)
 
@@ -381,9 +405,12 @@
     to_ahead = functools.partial(lax.ppermute, axis_name="space", perm=ahead)
     to_behind = functools.partial(lax.ppermute, axis_name="space", perm=behind)
 
+    row = directions.reshape(2, 2, 32, 128)
+    with jax.named_scope("directions_core"):
+        row_sib = to_core(row)
     own, other, rate_m = pl.pallas_call(
         arrange,
-        out_shape=(shape(2, 4, rows, width_z), shape(2, 4, rows, width_z), shape(4, rows, width_z)),
+        out_shape=(vmem(2, 4, rows, width_z), vmem(2, 4, rows, width_z), vmem(4 * rows, width_z)),
         in_specs=[SMEM, ANY, ANY],
         out_specs=[VMEM] * 3,
         cost_estimate=cost(0, 6 << 20),
@@ -392,67 +419,70 @@
     )(scal, store, rate)
     with jax.named_scope("store_core"):
         received = to_core(other)
-    gathered = after(directions, rate_m).reshape(1, 2, 2, 32, 128)
-    reach = 1
-    while reach < n_space:
-        pairs = [(i, i ^ reach) for i in range(n_space)]
+    def candidates(step, received):
+        here = group == owner_map[step]
+        first = jnp.where(here, own[:, :2], received[:, :2])
+        return first, jnp.where(here, own[:, 2:], after(received, first)[:, 2:])
+
+    def settled(step, have, came):
+        return jnp.where(column == owner_map[step] >> 1, have, came)
+
+    have0_a, have0_b = candidates(0, received)
+
+    coarse_own = pl.pallas_call(
+        window,
+        out_shape=vmem(8 * 17, 128),
+        in_specs=[SMEM, VMEM, VMEM],
+        out_specs=VMEM,
+        name="window",
+    )(scal, after(row, rate_m), row_sib)
+    with jax.named_scope("directions_pair"):
+        pair = jnp.stack([coarse_own, after(to_pair(coarse_own), have0_a)])
+    held = [pair]
+    for j in range(2, n_space, 2):
         with jax.named_scope("directions_space"):
-            gathered = jnp.concatenate([gathered, lax.ppermute(gathered, "space", pairs)], 0)
-        if reach == 1:
-            near = gathered
-        reach *= 2
-    with jax.named_scope("directions_core"):
-        gathered_sib = to_core(gathered)
+            held.append(lax.ppermute(pair, "space", [(i, i ^ j) for i in range(n_space)]))
+    have1_a, have1_b = candidates(1, after(received, have0_a, pair))
+    with jax.named_scope("rate_pair"):
+        rate_e = to_pair(after(rate_m, received))
+    with jax.named_scope("slab0_column"):
+        came0_a = to_column(have0_a)
+    with jax.named_scope("slab0_column"):
+        came0_b = to_column(after(have0_b, came0_a, have1_a, have1_b, *held))
+    with jax.named_scope("rate_ahead"):
+        rate_l = to_ahead(rate_e)
+
     local_coarse = jnp.arange(8, dtype=jnp.int32) - 3
     coarse_at = 2 * mine + jnp.where(odd == 1, 1 - local_coarse, local_coarse)
-    block = jnp.clip(coarse_at // 2, 0, n_space - 1)
-    coarse_scal = jnp.concatenate(
-        [scal, (block_map[block] ^ mine).astype(jnp.int32), (coarse_at % 2).astype(jnp.int32)]
-    )
-
-    vfine = pl.pallas_call(
-        expand,
-        out_shape=vmem(4, 8, rows, width_z),
-        in_specs=[SMEM, VMEM, VMEM],
-        out_specs=VMEM,
-        name="expand",
-        cost_estimate=cost(0, 25 << 20),
-        compiler_params=params(16),
-    )(coarse_scal, gathered, gathered_sib)
-    with jax.named_scope("rate_pair"):
-        rate_e = to_pair(after(rate_m, near))
-    with jax.named_scope("rate_ahead"):
-        rate_l = to_ahead(after(rate_e, gathered))
-
-    def candidates(step, received):
-        owner = owner_map[step]
-        return [jnp.where(group == owner, own[:, at : at + 2], received[:, at : at + 2]) for at in (0, 2)]
-
-    def settled(step, have, came):
-        return jnp.where(column == owner_map[step] // 2, have, came)
-
-    have0_a, have0_b = candidates(0, received)
-    with jax.named_scope("slab0_column"):
-        came0_a = to_column(have0_a)
-        came0_b = to_column(after(have0_b, came0_a))
-    have1_a, have1_b = candidates(1, after(received, have0_a, rate_e))
+    block = block_map[jnp.clip(coarse_at >> 1, 0, n_space - 1)] ^ mine
+    coarse_scal = jnp.concatenate([block, coarse_at & 1]).astype(jnp.int32)
     s0_a = settled(0, have0_a, came0_a)
     with jax.named_scope("slab0_pair"):
         e0_a = to_pair(after(s0_a, rate_e))
     s0_b = settled(0, have0_b, came0_b)
-    w_near = rate_scale * rate_m[0] * s0_a[0, 0] * s0_a[1, 0]
-    w_late = rate_scale * rate_m[3] * s0_b[0, 1] * s0_b[1, 1]
+    w_near = rate_scale * rate_m[:rows] * s0_a[0, 0] * s0_a[1, 0]
+    w_late = rate_scale * rate_m[3 * rows : 4 * rows] * s0_b[0, 1] * s0_b[1, 1]
     with jax.named_scope("far_layers"):
         far_e = to_behind(w_near)
         far_l = to_ahead(w_late)
-    with jax.named_scope("slab1_column"):
-        came1_a = to_column(after(have1_a, came0_b, vfine))
-        came1_b = to_column(after(have1_b, came1_a, far_e, far_l))
     with jax.named_scope("slab0_pair"):
         e0_b = to_pair(after(s0_b, e0_a))
+    vfine = pl.pallas_call(
+        expand,
+        out_shape=vmem(4, 8, rows, width_z),
+        in_specs=[SMEM, SMEM] + [VMEM] * len(held),
+        out_specs=VMEM,
+        scratch_shapes=[vmem(4, 24, 128)],
+        name="expand",
+        cost_estimate=cost(0, 25 << 20),
+        compiler_params=params(16),
+    )(scal, coarse_scal, *held)
+    with jax.named_scope("slab1_column"):
+        came1_a = to_column(after(have1_a, e0_a))
+        came1_b = to_column(after(have1_b, e0_b, far_e, far_l))
     with jax.named_scope("slab0_ahead"):
-        l0_a = to_ahead(after(e0_a, rate_l))
-        l0_b = to_ahead(after(e0_b, l0_a))
+        l0_a = to_ahead(after(e0_a, s0_b, rate_l))
+        l0_b = to_ahead(after(e0_b, l0_a, far_e, far_l, vfine))
     s1_a = settled(1, have1_a, came1_a)
     with jax.named_scope("slab1_pair"):
         e1_a = to_pair(after(s1_a, e0_b))
@@ -476,22 +506,23 @@
             vmem(4, 14, tall, width_z),
             vmem(4, 12, tall, width_z),
             vmem(4, 12, tall, width_z),
-            pltpu.SemaphoreType.DMA((21,)),
+            pltpu.SemaphoreType.DMA((24,)),
         ],
         name="first_step",
         cost_estimate=cost(0, 50 << 20),
         compiler_params=params(31),
     )(scal, rate_m, rate_e, rate_l, s0_a, s0_b, e0_a, e0_b, l0_a, l0_b, far_e, far_l, stay(vfine))
 
-    tangent, sent, means = pl.pallas_call(
+    tangent, sent, first, second = pl.pallas_call(
         second_step,
         out_shape=(
             shape(2, 2, 4, width_y, width_z),
             shape(2, 2, 4, half, width_z),
-            shape(4, 2, half // 16, 128),
+            vmem(2, 2, half // 16, 128),
+            vmem(2, 2, half // 16, 128),
         ),
         in_specs=[SMEM] + [ANY] * 7 + [VMEM] * 2,
-        out_specs=[ANY, ANY, VMEM],
+        out_specs=[ANY, ANY, VMEM, VMEM],
         scratch_shapes=[
             vmem(8, rows, width_z),
             vmem(2, 8, rows, width_z),
@@ -502,7 +533,7 @@
             vmem(4, 6, tall, width_z),
             vmem(4, 4, rows, width_z),
             vmem(4, 4, rows, width_z),
-            pltpu.SemaphoreType.DMA((11,)),
+            pltpu.SemaphoreType.DMA((14,)),
             pltpu.SemaphoreType.DMA((4, 4)),
         ],
         name="second_step",
@@ -510,17 +541,17 @@
         compiler_params=params(36),
     )(scal, rate_m, rate_e, rate_l, s1_a, s1_b, e1_b, l1_a, stay(vfine), stay(state))
 
-    first, second = means[:2], means[2:]
-    with jax.named_scope("tangent_core"):
-        rest = to_core(sent)
 
     def joined(a, b):
         return jnp.where(core == 0, jnp.concatenate([a, b], 2), jnp.concatenate([b, a], 2))
 
     both = [(i * n_space + j, (i ^ 1) * n_space + (j ^ 1)) for i in range(4) for j in range(n_space)]
-    here = joined(first, to_core(second))
-    there = joined(to_pair(first), lax.ppermute(second, ("dir", "space"), both))
-    source = jnp.argmax(block_map == mine).astype(jnp.int32)
+    with jax.named_scope("means_near"):
+        here = joined(first, to_core(second))
+        there = joined(to_pair(first), lax.ppermute(second, ("dir", "space"), both))
+    with jax.named_scope("tangent_core"):
+        rest = to_core(after(sent, here, there))
+    source = jnp.sum(jnp.where(block_map == mine, jnp.arange(n_space, dtype=jnp.int32), 0))
     sens = jnp.where(source == mine, here, there)
     came = []
     for j in range(2, n_space, 2):
@@ -540,7 +571,7 @@
     )(scal, tangent, rest)
     came[0] = after(came[0], tangent)
     for j, row in zip(range(2, n_space, 2), came):
-        sens = jnp.where(source // 2 == (mine ^ j) // 2, row, sens)
+        sens = jnp.where(source >> 1 == (mine ^ j) >> 1, row, sens)
     return tangent, sens.reshape(2, 1, -1)
 
 

time: 145 us -> 142 us (0.979)
  waiting for transfers between devices: 33.5 us -> 24.6 us
  starting transfers between devices: 43.3 us -> 49.8 us
  between operations: 12.3 us -> 6.97 us
  local copies, waits for them, and re-layouts: 4.88 us -> 6.45 us
    ppermute x12 -> x13, waiting for transfers between devices: 22.6 us -> 15.9 us  [the longest x1 5.37 us: local(): l0_b = to_ahead(after(e0_b, l0_a, far_e, far_l, vfine))]
    ppermute x12 -> x13, starting transfers between devices: 18.1 us -> 22.7 us  [the longest x1 5.2 us: local(): l0_a = to_ahead(after(e0_a, s0_b, rate_l))]
    ppermute x1, waiting for transfers between devices: 3.46 us -> 0.01 us  [local(): e0_a = to_pair(after(s0_a, rate_e))]
    ppermute x1, waiting for transfers between devices: 3.14 us -> 0.01 us  [local(): e0_b = to_pair(after(s0_b, e0_a))]
    ppermute x1, waiting for transfers between devices: 0.01 us -> 2.43 us  [local(): came0_a = to_column(have0_a)]
    unnamed x26, local copies, waits for them, and re-layouts: 3 us -> 4.57 us
    pallas_call x1 -> x2, Pallas kernels: 3.97 us -> 3.48 us  [the longest x1 2.59 us: local(): pl.pallas_call(arrange, out_shape=(vmem(2, 4, rows, width_z), vmem(2, 4,...]
  transfers between devices with their start and end apart: 27 -> 28, of which waited for: 9 -> 10; matrix products, arithmetic and copies ran while one was open for 7% -> 8% of each run, Pallas kernels for 15% -> 17%
where the time goes in v3:
time: 142 us; the launch traced here: 141 us
  starting transfers between devices  49.8 us (35%)
  Pallas kernels  42.3 us (30%)
  waiting for transfers between devices  24.6 us (17%)
  other arithmetic  10.7 us (8%)
  between operations  6.97 us (5%)
  local copies, waits for them, and re-layouts  6.45 us (5%)
    pallas_call x1, Pallas kernels, local(): pl.pallas_call(second_step, out_shape=(shape(2, 2, 4, width_y, width_z),...  15.7 us
    pallas_call x1, Pallas kernels, local(): pl.pallas_call(first_step, out_shape=vmem(2, 4, 10, tall, width_z), in_sp...  13.5 us
    ppermute x2, starting transfers between devices, local(): there = joined(to_pair(first), lax.ppermute(second, ('dir', 'space'), both))  9.1 us
    pallas_call x1, Pallas kernels, local(): pl.pallas_call(expand, out_shape=vmem(4, 8, rows, width_z), in_specs=[SME...  6.74 us
    ppermute x1, waiting for transfers between devices, local(): l0_b = to_ahead(after(e0_b, l0_a, far_e, far_l, vfine))  5.37 us
    ppermute x1, starting transfers between devices, local(): far_l = to_ahead(w_late)  5.22 us
    ppermute x1, starting transfers between devices, local(): l0_a = to_ahead(after(e0_a, s0_b, rate_l))  5.2 us
    ppermute x1, waiting for transfers between devices, local(): came0_b = to_column(after(have0_b, came0_a, have1_a, have1_b, *held))  4.77 us
  transfers between devices with their start and end apart: 28, of which 10 were waited for; matrix products, arithmetic and copies ran while one was open for 8% of the time, Pallas kernels for 17%

profile of v3, /device:TPU:0, one launch (start us, length us, event | category | flops | bytes accessed | tf_op | source)
XLA Modules:
  0.0 140.9 jit_solution(8396321498530328951)
XLA Ops:
  1.3 2.6 %arrange.1 = (f32[2,4,264,128]{3,2,1,0:T(8,128)S(1)}, f32[2,4,264,128]{3,2,1,0:T(8,128)S(1)}, f32[1056,128]{1,0:T(8,128)S(1)}) custom-call(s32[3]{0:T(128)} %pad_add_fusion.scal, f32[1,2,4,512,128]{4,3,2,1,0:T(8,128)} %store.1, f32[4,512,128]{2,1,0:T(8,128)} %rate.1), custom_call_target="tpu_custom_call" | custom-call | bytes 6291456 | tf_op jit(solution)/shard_map/arrange/pallas_call | solution.py:411
  9.6 3.0 %collective-permute-start.4 = (f32[136,128]{1,0:T(8,128)S(1)}, f32[136,128]{1,0:T(8,128)S(1)}, u32[]{:S(2)}, u32[]{:S(2)}) collective-permute-start(f32[136,128]{1,0:T(8,128)S(1)} %window.1), channel_id=1, source_target_pairs={{0,1},{1,0},{2,3},{3,2},{4,5},{5,4},{6,7},{7,6},{8,9},{9,8},{10,11... | collective-permute-start | bytes 208904 | tf_op jit(solution)/shard_map/directions_pair/ppermute | solution.py:440
  15.0 4.0 %collective-permute-start.10 = (f32[2,136,128]{2,1,0:T(8,128)S(1)}, f32[2,136,128]{2,1,0:T(8,128)S(1)}, u32[]{:S(2)}, u32[]{:S(2)}) collective-permute-start(f32[2,136,128]{2,1,0:T(8,128)S(1)} %pad_maximum_fusion.refs_0_), channel_id=1, source_target_pairs={{0,6},{1,7},{2,4},{3,5},{4,2},{5,3},{6,0},{7,1},{8,14},{9,15},{10,... | collective-permute-start | bytes 417800 | tf_op jit(solution)/shard_map/directions_space/ppermute | solution.py:444
  19.7 1.6 %collective-permute-start.5 = (f32[2,2,264,128]{3,2,1,0:T(8,128)S(1)}, f32[2,2,264,128]{3,2,1,0:T(8,128)S(1)}, u32[]{:S(2)}, u32[]{:S(2)}) collective-permute-start(f32[2,2,264,128]{3,2,1,0:T(8,128)S(1)} %slice_select_fusion), channel_id=1, source_target_pairs={{0,16},{8,24},{16,0},{24,8},{1,17},{9,25},{17,1},{25,9},{2,18},{10... | collective-permute-start | bytes 1622024 | tf_op jit(solution)/shard_map/slab0_column/ppermute | solution.py:449
  22.9 2.2 %slice_select_fusion.1 = (f32[2,2,264,128]{3,2,1,0:T(8,128)S(1)}, f32[2,2,264,128]{3,2,1,0:T(8,128)}) fusion(f32[2,4,264,128]{3,2,1,0:T(8,128)} %collective-permute-done, f32[2,4,264,128]{3,2,1,0:T(8,128)S(1)} %copy-done.1, pred[]{:T(512)S(6)} %eq.48, pred[]{:T(512)S(6)} %eq.47), kind=kLoop, calls=%fused_computation.2 | loop fusion | flops 270336 | bytes 3244034 | tf_op jit(solution)/shard_map/jit(_where)/select_n | solution.py:425
  25.0 2.2 %slice_select_fusion.2 = f32[2,2,264,128]{3,2,1,0:T(8,128)} fusion(f32[2,4,264,128]{3,2,1,0:T(8,128)} %collective-permute-done, f32[2,4,264,128]{3,2,1,0:T(8,128)S(1)} %copy-done.1, pred[]{:T(512)S(6)} %eq.47), kind=kLoop, calls=%fused_computation.3 | loop fusion | flops 135168 | bytes 1622017 | tf_op jit(solution)/shard_map/jit(_where)/select_n | solution.py:425
  27.2 2.7 %collective-permute-done.9.refs_2_ = f32[2,136,128]{2,1,0:T(8,128)S(1)} collective-permute-done((f32[2,136,128]{2,1,0:T(8,128)S(1)}, f32[2,136,128]{2,1,0:T(8,128)S(1)}, u32[]{:S(2)}, u32[]{:S(2)}) %collective-permute-start.9) | collective-permute-done | bytes 139296 | tf_op jit(solution)/shard_map/directions_space/ppermute | solution.py:444
  29.9 2.4 %collective-permute-done.5 = f32[2,2,264,128]{3,2,1,0:T(8,128)S(1)} collective-permute-done((f32[2,2,264,128]{3,2,1,0:T(8,128)S(1)}, f32[2,2,264,128]{3,2,1,0:T(8,128)S(1)}, u32[]{:S(2)}, u32[]{:S(2)}) %collective-permute-start.5) | collective-permute-done | bytes 540704 | tf_op jit(solution)/shard_map/slab0_column/ppermute | solution.py:449
  33.9 1.6 %collective-permute-start.6 = (f32[2,2,264,128]{3,2,1,0:T(8,128)S(1)}, f32[2,2,264,128]{3,2,1,0:T(8,128)}, u32[]{:S(2)}, u32[]{:S(2)}) collective-permute-start(f32[2,2,264,128]{3,2,1,0:T(8,128)S(1)} %broadcast_select_fusion.1.s_a), channel_id=1, source_target_pairs={{0,1},{1,0},{2,3},{3,2},{4,5},{5,4},{6,7},{7,6},{8,9},{9,8},{10,11... | collective-permute-start | bytes 1622024 | tf_op jit(solution)/shard_map/slab0_pair/ppermute | solution.py:461
  35.4 3.3 %collective-permute-start.2 = (f32[1056,128]{1,0:T(8,128)S(1)}, f32[1056,128]{1,0:T(8,128)S(1)}, u32[]{:S(2)}, u32[]{:S(2)}) collective-permute-start(f32[1056,128]{1,0:T(8,128)S(1)} %collective-permute-done.1.rate_e), channel_id=1, source_target_pairs={{0,2},{2,4},{4,6},{3,1},{5,3},{7,5},{8,10},{10,12},{12,14},{11,9},... | collective-permute-start | bytes 1622024 | tf_op jit(solution)/shard_map/rate_ahead/ppermute | solution.py:453
  39.4 4.8 %collective-permute-done.11 = f32[2,2,264,128]{3,2,1,0:T(8,128)} collective-permute-done((f32[2,2,264,128]{3,2,1,0:T(8,128)S(1)}, f32[2,2,264,128]{3,2,1,0:T(8,128)}, u32[]{:S(2)}, u32[]{:S(2)}) %collective-permute-start.11) | collective-permute-done | bytes 540704 | tf_op jit(solution)/shard_map/slab0_column/ppermute | solution.py:451
  45.3 1.9 %collective-permute-done.2.rate_l = f32[1056,128]{1,0:T(8,128)S(1)} collective-permute-done((f32[1056,128]{1,0:T(8,128)S(1)}, f32[1056,128]{1,0:T(8,128)S(1)}, u32[]{:S(2)}, u32[]{:S(2)}) %collective-permute-start.2) | collective-permute-done | bytes 540704 | tf_op jit(solution)/shard_map/rate_ahead/ppermute | solution.py:453
  47.2 5.2 %collective-permute-start.18 = (f32[2,2,264,128]{3,2,1,0:T(8,128)}, f32[2,2,264,128]{3,2,1,0:T(8,128)}, u32[]{:S(2)}, u32[]{:S(2)}) collective-permute-start(f32[2,2,264,128]{3,2,1,0:T(8,128)} %collective-permute-done.6.e_a), channel_id=1, source_target_pairs={{0,2},{2,4},{4,6},{3,1},{5,3},{7,5},{8,10},{10,12},{12,14},{11,9},... | collective-permute-start | bytes 1622024 | tf_op jit(solution)/shard_map/slab0_ahead/ppermute | solution.py:484
  55.0 5.2 %collective-permute-start.14 = (f32[264,128]{1,0:T(8,128)S(1)}, f32[264,128]{1,0:T(8,128)}, u32[]{:S(2)}, u32[]{:S(2)}) collective-permute-start(f32[264,128]{1,0:T(8,128)S(1)} %get-tuple-element.63), channel_id=1, source_target_pairs={{0,2},{2,4},{4,6},{3,1},{5,3},{7,5},{8,10},{10,12},{12,14},{11,9},... | collective-permute-start | bytes 405512 | tf_op jit(solution)/shard_map/far_layers/ppermute | solution.py:467
  61.0 6.7 %expand.1.v = f32[4,8,264,128]{3,2,1,0:T(8,128)S(1)} custom-call(s32[3]{0:T(128)S(1)} %copy-done.2, s32[16]{0:T(128)S(1)} %pad_add_fusion.1.where, f32[2,136,128]{2,1,0:T(8,128)S(1)} %pad_maximum_fusion.refs_0_, f32[2,136,128]{2,1,0:T(8,128)S(1)} %collective-permute-done.8.refs_1_, f32[2,136,128]{2,1,0:T(8,128)S(1)} %collective-permute-done.9.refs_2_, ...), custom_call_target="tpu_custom_call" | custom-call | bytes 26214400 | tf_op jit(solution)/shard_map/expand/pallas_call | solution.py:470
  67.8 2.2 %collective-permute-start.19 = (f32[2,2,264,128]{3,2,1,0:T(8,128)}, f32[2,2,264,128]{3,2,1,0:T(8,128)S(1)}, u32[]{:S(2)}, u32[]{:S(2)}) collective-permute-start(f32[2,2,264,128]{3,2,1,0:T(8,128)} %collective-permute-done.12.e_b), channel_id=1, source_target_pairs={{0,2},{2,4},{4,6},{3,1},{5,3},{7,5},{8,10},{10,12},{12,14},{11,9},... | collective-permute-start | bytes 1622024 | tf_op jit(solution)/shard_map/slab0_ahead/ppermute | solution.py:485
  71.8 5.4 %collective-permute-done.19.l_b = f32[2,2,264,128]{3,2,1,0:T(8,128)S(1)} collective-permute-done((f32[2,2,264,128]{3,2,1,0:T(8,128)}, f32[2,2,264,128]{3,2,1,0:T(8,128)S(1)}, u32[]{:S(2)}, u32[]{:S(2)}) %collective-permute-start.19) | collective-permute-done | bytes 540704 | tf_op jit(solution)/shard_map/slab0_ahead/ppermute | solution.py:485
  77.1 4.0 %collective-permute-done.16 = f32[2,2,264,128]{3,2,1,0:T(8,128)S(1)} collective-permute-done((f32[2,2,264,128]{3,2,1,0:T(8,128)S(1)}, f32[2,2,264,128]{3,2,1,0:T(8,128)S(1)}, u32[]{:S(2)}, u32[]{:S(2)}) %collective-permute-start.16) | collective-permute-done | bytes 540704 | tf_op jit(solution)/shard_map/slab1_pair/ppermute | solution.py:488
  81.2 4.1 %collective-permute-start.20 = (f32[2,2,264,128]{3,2,1,0:T(8,128)S(1)}, f32[2,2,264,128]{3,2,1,0:T(8,128)S(1)}, u32[]{:S(2)}, u32[]{:S(2)}) collective-permute-start(f32[2,2,264,128]{3,2,1,0:T(8,128)S(1)} %collective-permute-done.16), channel_id=1, source_target_pairs={{0,2},{2,4},{4,6},{3,1},{5,3},{7,5},{8,10},{10,12},{12,14},{11,9},... | collective-permute-start | bytes 1622024 | tf_op jit(solution)/shard_map/slab1_ahead/ppermute | solution.py:490
  85.4 13.5 %first_step.1.state = f32[2,4,10,280,128]{4,3,2,1,0:T(8,128)S(1)} custom-call(s32[3]{0:T(128)S(1)} %copy-done.2, f32[1056,128]{1,0:T(8,128)S(1)} %get-tuple-element.30.rate_m, f32[1056,128]{1,0:T(8,128)S(1)} %collective-permute-done.1.rate_e, f32[1056,128]{1,0:T(8,128)S(1)} %collective-permute-done.2.rate_l, ...), custom_call_target="tpu_custom_call" | custom-call | bytes 52428800 | tf_op jit(solution)/shard_map/first_step/pallas_call | solution.py:497
  100.5 15.7 %second_step.1 = (f32[2,2,4,512,128]{4,3,2,1,0:T(8,128)}, f32[2,2,4,256,128]{4,3,2,1,0:T(8,128)}, f32[2,2,16,128]{3,2,1,0:T(8,128)S(1)}, f32[2,2,16,128]{3,2,1,0:T(8,128)S(1)}) custom-call(s32[3]{0:T(128)S(1)} %copy-done.2, f32[1056,128]{1,0:T(8,128)S(1)} %get-tuple-element.30.rate_m, f32[1056,128]{1,0:T(8,128)S(1)} %collective-permute-done.1.rate_e, ...), custom_call_target="tpu_custom_call" | custom-call | bytes 57671680 | tf_op jit(solution)/shard_map/second_step/pallas_call | solution.py:516
  116.3 9.0 %collective-permute-start.22 = (f32[2,2,16,128]{3,2,1,0:T(8,128)S(1)}, f32[2,2,16,128]{3,2,1,0:T(8,128)S(1)}, u32[]{:S(2)}, u32[]{:S(2)}) collective-permute-start(f32[2,2,16,128]{3,2,1,0:T(8,128)S(1)} %get-tuple-element.50), channel_id=1, source_target_pairs={{0,1},{1,0},{2,3},{3,2},{4,5},{5,4},{6,7},{7,6},{8,9},{9,8},{10,11... | collective-permute-start | bytes 98312 | tf_op jit(solution)/shard_map/means_near/ppermute | solution.py:551
  130.8 2.4 %collective-permute-start.25 = (f32[2,2,32,128]{3,2,1,0:T(8,128)S(1)}, f32[2,2,32,128]{3,2,1,0:T(8,128)S(1)}, u32[]{:S(2)}, u32[]{:S(2)}) collective-permute-start(f32[2,2,32,128]{3,2,1,0:T(8,128)S(1)} %get-tuple-element.66), channel_id=1, source_target_pairs={{0,6},{1,7},{2,4},{3,5},{4,2},{5,3},{6,0},{7,1},{8,14},{9,15},{10,... | collective-permute-start | bytes 196616 | tf_op jit(solution)/shard_map/means_space/ppermute | solution.py:561
  137.1 2.9 %finish.1 = f32[2,2,4,512,128]{4,3,2,1,0:T(8,128)} custom-call(s32[3]{0:T(128)} %pad_add_fusion.scal, f32[2,2,4,512,128]{4,3,2,1,0:T(8,128)} %get-tuple-element.48.held, f32[2,2,4,256,128]{4,3,2,1,0:T(8,128)} %copy-done.7), custom_call_target="tpu_custom_call", output_to_operand_aliasing={{}: (1, {})} | custom-call | bytes 8388608 | tf_op jit(solution)/shard_map/finish/pallas_call | solution.py:562
  (86 shorter events, 25.2 us)
Async XLA Ops:
  4.8 7.8 %collective-permute-start = (f32[2,4,264,128]{3,2,1,0:T(8,128)S(1)}, f32[2,4,264,128]{3,2,1,0:T(8,128)}, u32[]{:S(2)}, u32[]{:S(2)}) collective-permute-start(f32[2,4,264,128]{3,2,1,0:T(8,128)S(1)} %get-tuple-element.29), channel_id=1, source_target_pairs={{0,8},{8,0},{16,24},{24,16},{1,9},{9,1},{17,25},{25,17},{2,10},{10... | collective-permute-start | bytes 3244040 | tf_op jit(solution)/shard_map/store_core/ppermute | solution.py:421
  15.0 12.2 %collective-permute-start.10 = (f32[2,136,128]{2,1,0:T(8,128)S(1)}, f32[2,136,128]{2,1,0:T(8,128)S(1)}, u32[]{:S(2)}, u32[]{:S(2)}) collective-permute-start(f32[2,136,128]{2,1,0:T(8,128)S(1)} %pad_maximum_fusion.refs_0_), channel_id=1, source_target_pairs={{0,6},{1,7},{2,4},{3,5},{4,2},{5,3},{6,0},{7,1},{8,14},{9,15},{10,... | collective-permute-start | bytes 417800 | tf_op jit(solution)/shard_map/directions_space/ppermute | solution.py:444
  19.1 8.2 %collective-permute-start.8 = (f32[2,136,128]{2,1,0:T(8,128)S(1)}, f32[2,136,128]{2,1,0:T(8,128)S(1)}, u32[]{:S(2)}, u32[]{:S(2)}) collective-permute-start(f32[2,136,128]{2,1,0:T(8,128)S(1)} %pad_maximum_fusion.refs_0_), channel_id=1, source_target_pairs={{0,2},{1,3},{2,0},{3,1},{4,6},{5,7},{6,4},{7,5},{8,10},{9,11},{10,... | collective-permute-start | bytes 417800 | tf_op jit(solution)/shard_map/directions_space/ppermute | solution.py:444
  19.1 10.9 %collective-permute-start.9 = (f32[2,136,128]{2,1,0:T(8,128)S(1)}, f32[2,136,128]{2,1,0:T(8,128)S(1)}, u32[]{:S(2)}, u32[]{:S(2)}) collective-permute-start(f32[2,136,128]{2,1,0:T(8,128)S(1)} %pad_maximum_fusion.refs_0_), channel_id=1, source_target_pairs={{0,4},{1,5},{2,6},{3,7},{4,0},{5,1},{6,2},{7,3},{8,12},{9,13},{10,... | collective-permute-start | bytes 417800 | tf_op jit(solution)/shard_map/directions_space/ppermute | solution.py:444
  19.7 12.6 %collective-permute-start.5 = (f32[2,2,264,128]{3,2,1,0:T(8,128)S(1)}, f32[2,2,264,128]{3,2,1,0:T(8,128)S(1)}, u32[]{:S(2)}, u32[]{:S(2)}) collective-permute-start(f32[2,2,264,128]{3,2,1,0:T(8,128)S(1)} %slice_select_fusion), channel_id=1, source_target_pairs={{0,16},{8,24},{16,0},{24,8},{1,17},{9,25},{17,1},{25,9},{2,18},{10... | collective-permute-start | bytes 1622024 | tf_op jit(solution)/shard_map/slab0_column/ppermute | solution.py:449
  21.3 12.5 %collective-permute-start.1 = (f32[1056,128]{1,0:T(8,128)S(1)}, f32[1056,128]{1,0:T(8,128)S(1)}, u32[]{:S(2)}, u32[]{:S(2)}) collective-permute-start(f32[1056,128]{1,0:T(8,128)S(1)} %get-tuple-element.30.rate_m), channel_id=1, source_target_pairs={{0,1},{1,0},{2,3},{3,2},{4,5},{5,4},{6,7},{7,6},{8,9},{9,8},{10,11... | collective-permute-start | bytes 1622024 | tf_op jit(solution)/shard_map/rate_pair/ppermute | solution.py:447
  32.3 11.8 %collective-permute-start.11 = (f32[2,2,264,128]{3,2,1,0:T(8,128)S(1)}, f32[2,2,264,128]{3,2,1,0:T(8,128)}, u32[]{:S(2)}, u32[]{:S(2)}) collective-permute-start(f32[2,2,264,128]{3,2,1,0:T(8,128)S(1)} %get-tuple-element.39), channel_id=1, source_target_pairs={{0,16},{8,24},{16,0},{24,8},{1,17},{9,25},{17,1},{25,9},{2,18},{10... | collective-permute-start | bytes 1622024 | tf_op jit(solution)/shard_map/slab0_column/ppermute | solution.py:451
  33.9 11.4 %collective-permute-start.6 = (f32[2,2,264,128]{3,2,1,0:T(8,128)S(1)}, f32[2,2,264,128]{3,2,1,0:T(8,128)}, u32[]{:S(2)}, u32[]{:S(2)}) collective-permute-start(f32[2,2,264,128]{3,2,1,0:T(8,128)S(1)} %broadcast_select_fusion.1.s_a), channel_id=1, source_target_pairs={{0,1},{1,0},{2,3},{3,2},{4,5},{5,4},{6,7},{7,6},{8,9},{9,8},{10,11... | collective-permute-start | bytes 1622024 | tf_op jit(solution)/shard_map/slab0_pair/ppermute | solution.py:461
  35.4 11.8 %collective-permute-start.2 = (f32[1056,128]{1,0:T(8,128)S(1)}, f32[1056,128]{1,0:T(8,128)S(1)}, u32[]{:S(2)}, u32[]{:S(2)}) collective-permute-start(f32[1056,128]{1,0:T(8,128)S(1)} %collective-permute-done.1.rate_e), channel_id=1, source_target_pairs={{0,2},{2,4},{4,6},{3,1},{5,3},{7,5},{8,10},{10,12},{12,14},{11,9},... | collective-permute-start | bytes 1622024 | tf_op jit(solution)/shard_map/rate_ahead/ppermute | solution.py:453
  47.2 20.5 %collective-permute-start.18 = (f32[2,2,264,128]{3,2,1,0:T(8,128)}, f32[2,2,264,128]{3,2,1,0:T(8,128)}, u32[]{:S(2)}, u32[]{:S(2)}) collective-permute-start(f32[2,2,264,128]{3,2,1,0:T(8,128)} %collective-permute-done.6.e_a), channel_id=1, source_target_pairs={{0,2},{2,4},{4,6},{3,1},{5,3},{7,5},{8,10},{10,12},{12,14},{11,9},... | collective-permute-start | bytes 1622024 | tf_op jit(solution)/shard_map/slab0_ahead/ppermute | solution.py:484
  52.4 15.3 %collective-permute-start.12 = (f32[2,2,264,128]{3,2,1,0:T(8,128)S(1)}, f32[2,2,264,128]{3,2,1,0:T(8,128)}, u32[]{:S(2)}, u32[]{:S(2)}) collective-permute-start(f32[2,2,264,128]{3,2,1,0:T(8,128)S(1)} %broadcast_select_fusion.s_b), channel_id=1, source_target_pairs={{0,1},{1,0},{2,3},{3,2},{4,5},{5,4},{6,7},{7,6},{8,9},{9,8},{10,11... | collective-permute-start | bytes 1622024 | tf_op jit(solution)/shard_map/slab0_pair/ppermute | solution.py:469
  52.4 17.6 %collective-permute-start.7 = (f32[2,2,264,128]{3,2,1,0:T(8,128)}, f32[2,2,264,128]{3,2,1,0:T(8,128)}, u32[]{:S(2)}, u32[]{:S(2)}) collective-permute-start(f32[2,2,264,128]{3,2,1,0:T(8,128)} %get-tuple-element.36), channel_id=1, source_target_pairs={{0,16},{8,24},{16,0},{24,8},{1,17},{9,25},{17,1},{25,9},{2,18},{10... | collective-permute-start | bytes 1622024 | tf_op jit(solution)/shard_map/slab1_column/ppermute | solution.py:481
  53.7 14.1 %collective-permute-start.13 = (f32[264,128]{1,0:T(8,128)}, f32[264,128]{1,0:T(8,128)S(1)}, u32[]{:S(2)}, u32[]{:S(2)}) collective-permute-start(f32[264,128]{1,0:T(8,128)} %get-tuple-element.64), channel_id=1, source_target_pairs={{2,0},{4,2},{6,4},{1,3},{3,5},{5,7},{10,8},{12,10},{14,12},{9,11},... | collective-permute-start | bytes 405512 | tf_op jit(solution)/shard_map/far_layers/ppermute | solution.py:466
  55.0 12.8 %collective-permute-start.14 = (f32[264,128]{1,0:T(8,128)S(1)}, f32[264,128]{1,0:T(8,128)}, u32[]{:S(2)}, u32[]{:S(2)}) collective-permute-start(f32[264,128]{1,0:T(8,128)S(1)} %get-tuple-element.63), channel_id=1, source_target_pairs={{0,2},{2,4},{4,6},{3,1},{5,3},{7,5},{8,10},{10,12},{12,14},{11,9},... | collective-permute-start | bytes 405512 | tf_op jit(solution)/shard_map/far_layers/ppermute | solution.py:467
  67.8 9.4 %collective-permute-start.19 = (f32[2,2,264,128]{3,2,1,0:T(8,128)}, f32[2,2,264,128]{3,2,1,0:T(8,128)S(1)}, u32[]{:S(2)}, u32[]{:S(2)}) collective-permute-start(f32[2,2,264,128]{3,2,1,0:T(8,128)} %collective-permute-done.12.e_b), channel_id=1, source_target_pairs={{0,2},{2,4},{4,6},{3,1},{5,3},{7,5},{8,10},{10,12},{12,14},{11,9},... | collective-permute-start | bytes 1622024 | tf_op jit(solution)/shard_map/slab0_ahead/ppermute | solution.py:485
  71.2 10.0 %collective-permute-start.16 = (f32[2,2,264,128]{3,2,1,0:T(8,128)S(1)}, f32[2,2,264,128]{3,2,1,0:T(8,128)S(1)}, u32[]{:S(2)}, u32[]{:S(2)}) collective-permute-start(f32[2,2,264,128]{3,2,1,0:T(8,128)S(1)} %broadcast_select_fusion.3.s_a), channel_id=1, source_target_pairs={{0,1},{1,0},{2,3},{3,2},{4,5},{5,4},{6,7},{7,6},{8,9},{9,8},{10,11... | collective-permute-start | bytes 1622024 | tf_op jit(solution)/shard_map/slab1_pair/ppermute | solution.py:488
  71.2 14.0 %collective-permute-start.15 = (f32[2,2,264,128]{3,2,1,0:T(8,128)S(1)}, f32[2,2,264,128]{3,2,1,0:T(8,128)S(1)}, u32[]{:S(2)}, u32[]{:S(2)}) collective-permute-start(f32[2,2,264,128]{3,2,1,0:T(8,128)S(1)} %copy-done.4), channel_id=1, source_target_pairs={{0,16},{8,24},{16,0},{24,8},{1,17},{9,25},{17,1},{25,9},{2,18},{10... | collective-permute-start | bytes 1622024 | tf_op jit(solution)/shard_map/slab1_column/ppermute | solution.py:482
  81.2 17.7 %collective-permute-start.20 = (f32[2,2,264,128]{3,2,1,0:T(8,128)S(1)}, f32[2,2,264,128]{3,2,1,0:T(8,128)S(1)}, u32[]{:S(2)}, u32[]{:S(2)}) collective-permute-start(f32[2,2,264,128]{3,2,1,0:T(8,128)S(1)} %collective-permute-done.16), channel_id=1, source_target_pairs={{0,2},{2,4},{4,6},{3,1},{5,3},{7,5},{8,10},{10,12},{12,14},{11,9},... | collective-permute-start | bytes 1622024 | tf_op jit(solution)/shard_map/slab1_ahead/ppermute | solution.py:490
  85.3 13.6 %collective-permute-start.17 = (f32[2,2,264,128]{3,2,1,0:T(8,128)S(1)}, f32[2,2,264,128]{3,2,1,0:T(8,128)S(1)}, u32[]{:S(2)}, u32[]{:S(2)}) collective-permute-start(f32[2,2,264,128]{3,2,1,0:T(8,128)S(1)} %broadcast_select_fusion.2.s_b), channel_id=1, source_target_pairs={{0,1},{1,0},{2,3},{3,2},{4,5},{5,4},{6,7},{7,6},{8,9},{9,8},{10,11... | collective-permute-start | bytes 1622024 | tf_op jit(solution)/shard_map/slab1_pair/ppermute | solution.py:493
  116.2 10.4 %collective-permute-start.21 = (f32[2,2,16,128]{3,2,1,0:T(8,128)S(1)}, f32[2,2,16,128]{3,2,1,0:T(8,128)S(1)}, u32[]{:S(2)}, u32[]{:S(2)}) collective-permute-start(f32[2,2,16,128]{3,2,1,0:T(8,128)S(1)} %get-tuple-element.51), channel_id=1, source_target_pairs={{0,8},{8,0},{16,24},{24,16},{1,9},{9,1},{17,25},{25,17},{2,10},{10... | collective-permute-start | bytes 98312 | tf_op jit(solution)/shard_map/means_near/ppermute | solution.py:550
  116.3 11.0 %collective-permute-start.22 = (f32[2,2,16,128]{3,2,1,0:T(8,128)S(1)}, f32[2,2,16,128]{3,2,1,0:T(8,128)S(1)}, u32[]{:S(2)}, u32[]{:S(2)}) collective-permute-start(f32[2,2,16,128]{3,2,1,0:T(8,128)S(1)} %get-tuple-element.50), channel_id=1, source_target_pairs={{0,1},{1,0},{2,3},{3,2},{4,5},{5,4},{6,7},{7,6},{8,9},{9,8},{10,11... | collective-permute-start | bytes 98312 | tf_op jit(solution)/shard_map/means_near/ppermute | solution.py:551
  128.7 7.1 %collective-permute-start.24 = (f32[2,2,4,256,128]{4,3,2,1,0:T(8,128)}, f32[2,2,4,256,128]{4,3,2,1,0:T(8,128)S(1)}, u32[]{:S(2)}, u32[]{:S(2)}) collective-permute-start(f32[2,2,4,256,128]{4,3,2,1,0:T(8,128)} %get-tuple-element.52), channel_id=1, source_target_pairs={{0,8},{8,0},{16,24},{24,16},{1,9},{9,1},{17,25},{25,17},{2,10},{10... | collective-permute-start | bytes 6291464 | tf_op jit(solution)/shard_map/tangent_core/ppermute | solution.py:553
  130.2 9.9 %collective-permute-start.27 = (f32[2,2,32,128]{3,2,1,0:T(8,128)S(1)}, f32[2,2,32,128]{3,2,1,0:T(8,128)S(1)}, u32[]{:S(2)}, u32[]{:S(2)}) collective-permute-start(f32[2,2,32,128]{3,2,1,0:T(8,128)S(1)} %get-tuple-element.58), channel_id=1, source_target_pairs={{0,2},{1,3},{2,0},{3,1},{4,6},{5,7},{6,4},{7,5},{8,10},{9,11},{10,... | collective-permute-start | bytes 196616 | tf_op jit(solution)/shard_map/means_space/ppermute | solution.py:561
  130.8 9.4 %collective-permute-start.25 = (f32[2,2,32,128]{3,2,1,0:T(8,128)S(1)}, f32[2,2,32,128]{3,2,1,0:T(8,128)S(1)}, u32[]{:S(2)}, u32[]{:S(2)}) collective-permute-start(f32[2,2,32,128]{3,2,1,0:T(8,128)S(1)} %get-tuple-element.66), channel_id=1, source_target_pairs={{0,6},{1,7},{2,4},{3,5},{4,2},{5,3},{6,0},{7,1},{8,14},{9,15},{10,... | collective-permute-start | bytes 196616 | tf_op jit(solution)/shard_map/means_space/ppermute | solution.py:561
  (17 other events, 103.8 us)

commit v4 on v3

--- a/solution.py
+++ b/solution.py
@@ -52,6 +52,13 @@
     run_all([pltpu.make_async_copy(a, b, sems.at[i]) for i, (a, b) in enumerate(copies)])
 
 
+def parts(value):
+    first = value.astype(jnp.bfloat16)
+    rest = value - first.astype(jnp.float32)
+    second = rest.astype(jnp.bfloat16)
+    return [first, second, (rest - second.astype(jnp.float32)).astype(jnp.bfloat16)]
+
+
 def exact_dot(a, b):
     return jnp.dot(a, b, precision=lax.Precision.HIGHEST, preferred_element_type=jnp.float32)
 
@@ -76,14 +83,17 @@
     shift = rows - 2 * EDGE
     count = held[0].shape[1] // 8
     tall = blocks.shape[1]
-    row = lax.broadcasted_iota(jnp.int32, (rows, 4 * tall), 0) + core * shift
-    column = lax.broadcasted_iota(jnp.int32, (rows, 4 * tall), 1)
+    padded = (rows + 15) // 16 * 16
+    row = lax.broadcasted_iota(jnp.int32, (padded, 4 * tall), 0) + core * shift
+    column = lax.broadcasted_iota(jnp.int32, (padded, 4 * tall), 1)
     place = column % tall
     there = 4 * (place + core * (count - 2)) + column // tall
     pick_rows = ((row // 4 == there) & (place < count)).astype(jnp.float32)
+    pick_rows = jnp.concatenate([pick_rows] * 3, 1).astype(jnp.bfloat16)
     lane = lax.broadcasted_iota(jnp.int32, (128, 512), 0)
     z = lax.broadcasted_iota(jnp.int32, (128, 512), 1)
     pick_lanes = (lane == 32 * (z // 128) + (z % 128) // 4).astype(jnp.float32)
+    pick_lanes = jnp.concatenate([pick_lanes] * 3, 0).astype(jnp.bfloat16)
     blocks[...] = jnp.zeros(blocks.shape, jnp.float32)
     for k in range(8):
         for d in range(4):
@@ -94,7 +104,11 @@
                         hit = (where[k] == 2 * i + j) & (where[8 + k] == h)
                         block = jnp.where(hit, ref[j, pl.ds((2 * d + h) * count, count)], block)
             blocks[d, pl.ds(0, count)] = block
-        wide = exact_dot(blocks[...].reshape(4 * tall, 128), pick_lanes)
+        wide = jnp.dot(
+            jnp.concatenate(parts(blocks[...].reshape(4 * tall, 128)), 1),
+            pick_lanes,
+            preferred_element_type=jnp.float32,
+        )
         table = jnp.concatenate(
             [
                 jnp.concatenate(
@@ -104,7 +118,9 @@
             ],
             1,
         )
-        filled = exact_dot(pick_rows, table)
+        filled = jnp.dot(
+            pick_rows, jnp.concatenate(parts(table), 0), preferred_element_type=jnp.float32
+        )[:rows]
         for d in range(4):
             vfine[d, k] = filled[:, 128 * d : 128 * (d + 1)]
 
@@ -124,11 +140,11 @@
     return here, total, ref[lead, before, pl.ds(PAD + at, rows)]
 
 
-def clear_pads(ref):
-    dirs, layers, rows, lanes = ref.shape
+def clear_pads(ref, layers=None):
+    dirs, every, rows, lanes = ref.shape
     zero = jnp.zeros((dirs, PAD, lanes), jnp.float32)
 
-    @pl.loop(0, layers)
+    @pl.loop(0, layers or every)
     def _(i):
         ref[:, i, pl.ds(0, PAD)] = zero
         ref[:, i, pl.ds(rows - PAD, PAD)] = zero
@@ -158,44 +174,10 @@
             )
 
 
-def first_step(
-    scal, rate_m, rate_e, rate_l, s_a, s_b, e_a, e_b, l_a, l_b, far_e, far_l, v,
-    state, rate, slab, far, q1, p2, q2, sems,
-):
-    sigma = 1 - 2 * scal[1]
-    has_late = scal[2]
-    p3, q3 = state.at[0], state.at[1]
+def weigh(low, high, rate, slab, v, q1):
     rows = rate.shape[1]
-    moves = [(rate_m.at[pl.ds(rows * j, rows)], rate.at[4 + j]) for j in range(4)]
-    moves += [(s_a, slab.at[:, pl.ds(4, 2)]), (s_b, slab.at[:, pl.ds(6, 2)])]
-    for j in range(4):
-        moves.append((rate_e.at[pl.ds(rows * j, rows)], rate.at[11 - j]))
-        moves.append((rate_l.at[pl.ds(rows * j, rows)], rate.at[3 - j]))
-    for j in range(2):
-        moves.append((e_a.at[:, j], slab.at[:, 11 - j]))
-        moves.append((e_b.at[:, j], slab.at[:, 9 - j]))
-        moves.append((l_a.at[:, j], slab.at[:, 3 - j]))
-        moves.append((l_b.at[:, j], slab.at[:, 1 - j]))
-    moves += [(far_l, far.at[0]), (far_e, far.at[1])]
-    copies = [pltpu.make_async_copy(a, b, sems.at[i]) for i, (a, b) in enumerate(moves)]
-    for copy in copies:
-        copy.start()
-    for ref in (q1, p2, q2, p3, q3):
-        clear_pads(ref)
-    for ref in (p2, q2):
-        clear_layer(ref, 3)
-    for ref in (p3, q3):
-        clear_layer(ref, 2)
-    for copy in copies:
-        copy.wait()
-
-    for i, (layer, coarse) in enumerate(((0, 0), (13, 7))):
-        for at, n in chunks(rows):
-            w = far[i, pl.ds(at, n)]
-            for d in range(4):
-                q1[d, layer, pl.ds(PAD + at, n)] = w * v[d, coarse, pl.ds(at, n)]
-
-    @pl.loop(0, 12)
+
+    @pl.loop(low, high)
     def _(i):
         coarse = (i + 2) // 2
         for at, n in chunks(rows):
@@ -208,7 +190,18 @@
             for d in range(4):
                 q1[d, i + 1, pl.ds(PAD + at, n)] = w * v[d, coarse, pl.ds(at, n)]
 
-    @pl.loop(jnp.where(has_late == 1, 0, 4), 12)
+
+def outermost(far, layer, coarse, v, q1):
+    for at, n in chunks(far.shape[0]):
+        w = far[pl.ds(at, n)]
+        for d in range(4):
+            q1[d, layer, pl.ds(PAD + at, n)] = w * v[d, coarse, pl.ds(at, n)]
+
+
+def second_update(low, high, sigma, slab, q1, p2, q2):
+    rows = slab.shape[2]
+
+    @pl.loop(low, high)
     def _(i):
         for at, n in chunks(rows):
             both = slab[0, i, pl.ds(at, n)] - slab[1, i, pl.ds(at, n)]
@@ -219,7 +212,11 @@
                 p2[d, i, pl.ds(PAD + at, n)] = -(spread_a * (total + back_a * back) + hold_a * q)
                 q2[d, i, pl.ds(PAD + at, n)] = spread_b * (total + back_b * back) + hold_b * q
 
-    @pl.loop(jnp.where(has_late == 1, 0, 3), 10)
+
+def third_update(low, high, sigma, slab, q1, p2, q2, p3, q3, shift):
+    rows = slab.shape[2]
+
+    @pl.loop(low, high)
     def _(i):
         for at, n in chunks(rows):
             a = slab[0, i + 1, pl.ds(at, n)]
@@ -230,23 +227,108 @@
                 p, p_sum, p_back = around(p2, d, i + 1, i + 1 - sigma, i + 1 + sigma, at, n)
                 q, q_sum, q_back = around(q2, d, i + 1, i + 1 - sigma, i + 1 + sigma, at, n)
                 w = q1[d, i + 2, pl.ds(PAD + at, n)]
-                p3[d, i, pl.ds(PAD + at, n)] = (
+                p3[d, i - shift, pl.ds(PAD + at, n)] = (
                     spread_a * (p_sum + back_a * p_back) + hold_a * p - (a * q + w)
                 )
-                q3[d, i, pl.ds(PAD + at, n)] = (
+                q3[d, i - shift, pl.ds(PAD + at, n)] = (
                     spread_b * (q_sum + back_b * q_back) + hold_b * q + (b * p + w)
                 )
 
 
+def first_step(
+    scal, rate_m, rate_e, rate_l, s_a, s_b, e_a, e_b, l_a, far_e, v,
+    state, edge1, edge2, edge_slab, rate, slab, far, q1, p2, q2, sems,
+):
+    sigma = 1 - 2 * scal[1]
+    has_late = scal[2]
+    p3, q3 = state.at[0], state.at[1]
+    rows = rate.shape[1]
+    moves = [(rate_m.at[pl.ds(rows * j, rows)], rate.at[4 + j]) for j in range(4)]
+    moves += [(s_a, slab.at[:, pl.ds(4, 2)]), (s_b, slab.at[:, pl.ds(6, 2)])]
+    for j in range(4):
+        moves.append((rate_e.at[pl.ds(rows * j, rows)], rate.at[11 - j]))
+    for j in range(2):
+        moves.append((rate_l.at[pl.ds(rows * j, rows)], rate.at[3 - j]))
+        moves.append((e_a.at[:, j], slab.at[:, 11 - j]))
+        moves.append((e_b.at[:, j], slab.at[:, 9 - j]))
+        moves.append((l_a.at[:, j], slab.at[:, 3 - j]))
+    moves.append((far_e, far))
+    copies = [pltpu.make_async_copy(a, b, sems.at[i]) for i, (a, b) in enumerate(moves)]
+    for copy in copies:
+        copy.start()
+    for ref in (q1, p2, q2, p3, q3):
+        clear_pads(ref)
+
+    @pl.when(has_late == 0)
+    def _():
+        for ref in (p2, q2):
+            clear_layer(ref, 3)
+
+    for copy in copies:
+        copy.wait()
+    outermost(far, 13, 7, v, q1)
+    weigh(2, 12, rate, slab, v, q1)
+    second_update(jnp.where(has_late == 1, 3, 4), 12, sigma, slab, q1, p2, q2)
+    moves = [(q1.at[:, pl.ds(3, 2)], edge1), (slab.at[:, pl.ds(2, 2)], edge_slab)]
+    moves += [(p2.at[:, pl.ds(3, 2)], edge2.at[0]), (q2.at[:, pl.ds(3, 2)], edge2.at[1])]
+    copies = [pltpu.make_async_copy(a, b, sems.at[i]) for i, (a, b) in enumerate(moves)]
+    for copy in copies:
+        copy.start()
+    third_update(3, 10, sigma, slab, q1, p2, q2, p3, q3, 3)
+    for copy in copies:
+        copy.wait()
+
+
+def late_layers(
+    scal, rate_l, l_b, far_l, v, state, edge1, edge2, edge_slab,
+    late, rate, slab, far, q1, p2, q2, sems,
+):
+    sigma = 1 - 2 * scal[1]
+    rows = rate.shape[1]
+    p3, q3 = late.at[0], late.at[1]
+    kept = [
+        pltpu.make_async_copy(state.at[i, :, pl.ds(0, 2)], late.at[i, :, pl.ds(3, 2)], sems.at[i])
+        for i in range(2)
+    ]
+    for copy in kept:
+        copy.start()
+
+    @pl.when(scal[2] == 0)
+    def _():
+        for ref in (p3, q3):
+            clear_layer(ref, 2)
+
+    @pl.when(scal[2] == 1)
+    def _():
+        moves = [(far_l, far), (edge1, q1.at[:, pl.ds(3, 2)]), (edge_slab, slab.at[:, pl.ds(2, 2)])]
+        moves += [(edge2.at[0], p2.at[:, pl.ds(3, 2)]), (edge2.at[1], q2.at[:, pl.ds(3, 2)])]
+        for j in range(2):
+            moves.append((rate_l.at[pl.ds(rows * (2 + j), rows)], rate.at[1 - j]))
+            moves.append((l_b.at[:, j], slab.at[:, 1 - j]))
+        copies = [pltpu.make_async_copy(a, b, sems.at[2 + i]) for i, (a, b) in enumerate(moves)]
+        for copy in copies:
+            copy.start()
+        for ref in (q1, p2, q2, p3, q3):
+            clear_pads(ref, 3)
+        for copy in copies:
+            copy.wait()
+        outermost(far, 0, 0, v, q1)
+        weigh(0, 2, rate, slab, v, q1)
+        second_update(0, 3, sigma, slab, q1, p2, q2)
+        third_update(0, 3, sigma, slab, q1, p2, q2, p3, q3, 0)
+
+    for copy in kept:
+        copy.wait()
+
+
 def second_step(
-    scal, rate_m, rate_e, rate_l, s_a, s_b, e_b, l_a, v, state,
+    scal, rate_m, rate_e, rate_l, s_a, s_b, e_b, l_a, v, state, late,
     tangent, sent, means, means_sib, rate, slab, weight, p4, q4, p5, q5, p6, q6, sems, out_sems,
 ):
     core, odd, has_late = scal[0], scal[1], scal[2]
     sigma = 1 - 2 * odd
     rows = rate.shape[1]
     half = rows - EDGE
-    p3, q3 = state.at[0], state.at[1]
     moves = [(rate_m.at[pl.ds(rows * j, rows)], rate.at[2 + j]) for j in range(4)]
     moves += [(s_a, slab.at[:, pl.ds(2, 2)]), (s_b, slab.at[:, pl.ds(4, 2)])]
     for j in range(2):
@@ -259,10 +341,12 @@
         copy.start()
     for ref in (p4, q4, p5, q5):
         clear_pads(ref)
-    for ref in (p4, q4):
-        clear_layer(ref, 1)
-    for ref in (p5, q5):
-        clear_layer(ref, 0)
+
+    @pl.when(has_late == 0)
+    def _():
+        for ref, layer in ((p4, 1), (q4, 1), (p5, 0), (q5, 0)):
+            clear_layer(ref, layer)
+
     for copy in copies:
         copy.wait()
 
@@ -279,9 +363,13 @@
             for d in range(4):
                 weight[d, i, pl.ds(at, n)] = w * v[d, coarse, pl.ds(at, n)]
 
-    @pl.loop(jnp.where(has_late == 1, 0, 2), 8)
-    def _(i):
-        update((p3, q3), (p4, q4, PAD), i, i + 1, i, sigma, slab, weight, rows)
+    @pl.loop(jnp.where(has_late == 1, 0, 2), 3)
+    def _(i):
+        update((late.at[0], late.at[1]), (p4, q4, PAD), i, i + 1, i, sigma, slab, weight, rows)
+
+    @pl.loop(3, 8)
+    def _(i):
+        update((state.at[0], state.at[1]), (p4, q4, PAD), i, i - 2, i, sigma, slab, weight, rows)
 
     @pl.loop(jnp.where(has_late == 1, 0, 1), 6)
     def _(i):
@@ -419,6 +507,7 @@
     )(scal, store, rate)
     with jax.named_scope("store_core"):
         received = to_core(other)
+
     def candidates(step, received):
         here = group == owner_map[step]
         first = jnp.where(here, own[:, :2], received[:, :2])
@@ -428,6 +517,7 @@
         return jnp.where(column == owner_map[step] >> 1, have, came)
 
     have0_a, have0_b = candidates(0, received)
+    have1_a, have1_b = candidates(1, after(received, have0_a))
 
     coarse_own = pl.pallas_call(
         window,
@@ -437,36 +527,33 @@
         name="window",
     )(scal, after(row, rate_m), row_sib)
     with jax.named_scope("directions_pair"):
-        pair = jnp.stack([coarse_own, after(to_pair(coarse_own), have0_a)])
+        pair = jnp.stack([coarse_own, after(to_pair(coarse_own), have0_b)])
     held = [pair]
     for j in range(2, n_space, 2):
         with jax.named_scope("directions_space"):
-            held.append(lax.ppermute(pair, "space", [(i, i ^ j) for i in range(n_space)]))
-    have1_a, have1_b = candidates(1, after(received, have0_a, pair))
+            held.append(lax.ppermute(after(pair), "space", [(i, i ^ j) for i in range(n_space)]))
     with jax.named_scope("rate_pair"):
         rate_e = to_pair(after(rate_m, received))
     with jax.named_scope("slab0_column"):
-        came0_a = to_column(have0_a)
-    with jax.named_scope("slab0_column"):
-        came0_b = to_column(after(have0_b, came0_a, have1_a, have1_b, *held))
+        came0_a = to_column(after(have0_a))
+        came0_b = to_column(after(have0_b, came0_a, have1_a, have1_b))
     with jax.named_scope("rate_ahead"):
-        rate_l = to_ahead(rate_e)
-
+        rate_l = to_ahead(after(rate_e))
+    s0_a = settled(0, have0_a, came0_a)
+    with jax.named_scope("slab0_pair"):
+        e0_a = to_pair(after(s0_a, rate_e, *held))
+    s0_b = settled(0, have0_b, after(came0_b))
+    w_near = rate_scale * rate_m[:rows] * s0_a[0, 0] * s0_a[1, 0]
+    w_late = rate_scale * rate_m[3 * rows : 4 * rows] * s0_b[0, 1] * s0_b[1, 1]
+    with jax.named_scope("far_layers"):
+        far_e = to_behind(after(w_near, rate_l))
+        far_l = to_ahead(after(w_late, rate_l))
+    with jax.named_scope("slab1_column"):
+        came1_a = to_column(after(have1_a, e0_a))
     local_coarse = jnp.arange(8, dtype=jnp.int32) - 3
     coarse_at = 2 * mine + jnp.where(odd == 1, 1 - local_coarse, local_coarse)
     block = block_map[jnp.clip(coarse_at >> 1, 0, n_space - 1)] ^ mine
     coarse_scal = jnp.concatenate([block, coarse_at & 1]).astype(jnp.int32)
-    s0_a = settled(0, have0_a, came0_a)
-    with jax.named_scope("slab0_pair"):
-        e0_a = to_pair(after(s0_a, rate_e))
-    s0_b = settled(0, have0_b, came0_b)
-    w_near = rate_scale * rate_m[:rows] * s0_a[0, 0] * s0_a[1, 0]
-    w_late = rate_scale * rate_m[3 * rows : 4 * rows] * s0_b[0, 1] * s0_b[1, 1]
-    with jax.named_scope("far_layers"):
-        far_e = to_behind(w_near)
-        far_l = to_ahead(w_late)
-    with jax.named_scope("slab0_pair"):
-        e0_b = to_pair(after(s0_b, e0_a))
     vfine = pl.pallas_call(
         expand,
         out_shape=vmem(4, 8, rows, width_z),
@@ -476,42 +563,67 @@
         name="expand",
         cost_estimate=cost(0, 25 << 20),
         compiler_params=params(16),
-    )(scal, coarse_scal, *held)
+    )(scal, coarse_scal, *held[:-1], after(held[-1]))
+    with jax.named_scope("slab0_pair"):
+        e0_b = to_pair(after(s0_b, e0_a))
     with jax.named_scope("slab1_column"):
-        came1_a = to_column(after(have1_a, e0_a))
         came1_b = to_column(after(have1_b, e0_b, far_e, far_l))
     with jax.named_scope("slab0_ahead"):
-        l0_a = to_ahead(after(e0_a, s0_b, rate_l))
+        l0_a = to_ahead(after(e0_a, s0_b))
         l0_b = to_ahead(after(e0_b, l0_a, far_e, far_l, vfine))
     s1_a = settled(1, have1_a, came1_a)
     with jax.named_scope("slab1_pair"):
         e1_a = to_pair(after(s1_a, e0_b))
     with jax.named_scope("slab1_ahead"):
         l1_a = to_ahead(after(e1_a, l0_b))
-    s1_b = settled(1, have1_b, came1_b)
-    with jax.named_scope("slab1_pair"):
-        e1_b = to_pair(after(s1_b, e1_a))
-    l0_b = after(l0_b, s1_b, e1_a)
-
     tall = rows + 2 * PAD
-    state = pl.pallas_call(
+    state, *edges = pl.pallas_call(
         first_step,
-        out_shape=vmem(2, 4, 10, tall, width_z),
-        in_specs=[SMEM] + [ANY] * 11 + [VMEM],
-        out_specs=VMEM,
+        out_shape=(
+            vmem(2, 4, 7, tall, width_z),
+            vmem(4, 2, tall, width_z),
+            vmem(2, 4, 2, tall, width_z),
+            vmem(2, 2, rows, width_z),
+        ),
+        in_specs=[SMEM] + [ANY] * 9 + [VMEM],
+        out_specs=[VMEM] * 4,
         scratch_shapes=[
             vmem(12, rows, width_z),
             vmem(2, 12, rows, width_z),
-            vmem(2, rows, width_z),
+            vmem(rows, width_z),
             vmem(4, 14, tall, width_z),
             vmem(4, 12, tall, width_z),
             vmem(4, 12, tall, width_z),
-            pltpu.SemaphoreType.DMA((24,)),
+            pltpu.SemaphoreType.DMA((19,)),
         ],
         name="first_step",
-        cost_estimate=cost(0, 50 << 20),
-        compiler_params=params(31),
-    )(scal, rate_m, rate_e, rate_l, s0_a, s0_b, e0_a, e0_b, l0_a, l0_b, far_e, far_l, stay(vfine))
+        cost_estimate=cost(0, 40 << 20),
+        compiler_params=params(30),
+    )(scal, rate_m, rate_e, rate_l, s0_a, s0_b, e0_a, e0_b, after(l0_a), far_e, stay(vfine))
+    s1_b = settled(1, have1_b, after(came1_b, state))
+    with jax.named_scope("slab1_pair"):
+        e1_b = to_pair(after(s1_b))
+
+    l0_b = after(l0_b, e1_a, s1_b)
+
+    late = pl.pallas_call(
+        late_layers,
+        out_shape=vmem(2, 4, 5, tall, width_z),
+        in_specs=[SMEM] + [ANY] * 3 + [VMEM] * 5,
+        out_specs=VMEM,
+        scratch_shapes=[
+            vmem(2, rows, width_z),
+            vmem(2, 4, rows, width_z),
+            vmem(rows, width_z),
+            vmem(4, 5, tall, width_z),
+            vmem(4, 5, tall, width_z),
+            vmem(4, 5, tall, width_z),
+            pltpu.SemaphoreType.DMA((11,)),
+        ],
+        name="late_layers",
+        cost_estimate=cost(0, 20 << 20),
+        compiler_params=params(12),
+    )(scal, rate_l, l0_b, far_l, stay(vfine), stay(state), *[stay(x) for x in edges])
 
     tangent, sent, first, second = pl.pallas_call(
         second_step,
@@ -521,7 +633,7 @@
             vmem(2, 2, half // 16, 128),
             vmem(2, 2, half // 16, 128),
         ),
-        in_specs=[SMEM] + [ANY] * 7 + [VMEM] * 2,
+        in_specs=[SMEM] + [ANY] * 7 + [VMEM] * 3,
         out_specs=[ANY, ANY, VMEM, VMEM],
         scratch_shapes=[
             vmem(8, rows, width_z),
@@ -539,7 +651,7 @@
         name="second_step",
         cost_estimate=cost(0, 55 << 20),
         compiler_params=params(36),
-    )(scal, rate_m, rate_e, rate_l, s1_a, s1_b, e1_b, l1_a, stay(vfine), stay(state))
+    )(scal, rate_m, rate_e, rate_l, s1_a, s1_b, e1_b, l1_a, stay(vfine), stay(state), stay(late))
 
 
     def joined(a, b):
@@ -550,7 +662,7 @@
         here = joined(first, to_core(second))
         there = joined(to_pair(first), lax.ppermute(second, ("dir", "space"), both))
     with jax.named_scope("tangent_core"):
-        rest = to_core(after(sent, here, there))
+        rest = to_core(sent)
     source = jnp.sum(jnp.where(block_map == mine, jnp.arange(n_space, dtype=jnp.int32), 0))
     sens = jnp.where(source == mine, here, there)
     came = []

time: 142 us -> 135 us (0.951)
  waiting for transfers between devices: 24.6 us -> 21 us
  Pallas kernels: 42.3 us -> 39.5 us
    ppermute x1, waiting for transfers between devices: 0.01 us -> 6.49 us  [local(): l1_a = to_ahead(after(e1_a, l0_b))]
    ppermute x1, waiting for transfers between devices: 5.37 us -> 0.01 us  [local(): l0_b = to_ahead(after(e0_b, l0_a, far_e, far_l, vfine))]
    ppermute x2, starting transfers between devices: 9.1 us -> 4.09 us  [local(): there = joined(to_pair(first), lax.ppermute(second, ('dir', 'space'), both))]
    ppermute x1, waiting for transfers between devices: 4.04 us -> 0.01 us  [local(): e1_a = to_pair(after(s1_a, e0_b))]
    pallas_call x1, Pallas kernels: 6.74 us -> 3.67 us  [local(): pl.pallas_call(expand, out_shape=vmem(4, 8, rows, width_z), in_specs=[SME...]
    ppermute x1, starting transfers between devices: 2.21 us -> 4.57 us  [local(): l0_b = to_ahead(after(e0_b, l0_a, far_e, far_l, vfine))]
    unnamed x26 -> x40, local copies, waits for them, and re-layouts: 4.57 us -> 5.6 us
    pallas_call x1 -> x2, Pallas kernels: 13.5 us -> 14 us  [the longest x1 13.1 us: local(): pl.pallas_call(first_step, out_shape=(vmem(2, 4, 7, tall, width_z), vmem(...]
  transfers between devices with their start and end apart: 28 -> 28, of which waited for: 10 -> 8; matrix products, arithmetic and copies ran while one was open for 8% -> 8% of each run, Pallas kernels for 17% -> 16%
where the time goes in v4:
time: 135 us
  starting transfers between devices  49.2 us (36%)
  Pallas kernels  39.5 us (29%)
  waiting for transfers between devices  21 us (16%)
  other arithmetic  10.8 us (8%)
  local copies, waits for them, and re-layouts  7.43 us (6%)
  between operations  6.86 us (5%)
    pallas_call x1, Pallas kernels, local(): pl.pallas_call(second_step, out_shape=(shape(2, 2, 4, width_y, width_z),...  15.3 us
    pallas_call x1, Pallas kernels, local(): pl.pallas_call(first_step, out_shape=(vmem(2, 4, 7, tall, width_z), vmem(...  13.1 us
    ppermute x1, waiting for transfers between devices, local(): l1_a = to_ahead(after(e1_a, l0_b))  6.49 us
    ppermute x1, starting transfers between devices, local(): l0_a = to_ahead(after(e0_a, s0_b))  6.33 us
    unnamed x40, local copies, waits for them, and re-layouts  5.6 us
    ppermute x1, starting transfers between devices, local(): l1_a = to_ahead(after(e1_a, l0_b))  5.02 us
    ppermute x1, starting transfers between devices, local(): l0_b = to_ahead(after(e0_b, l0_a, far_e, far_l, vfine))  4.57 us
    ppermute x3, starting transfers between devices, local(): came.append(lax.ppermute(row, 'space', pairs))  4.52 us
  transfers between devices with their start and end apart: 28, of which 8 were waited for; matrix products, arithmetic and copies ran while one was open for 8% of the time, Pallas kernels for 16%

profile of v4, /device:TPU:0, one launch (start us, length us, event | category | flops | bytes accessed | tf_op | source)
XLA Modules:
  0.0 134.8 jit_solution(7831951445184602986)
XLA Ops:
  1.3 2.6 %arrange.1 = (f32[2,4,264,128]{3,2,1,0:T(8,128)S(1)}, f32[2,4,264,128]{3,2,1,0:T(8,128)S(1)}, f32[1056,128]{1,0:T(8,128)S(1)}) custom-call(s32[3]{0:T(128)} %pad_add_fusion.scal, f32[1,2,4,512,128]{4,3,2,1,0:T(8,128)} %store.1, f32[4,512,128]{2,1,0:T(8,128)} %rate.1), custom_call_target="tpu_custom_call" | custom-call | bytes 6291456 | tf_op jit(solution)/shard_map/arrange/pallas_call | solution.py:499
  9.5 3.0 %collective-permute-start.5 = (f32[136,128]{1,0:T(8,128)S(1)}, f32[136,128]{1,0:T(8,128)S(1)}, u32[]{:S(2)}, u32[]{:S(2)}) collective-permute-start(f32[136,128]{1,0:T(8,128)S(1)} %window.1), channel_id=1, source_target_pairs={{0,1},{1,0},{2,3},{3,2},{4,5},{5,4},{6,7},{7,6},{8,9},{9,8},{10,11... | collective-permute-start | bytes 208904 | tf_op jit(solution)/shard_map/directions_pair/ppermute | solution.py:530
  15.3 2.4 %slice_select_fusion.2 = (f32[2,2,264,128]{3,2,1,0:T(8,128)}, f32[2,2,264,128]{3,2,1,0:T(8,128)}) fusion(f32[2,4,264,128]{3,2,1,0:T(8,128)} %collective-permute-done, f32[2,4,264,128]{3,2,1,0:T(8,128)S(1)} %copy-done.2, pred[]{:T(512)S(6)} %eq.48, pred[]{:T(512)S(6)} %eq.47), kind=kLoop, calls=%fused_computation.3 | loop fusion | flops 270336 | bytes 3244034 | tf_op jit(solution)/shard_map/jit(_where)/select_n | solution.py:514
  18.2 1.6 %collective-permute-start.6 = (f32[2,136,128]{2,1,0:T(8,128)S(1)}, f32[2,136,128]{2,1,0:T(8,128)S(1)}, u32[]{:S(2)}, u32[]{:S(2)}) collective-permute-start(f32[2,136,128]{2,1,0:T(8,128)S(1)} %pad_maximum_fusion.refs_0_), channel_id=1, source_target_pairs={{0,2},{1,3},{2,0},{3,1},{4,6},{5,7},{6,4},{7,5},{8,10},{9,11},{10,... | collective-permute-start | bytes 417800 | tf_op jit(solution)/shard_map/directions_space/ppermute | solution.py:534
  19.9 2.6 %collective-permute-start.7 = (f32[2,136,128]{2,1,0:T(8,128)S(1)}, f32[2,136,128]{2,1,0:T(8,128)S(1)}, u32[]{:S(2)}, u32[]{:S(2)}) collective-permute-start(f32[2,136,128]{2,1,0:T(8,128)S(1)} %pad_maximum_fusion.refs_0_), channel_id=1, source_target_pairs={{0,4},{1,5},{2,6},{3,7},{4,0},{5,1},{6,2},{7,3},{8,12},{9,13},{10,... | collective-permute-start | bytes 417800 | tf_op jit(solution)/shard_map/directions_space/ppermute | solution.py:534
  22.7 1.9 %slice_select_fusion.1 = f32[2,2,264,128]{3,2,1,0:T(8,128)} fusion(f32[2,4,264,128]{3,2,1,0:T(8,128)} %collective-permute-done, f32[2,4,264,128]{3,2,1,0:T(8,128)S(1)} %copy-done.2, pred[]{:T(512)S(6)} %eq.47), kind=kLoop, calls=%fused_computation.2 | loop fusion | flops 135168 | bytes 1622017 | tf_op jit(solution)/shard_map/jit(_where)/select_n | solution.py:514
  24.6 3.2 %collective-permute-done.3 = f32[2,2,264,128]{3,2,1,0:T(8,128)S(1)} collective-permute-done((f32[2,2,264,128]{3,2,1,0:T(8,128)S(1)}, f32[2,2,264,128]{3,2,1,0:T(8,128)S(1)}, u32[]{:S(2)}, u32[]{:S(2)}) %collective-permute-start.3) | collective-permute-done | bytes 540704 | tf_op jit(solution)/shard_map/slab0_column/ppermute | solution.py:538
  29.4 3.4 %collective-permute-done.7.refs_2_ = f32[2,136,128]{2,1,0:T(8,128)S(1)} collective-permute-done((f32[2,136,128]{2,1,0:T(8,128)S(1)}, f32[2,136,128]{2,1,0:T(8,128)S(1)}, u32[]{:S(2)}, u32[]{:S(2)}) %collective-permute-start.7) | collective-permute-done | bytes 139296 | tf_op jit(solution)/shard_map/directions_space/ppermute | solution.py:534
  35.1 4.0 %collective-permute-start.2 = (f32[1056,128]{1,0:T(8,128)S(1)}, f32[1056,128]{1,0:T(8,128)S(1)}, u32[]{:S(2)}, u32[]{:S(2)}) collective-permute-start(f32[1056,128]{1,0:T(8,128)S(1)} %collective-permute-done.1.rate_e), channel_id=1, source_target_pairs={{0,2},{2,4},{4,6},{3,1},{5,3},{7,5},{8,10},{10,12},{12,14},{11,9},... | collective-permute-start | bytes 1622024 | tf_op jit(solution)/shard_map/rate_ahead/ppermute | solution.py:541
  39.1 2.1 %collective-permute-done.11 = f32[2,2,264,128]{3,2,1,0:T(8,128)} collective-permute-done((f32[2,2,264,128]{3,2,1,0:T(8,128)}, f32[2,2,264,128]{3,2,1,0:T(8,128)}, u32[]{:S(2)}, u32[]{:S(2)}) %collective-permute-start.11) | collective-permute-done | bytes 540704 | tf_op jit(solution)/shard_map/slab0_column/ppermute | solution.py:539
  42.3 1.9 %collective-permute-done.9.e_a = f32[2,2,264,128]{3,2,1,0:T(8,128)S(1)} collective-permute-done((f32[2,2,264,128]{3,2,1,0:T(8,128)S(1)}, f32[2,2,264,128]{3,2,1,0:T(8,128)S(1)}, u32[]{:S(2)}, u32[]{:S(2)}) %collective-permute-start.9) | collective-permute-done | bytes 540704 | tf_op jit(solution)/shard_map/slab0_pair/ppermute | solution.py:544
  44.2 6.3 %collective-permute-start.16 = (f32[2,2,264,128]{3,2,1,0:T(8,128)S(1)}, f32[2,2,264,128]{3,2,1,0:T(8,128)}, u32[]{:S(2)}, u32[]{:S(2)}) collective-permute-start(f32[2,2,264,128]{3,2,1,0:T(8,128)S(1)} %collective-permute-done.9.e_a), channel_id=1, source_target_pairs={{0,2},{2,4},{4,6},{3,1},{5,3},{7,5},{8,10},{10,12},{12,14},{11,9},... | collective-permute-start | bytes 1622024 | tf_op jit(solution)/shard_map/slab0_ahead/ppermute | solution.py:572
  51.6 4.1 %collective-permute-start.14 = (f32[264,128]{1,0:T(8,128)}, f32[264,128]{1,0:T(8,128)}, u32[]{:S(2)}, u32[]{:S(2)}) collective-permute-start(f32[264,128]{1,0:T(8,128)} %get-tuple-element.45), channel_id=1, source_target_pairs={{0,2},{2,4},{4,6},{3,1},{5,3},{7,5},{8,10},{10,12},{12,14},{11,9},... | collective-permute-start | bytes 405512 | tf_op jit(solution)/shard_map/far_layers/ppermute | solution.py:550
  59.5 3.7 %expand.1.v = f32[4,8,264,128]{3,2,1,0:T(8,128)S(1)} custom-call(s32[3]{0:T(128)S(1)} %copy-done.8, s32[16]{0:T(128)S(1)} %pad_add_fusion.1.where, f32[2,136,128]{2,1,0:T(8,128)S(1)} %pad_maximum_fusion.refs_0_, f32[2,136,128]{2,1,0:T(8,128)S(1)} %collective-permute-done.6.refs_1_, f32[2,136,128]{2,1,0:T(8,128)S(1)} %copy-done.5, f32[2,136,128]{2,1,0:T(8,128)S(1)} %copy-done.7), custom_call_target="tpu_custom_call" | custom-call | bytes 26214400 | tf_op jit(solution)/shard_map/expand/pallas_call | solution.py:557
  64.4 4.6 %collective-permute-start.19 = (f32[2,2,264,128]{3,2,1,0:T(8,128)}, f32[2,2,264,128]{3,2,1,0:T(8,128)S(1)}, u32[]{:S(2)}, u32[]{:S(2)}) collective-permute-start(f32[2,2,264,128]{3,2,1,0:T(8,128)} %collective-permute-done.12.e_b), channel_id=1, source_target_pairs={{0,2},{2,4},{4,6},{3,1},{5,3},{7,5},{8,10},{10,12},{12,14},{11,9},... | collective-permute-start | bytes 1622024 | tf_op jit(solution)/shard_map/slab0_ahead/ppermute | solution.py:573
  70.7 13.1 %first_step.1 = (f32[2,4,7,280,128]{4,3,2,1,0:T(8,128)S(1)}, f32[4,2,280,128]{3,2,1,0:T(8,128)S(1)}, f32[2,4,2,280,128]{4,3,2,1,0:T(8,128)S(1)}, f32[2,2,264,128]{3,2,1,0:T(8,128)S(1)}) custom-call(s32[3]{0:T(128)S(1)} %copy-done.8, f32[1056,128]{1,0:T(8,128)S(1)} %get-tuple-element.34.rate_m, f32[1056,128]{1,0:T(8,128)S(1)} %collective-permute-done.1.rate_e, ...), custom_call_target="tpu_custom_call" | custom-call | bytes 41943040 | tf_op jit(solution)/shard_map/first_step/pallas_call | solution.py:580
  83.9 5.0 %collective-permute-start.20 = (f32[2,2,264,128]{3,2,1,0:T(8,128)S(1)}, f32[2,2,264,128]{3,2,1,0:T(8,128)S(1)}, u32[]{:S(2)}, u32[]{:S(2)}) collective-permute-start(f32[2,2,264,128]{3,2,1,0:T(8,128)S(1)} %collective-permute-done.18), channel_id=1, source_target_pairs={{0,2},{2,4},{4,6},{3,1},{5,3},{7,5},{8,10},{10,12},{12,14},{11,9},... | collective-permute-start | bytes 1622024 | tf_op jit(solution)/shard_map/slab1_ahead/ppermute | solution.py:578
  90.0 6.5 %collective-permute-done.20.l_a = f32[2,2,264,128]{3,2,1,0:T(8,128)S(1)} collective-permute-done((f32[2,2,264,128]{3,2,1,0:T(8,128)S(1)}, f32[2,2,264,128]{3,2,1,0:T(8,128)S(1)}, u32[]{:S(2)}, u32[]{:S(2)}) %collective-permute-start.20) | collective-permute-done | bytes 540704 | tf_op jit(solution)/shard_map/slab1_ahead/ppermute | solution.py:578
  96.5 2.3 %collective-permute-done.17.e_b = f32[2,2,264,128]{3,2,1,0:T(8,128)S(1)} collective-permute-done((f32[2,2,264,128]{3,2,1,0:T(8,128)S(1)}, f32[2,2,264,128]{3,2,1,0:T(8,128)S(1)}, u32[]{:S(2)}, u32[]{:S(2)}) %collective-permute-start.17) | collective-permute-done | bytes 540704 | tf_op jit(solution)/shard_map/slab1_pair/ppermute | solution.py:605
  99.6 15.3 %second_step.1 = (f32[2,2,4,512,128]{4,3,2,1,0:T(8,128)}, f32[2,2,4,256,128]{4,3,2,1,0:T(8,128)}, f32[2,2,16,128]{3,2,1,0:T(8,128)S(1)}, f32[2,2,16,128]{3,2,1,0:T(8,128)S(1)}) custom-call(s32[3]{0:T(128)S(1)} %copy-done.8, f32[1056,128]{1,0:T(8,128)S(1)} %get-tuple-element.34.rate_m, f32[1056,128]{1,0:T(8,128)} %copy-done.3, f32[1056,128]{1,0:T(8,128)} %copy-done, ...), custom_call_target="tpu_custom_call" | custom-call | bytes 57671680 | tf_op jit(solution)/shard_map/second_step/pallas_call | solution.py:628
  115.5 4.1 %collective-permute-start.23 = (f32[2,2,16,128]{3,2,1,0:T(8,128)S(1)}, f32[2,2,16,128]{3,2,1,0:T(8,128)S(1)}, u32[]{:S(2)}, u32[]{:S(2)}) collective-permute-start(f32[2,2,16,128]{3,2,1,0:T(8,128)S(1)} %get-tuple-element.59), channel_id=1, source_target_pairs={{0,1},{1,0},{2,3},{3,2},{4,5},{5,4},{6,7},{7,6},{8,9},{9,8},{10,11... | collective-permute-start | bytes 98312 | tf_op jit(solution)/shard_map/means_near/ppermute | solution.py:663
  123.3 1.6 %collective-permute-start.27 = (f32[2,2,32,128]{3,2,1,0:T(8,128)S(1)}, f32[2,2,32,128]{3,2,1,0:T(8,128)S(1)}, u32[]{:S(2)}, u32[]{:S(2)}) collective-permute-start(f32[2,2,32,128]{3,2,1,0:T(8,128)S(1)} %get-tuple-element.70), channel_id=1, source_target_pairs={{0,2},{1,3},{2,0},{3,1},{4,6},{5,7},{6,4},{7,5},{8,10},{9,11},{10,... | collective-permute-start | bytes 196616 | tf_op jit(solution)/shard_map/means_space/ppermute | solution.py:673
  125.5 2.3 %collective-permute-start.25 = (f32[2,2,32,128]{3,2,1,0:T(8,128)S(1)}, f32[2,2,32,128]{3,2,1,0:T(8,128)S(1)}, u32[]{:S(2)}, u32[]{:S(2)}) collective-permute-start(f32[2,2,32,128]{3,2,1,0:T(8,128)S(1)} %broadcast_select_fusion.6), channel_id=1, source_target_pairs={{0,6},{1,7},{2,4},{3,5},{4,2},{5,3},{6,0},{7,1},{8,14},{9,15},{10,... | collective-permute-start | bytes 196616 | tf_op jit(solution)/shard_map/means_space/ppermute | solution.py:673
  131.1 2.9 %finish.1 = f32[2,2,4,512,128]{4,3,2,1,0:T(8,128)} custom-call(s32[3]{0:T(128)} %pad_add_fusion.scal, f32[2,2,4,512,128]{4,3,2,1,0:T(8,128)} %get-tuple-element.57.held, f32[2,2,4,256,128]{4,3,2,1,0:T(8,128)} %copy-done.14), custom_call_target="tpu_custom_call", output_to_operand_aliasing={{}: (1, {})} | custom-call | bytes 8388608 | tf_op jit(solution)/shard_map/finish/pallas_call | solution.py:674
  (101 shorter events, 27.3 us)
Async XLA Ops:
  4.9 7.6 %collective-permute-start = (f32[2,4,264,128]{3,2,1,0:T(8,128)S(1)}, f32[2,4,264,128]{3,2,1,0:T(8,128)}, u32[]{:S(2)}, u32[]{:S(2)}) collective-permute-start(f32[2,4,264,128]{3,2,1,0:T(8,128)S(1)} %get-tuple-element.33), channel_id=1, source_target_pairs={{0,8},{8,0},{16,24},{24,16},{1,9},{9,1},{17,25},{25,17},{2,10},{10... | collective-permute-start | bytes 3244040 | tf_op jit(solution)/shard_map/store_core/ppermute | solution.py:509
  9.5 8.2 %collective-permute-start.5 = (f32[136,128]{1,0:T(8,128)S(1)}, f32[136,128]{1,0:T(8,128)S(1)}, u32[]{:S(2)}, u32[]{:S(2)}) collective-permute-start(f32[136,128]{1,0:T(8,128)S(1)} %window.1), channel_id=1, source_target_pairs={{0,1},{1,0},{2,3},{3,2},{4,5},{5,4},{6,7},{7,6},{8,9},{9,8},{10,11... | collective-permute-start | bytes 208904 | tf_op jit(solution)/shard_map/directions_pair/ppermute | solution.py:530
  13.8 14.0 %collective-permute-start.3 = (f32[2,2,264,128]{3,2,1,0:T(8,128)S(1)}, f32[2,2,264,128]{3,2,1,0:T(8,128)S(1)}, u32[]{:S(2)}, u32[]{:S(2)}) collective-permute-start(f32[2,2,264,128]{3,2,1,0:T(8,128)S(1)} %slice_select_fusion), channel_id=1, source_target_pairs={{0,16},{8,24},{16,0},{24,8},{1,17},{9,25},{17,1},{25,9},{2,18},{10... | collective-permute-start | bytes 1622024 | tf_op jit(solution)/shard_map/slab0_column/ppermute | solution.py:538
  17.7 15.1 %collective-permute-start.1 = (f32[1056,128]{1,0:T(8,128)S(1)}, f32[1056,128]{1,0:T(8,128)S(1)}, u32[]{:S(2)}, u32[]{:S(2)}) collective-permute-start(f32[1056,128]{1,0:T(8,128)S(1)} %get-tuple-element.34.rate_m), channel_id=1, source_target_pairs={{0,1},{1,0},{2,3},{3,2},{4,5},{5,4},{6,7},{7,6},{8,9},{9,8},{10,11... | collective-permute-start | bytes 1622024 | tf_op jit(solution)/shard_map/rate_pair/ppermute | solution.py:536
  18.2 11.2 %collective-permute-start.6 = (f32[2,136,128]{2,1,0:T(8,128)S(1)}, f32[2,136,128]{2,1,0:T(8,128)S(1)}, u32[]{:S(2)}, u32[]{:S(2)}) collective-permute-start(f32[2,136,128]{2,1,0:T(8,128)S(1)} %pad_maximum_fusion.refs_0_), channel_id=1, source_target_pairs={{0,2},{1,3},{2,0},{3,1},{4,6},{5,7},{6,4},{7,5},{8,10},{9,11},{10,... | collective-permute-start | bytes 417800 | tf_op jit(solution)/shard_map/directions_space/ppermute | solution.py:534
  19.9 12.9 %collective-permute-start.7 = (f32[2,136,128]{2,1,0:T(8,128)S(1)}, f32[2,136,128]{2,1,0:T(8,128)S(1)}, u32[]{:S(2)}, u32[]{:S(2)}) collective-permute-start(f32[2,136,128]{2,1,0:T(8,128)S(1)} %pad_maximum_fusion.refs_0_), channel_id=1, source_target_pairs={{0,4},{1,5},{2,6},{3,7},{4,0},{5,1},{6,2},{7,3},{8,12},{9,13},{10,... | collective-permute-start | bytes 417800 | tf_op jit(solution)/shard_map/directions_space/ppermute | solution.py:534
  22.5 10.3 %collective-permute-start.8 = (f32[2,136,128]{2,1,0:T(8,128)S(1)}, f32[2,136,128]{2,1,0:T(8,128)S(1)}, u32[]{:S(2)}, u32[]{:S(2)}) collective-permute-start(f32[2,136,128]{2,1,0:T(8,128)S(1)} %pad_maximum_fusion.refs_0_), channel_id=1, source_target_pairs={{0,6},{1,7},{2,4},{3,5},{4,2},{5,3},{6,0},{7,1},{8,14},{9,15},{10,... | collective-permute-start | bytes 417800 | tf_op jit(solution)/shard_map/directions_space/ppermute | solution.py:534
  27.8 13.4 %collective-permute-start.11 = (f32[2,2,264,128]{3,2,1,0:T(8,128)}, f32[2,2,264,128]{3,2,1,0:T(8,128)}, u32[]{:S(2)}, u32[]{:S(2)}) collective-permute-start(f32[2,2,264,128]{3,2,1,0:T(8,128)} %get-tuple-element.42), channel_id=1, source_target_pairs={{0,16},{8,24},{16,0},{24,8},{1,17},{9,25},{17,1},{25,9},{2,18},{10... | collective-permute-start | bytes 1622024 | tf_op jit(solution)/shard_map/slab0_column/ppermute | solution.py:539
  32.8 11.3 %collective-permute-start.9 = (f32[2,2,264,128]{3,2,1,0:T(8,128)S(1)}, f32[2,2,264,128]{3,2,1,0:T(8,128)S(1)}, u32[]{:S(2)}, u32[]{:S(2)}) collective-permute-start(f32[2,2,264,128]{3,2,1,0:T(8,128)S(1)} %broadcast_select_fusion.1.s_a), channel_id=1, source_target_pairs={{0,1},{1,0},{2,3},{3,2},{4,5},{5,4},{6,7},{7,6},{8,9},{9,8},{10,11... | collective-permute-start | bytes 1622024 | tf_op jit(solution)/shard_map/slab0_pair/ppermute | solution.py:544
  35.1 16.5 %collective-permute-start.2 = (f32[1056,128]{1,0:T(8,128)S(1)}, f32[1056,128]{1,0:T(8,128)S(1)}, u32[]{:S(2)}, u32[]{:S(2)}) collective-permute-start(f32[1056,128]{1,0:T(8,128)S(1)} %collective-permute-done.1.rate_e), channel_id=1, source_target_pairs={{0,2},{2,4},{4,6},{3,1},{5,3},{7,5},{8,10},{10,12},{12,14},{11,9},... | collective-permute-start | bytes 1622024 | tf_op jit(solution)/shard_map/rate_ahead/ppermute | solution.py:541
  44.2 19.6 %collective-permute-start.16 = (f32[2,2,264,128]{3,2,1,0:T(8,128)S(1)}, f32[2,2,264,128]{3,2,1,0:T(8,128)}, u32[]{:S(2)}, u32[]{:S(2)}) collective-permute-start(f32[2,2,264,128]{3,2,1,0:T(8,128)S(1)} %collective-permute-done.9.e_a), channel_id=1, source_target_pairs={{0,2},{2,4},{4,6},{3,1},{5,3},{7,5},{8,10},{10,12},{12,14},{11,9},... | collective-permute-start | bytes 1622024 | tf_op jit(solution)/shard_map/slab0_ahead/ppermute | solution.py:572
  50.5 13.2 %collective-permute-start.12 = (f32[2,2,264,128]{3,2,1,0:T(8,128)S(1)}, f32[2,2,264,128]{3,2,1,0:T(8,128)}, u32[]{:S(2)}, u32[]{:S(2)}) collective-permute-start(f32[2,2,264,128]{3,2,1,0:T(8,128)S(1)} %broadcast_select_fusion.s_b), channel_id=1, source_target_pairs={{0,1},{1,0},{2,3},{3,2},{4,5},{5,4},{6,7},{7,6},{8,9},{9,8},{10,11... | collective-permute-start | bytes 1622024 | tf_op jit(solution)/shard_map/slab0_pair/ppermute | solution.py:568
  50.5 18.5 %collective-permute-start.10 = (f32[2,2,264,128]{3,2,1,0:T(8,128)}, f32[2,2,264,128]{3,2,1,0:T(8,128)}, u32[]{:S(2)}, u32[]{:S(2)}) collective-permute-start(f32[2,2,264,128]{3,2,1,0:T(8,128)} %get-tuple-element.40), channel_id=1, source_target_pairs={{0,16},{8,24},{16,0},{24,8},{1,17},{9,25},{17,1},{25,9},{2,18},{10... | collective-permute-start | bytes 1622024 | tf_op jit(solution)/shard_map/slab1_column/ppermute | solution.py:552
  51.6 12.1 %collective-permute-start.14 = (f32[264,128]{1,0:T(8,128)}, f32[264,128]{1,0:T(8,128)}, u32[]{:S(2)}, u32[]{:S(2)}) collective-permute-start(f32[264,128]{1,0:T(8,128)} %get-tuple-element.45), channel_id=1, source_target_pairs={{0,2},{2,4},{4,6},{3,1},{5,3},{7,5},{8,10},{10,12},{12,14},{11,9},... | collective-permute-start | bytes 405512 | tf_op jit(solution)/shard_map/far_layers/ppermute | solution.py:550
  55.7 8.0 %collective-permute-start.13 = (f32[264,128]{1,0:T(8,128)}, f32[264,128]{1,0:T(8,128)}, u32[]{:S(2)}, u32[]{:S(2)}) collective-permute-start(f32[264,128]{1,0:T(8,128)} %get-tuple-element.44), channel_id=1, source_target_pairs={{2,0},{4,2},{6,4},{1,3},{3,5},{5,7},{10,8},{12,10},{14,12},{9,11},... | collective-permute-start | bytes 405512 | tf_op jit(solution)/shard_map/far_layers/ppermute | solution.py:549
  63.8 20.1 %collective-permute-start.15 = (f32[2,2,264,128]{3,2,1,0:T(8,128)S(1)}, f32[2,2,264,128]{3,2,1,0:T(8,128)S(1)}, u32[]{:S(2)}, u32[]{:S(2)}) collective-permute-start(f32[2,2,264,128]{3,2,1,0:T(8,128)S(1)} %copy-done.12), channel_id=1, source_target_pairs={{0,16},{8,24},{16,0},{24,8},{1,17},{9,25},{17,1},{25,9},{2,18},{10... | collective-permute-start | bytes 1622024 | tf_op jit(solution)/shard_map/slab1_column/ppermute | solution.py:570
  64.4 19.5 %collective-permute-start.19 = (f32[2,2,264,128]{3,2,1,0:T(8,128)}, f32[2,2,264,128]{3,2,1,0:T(8,128)S(1)}, u32[]{:S(2)}, u32[]{:S(2)}) collective-permute-start(f32[2,2,264,128]{3,2,1,0:T(8,128)} %collective-permute-done.12.e_b), channel_id=1, source_target_pairs={{0,2},{2,4},{4,6},{3,1},{5,3},{7,5},{8,10},{10,12},{12,14},{11,9},... | collective-permute-start | bytes 1622024 | tf_op jit(solution)/shard_map/slab0_ahead/ppermute | solution.py:573
  70.2 13.7 %collective-permute-start.18 = (f32[2,2,264,128]{3,2,1,0:T(8,128)S(1)}, f32[2,2,264,128]{3,2,1,0:T(8,128)S(1)}, u32[]{:S(2)}, u32[]{:S(2)}) collective-permute-start(f32[2,2,264,128]{3,2,1,0:T(8,128)S(1)} %broadcast_select_fusion.3.s_a), channel_id=1, source_target_pairs={{0,1},{1,0},{2,3},{3,2},{4,5},{5,4},{6,7},{7,6},{8,9},{9,8},{10,11... | collective-permute-start | bytes 1622024 | tf_op jit(solution)/shard_map/slab1_pair/ppermute | solution.py:576
  83.9 12.6 %collective-permute-start.20 = (f32[2,2,264,128]{3,2,1,0:T(8,128)S(1)}, f32[2,2,264,128]{3,2,1,0:T(8,128)S(1)}, u32[]{:S(2)}, u32[]{:S(2)}) collective-permute-start(f32[2,2,264,128]{3,2,1,0:T(8,128)S(1)} %collective-permute-done.18), channel_id=1, source_target_pairs={{0,2},{2,4},{4,6},{3,1},{5,3},{7,5},{8,10},{10,12},{12,14},{11,9},... | collective-permute-start | bytes 1622024 | tf_op jit(solution)/shard_map/slab1_ahead/ppermute | solution.py:578
  88.9 9.9 %collective-permute-start.17 = (f32[2,2,264,128]{3,2,1,0:T(8,128)S(1)}, f32[2,2,264,128]{3,2,1,0:T(8,128)S(1)}, u32[]{:S(2)}, u32[]{:S(2)}) collective-permute-start(f32[2,2,264,128]{3,2,1,0:T(8,128)S(1)} %broadcast_select_fusion.2.s_b), channel_id=1, source_target_pairs={{0,1},{1,0},{2,3},{3,2},{4,5},{5,4},{6,7},{7,6},{8,9},{9,8},{10,11... | collective-permute-start | bytes 1622024 | tf_op jit(solution)/shard_map/slab1_pair/ppermute | solution.py:605
  115.0 14.8 %collective-permute-start.21 = (f32[2,2,4,256,128]{4,3,2,1,0:T(8,128)}, f32[2,2,4,256,128]{4,3,2,1,0:T(8,128)S(1)}, u32[]{:S(2)}, u32[]{:S(2)}) collective-permute-start(f32[2,2,4,256,128]{4,3,2,1,0:T(8,128)} %get-tuple-element.58), channel_id=1, source_target_pairs={{0,8},{8,0},{16,24},{24,16},{1,9},{9,1},{17,25},{25,17},{2,10},{10... | collective-permute-start | bytes 6291464 | tf_op jit(solution)/shard_map/tangent_core/ppermute | solution.py:665
  123.3 10.8 %collective-permute-start.27 = (f32[2,2,32,128]{3,2,1,0:T(8,128)S(1)}, f32[2,2,32,128]{3,2,1,0:T(8,128)S(1)}, u32[]{:S(2)}, u32[]{:S(2)}) collective-permute-start(f32[2,2,32,128]{3,2,1,0:T(8,128)S(1)} %get-tuple-element.70), channel_id=1, source_target_pairs={{0,2},{1,3},{2,0},{3,1},{4,6},{5,7},{6,4},{7,5},{8,10},{9,11},{10,... | collective-permute-start | bytes 196616 | tf_op jit(solution)/shard_map/means_space/ppermute | solution.py:673
  124.9 9.2 %collective-permute-start.26 = (f32[2,2,32,128]{3,2,1,0:T(8,128)S(1)}, f32[2,2,32,128]{3,2,1,0:T(8,128)S(1)}, u32[]{:S(2)}, u32[]{:S(2)}) collective-permute-start(f32[2,2,32,128]{3,2,1,0:T(8,128)S(1)} %get-tuple-element.71), channel_id=1, source_target_pairs={{0,4},{1,5},{2,6},{3,7},{4,0},{5,1},{6,2},{7,3},{8,12},{9,13},{10,... | collective-permute-start | bytes 196616 | tf_op jit(solution)/shard_map/means_space/ppermute | solution.py:673
  125.5 8.6 %collective-permute-start.25 = (f32[2,2,32,128]{3,2,1,0:T(8,128)S(1)}, f32[2,2,32,128]{3,2,1,0:T(8,128)S(1)}, u32[]{:S(2)}, u32[]{:S(2)}) collective-permute-start(f32[2,2,32,128]{3,2,1,0:T(8,128)S(1)} %broadcast_select_fusion.6), channel_id=1, source_target_pairs={{0,6},{1,7},{2,4},{3,5},{4,2},{5,3},{6,0},{7,1},{8,14},{9,15},{10,... | collective-permute-start | bytes 196616 | tf_op jit(solution)/shard_map/means_space/ppermute | solution.py:673
  (24 other events, 200.3 us)

commit v5 on v4

--- a/solution.py
+++ b/solution.py
@@ -667,7 +667,7 @@
     sens = jnp.where(source == mine, here, there)
     came = []
     for j in range(2, n_space, 2):
-        row = jnp.where(block_map[mine] == mine ^ j, here, there)
+        row = after(jnp.where(block_map[mine] == mine ^ j, here, there), rest)
         pairs = [(i, i ^ j) for i in range(n_space)]
         with jax.named_scope("means_space"):
             came.append(lax.ppermute(row, "space", pairs))

time: 135 us -> 134 us (level)
  transfers between devices with their start and end apart: 28 -> 28, of which waited for: 8 -> 9; matrix products, arithmetic and copies ran while one was open for 8% -> 8% of each run, Pallas kernels for 16% -> 16%
where the time goes in v5:
time: 134 us; the launch traced here: 133 us
  starting transfers between devices  49.1 us (37%)
  Pallas kernels  39.5 us (29%)
  waiting for transfers between devices  21.3 us (16%)
  other arithmetic  9.76 us (7%)
  between operations  6.86 us (5%)
  local copies, waits for them, and re-layouts  6.11 us (5%)
    pallas_call x1, Pallas kernels, local(): pl.pallas_call(second_step, out_shape=(shape(2, 2, 4, width_y, width_z),...  15.3 us
    pallas_call x1, Pallas kernels, local(): pl.pallas_call(first_step, out_shape=(vmem(2, 4, 7, tall, width_z), vmem(...  13.1 us
    ppermute x1, waiting for transfers between devices, local(): l1_a = to_ahead(after(e1_a, l0_b))  6.48 us
    ppermute x1, starting transfers between devices, local(): l0_a = to_ahead(after(e0_a, s0_b))  6.33 us
    ppermute x1, starting transfers between devices, local(): l1_a = to_ahead(after(e1_a, l0_b))  5.02 us
    ppermute x1, starting transfers between devices, local(): l0_b = to_ahead(after(e0_b, l0_a, far_e, far_l, vfine))  4.57 us
    ppermute x3, starting transfers between devices, local(): lax.ppermute(after(pair), 'space', [(i, i ^ j) for i in range(n_space)])  4.45 us
    ppermute x3, starting transfers between devices, local(): came.append(lax.ppermute(row, 'space', pairs))  4.45 us
  transfers between devices with their start and end apart: 28, of which 9 were waited for; matrix products, arithmetic and copies ran while one was open for 8% of the time, Pallas kernels for 16%

profile of v5, /device:TPU:0, one launch (start us, length us, event | category | flops | bytes accessed | tf_op | source)
XLA Modules:
  0.0 132.6 jit_solution(4991475897113462585)
XLA Ops:
  1.3 2.6 %arrange.1 = (f32[2,4,264,128]{3,2,1,0:T(8,128)S(1)}, f32[2,4,264,128]{3,2,1,0:T(8,128)S(1)}, f32[1056,128]{1,0:T(8,128)S(1)}) custom-call(s32[3]{0:T(128)} %pad_add_fusion.scal, f32[1,2,4,512,128]{4,3,2,1,0:T(8,128)} %store.1, f32[4,512,128]{2,1,0:T(8,128)} %rate.1), custom_call_target="tpu_custom_call" | custom-call | bytes 6291456 | tf_op jit(solution)/shard_map/arrange/pallas_call | solution.py:499
  9.5 3.0 %collective-permute-start.5 = (f32[136,128]{1,0:T(8,128)S(1)}, f32[136,128]{1,0:T(8,128)S(1)}, u32[]{:S(2)}, u32[]{:S(2)}) collective-permute-start(f32[136,128]{1,0:T(8,128)S(1)} %window.1), channel_id=1, source_target_pairs={{0,1},{1,0},{2,3},{3,2},{4,5},{5,4},{6,7},{7,6},{8,9},{9,8},{10,11... | collective-permute-start | bytes 208904 | tf_op jit(solution)/shard_map/directions_pair/ppermute | solution.py:530
  15.3 2.4 %slice_select_fusion.2 = (f32[2,2,264,128]{3,2,1,0:T(8,128)}, f32[2,2,264,128]{3,2,1,0:T(8,128)}) fusion(f32[2,4,264,128]{3,2,1,0:T(8,128)} %collective-permute-done, f32[2,4,264,128]{3,2,1,0:T(8,128)S(1)} %copy-done.2, pred[]{:T(512)S(6)} %eq.48, pred[]{:T(512)S(6)} %eq.47), kind=kLoop, calls=%fused_computation.3 | loop fusion | flops 270336 | bytes 3244034 | tf_op jit(solution)/shard_map/jit(_where)/select_n | solution.py:514
  18.2 1.6 %collective-permute-start.6 = (f32[2,136,128]{2,1,0:T(8,128)S(1)}, f32[2,136,128]{2,1,0:T(8,128)S(1)}, u32[]{:S(2)}, u32[]{:S(2)}) collective-permute-start(f32[2,136,128]{2,1,0:T(8,128)S(1)} %pad_maximum_fusion.refs_0_), channel_id=1, source_target_pairs={{0,2},{1,3},{2,0},{3,1},{4,6},{5,7},{6,4},{7,5},{8,10},{9,11},{10,... | collective-permute-start | bytes 417800 | tf_op jit(solution)/shard_map/directions_space/ppermute | solution.py:534
  19.9 2.6 %collective-permute-start.7 = (f32[2,136,128]{2,1,0:T(8,128)S(1)}, f32[2,136,128]{2,1,0:T(8,128)S(1)}, u32[]{:S(2)}, u32[]{:S(2)}) collective-permute-start(f32[2,136,128]{2,1,0:T(8,128)S(1)} %pad_maximum_fusion.refs_0_), channel_id=1, source_target_pairs={{0,4},{1,5},{2,6},{3,7},{4,0},{5,1},{6,2},{7,3},{8,12},{9,13},{10,... | collective-permute-start | bytes 417800 | tf_op jit(solution)/shard_map/directions_space/ppermute | solution.py:534
  22.7 1.9 %slice_select_fusion.1 = f32[2,2,264,128]{3,2,1,0:T(8,128)} fusion(f32[2,4,264,128]{3,2,1,0:T(8,128)} %collective-permute-done, f32[2,4,264,128]{3,2,1,0:T(8,128)S(1)} %copy-done.2, pred[]{:T(512)S(6)} %eq.47), kind=kLoop, calls=%fused_computation.2 | loop fusion | flops 135168 | bytes 1622017 | tf_op jit(solution)/shard_map/jit(_where)/select_n | solution.py:514
  24.6 3.2 %collective-permute-done.3 = f32[2,2,264,128]{3,2,1,0:T(8,128)S(1)} collective-permute-done((f32[2,2,264,128]{3,2,1,0:T(8,128)S(1)}, f32[2,2,264,128]{3,2,1,0:T(8,128)S(1)}, u32[]{:S(2)}, u32[]{:S(2)}) %collective-permute-start.3) | collective-permute-done | bytes 540704 | tf_op jit(solution)/shard_map/slab0_column/ppermute | solution.py:538
  29.4 3.4 %collective-permute-done.7.refs_2_ = f32[2,136,128]{2,1,0:T(8,128)S(1)} collective-permute-done((f32[2,136,128]{2,1,0:T(8,128)S(1)}, f32[2,136,128]{2,1,0:T(8,128)S(1)}, u32[]{:S(2)}, u32[]{:S(2)}) %collective-permute-start.7) | collective-permute-done | bytes 139296 | tf_op jit(solution)/shard_map/directions_space/ppermute | solution.py:534
  35.1 4.0 %collective-permute-start.2 = (f32[1056,128]{1,0:T(8,128)S(1)}, f32[1056,128]{1,0:T(8,128)S(1)}, u32[]{:S(2)}, u32[]{:S(2)}) collective-permute-start(f32[1056,128]{1,0:T(8,128)S(1)} %collective-permute-done.1.rate_e), channel_id=1, source_target_pairs={{0,2},{2,4},{4,6},{3,1},{5,3},{7,5},{8,10},{10,12},{12,14},{11,9},... | collective-permute-start | bytes 1622024 | tf_op jit(solution)/shard_map/rate_ahead/ppermute | solution.py:541
  39.1 2.1 %collective-permute-done.11 = f32[2,2,264,128]{3,2,1,0:T(8,128)} collective-permute-done((f32[2,2,264,128]{3,2,1,0:T(8,128)}, f32[2,2,264,128]{3,2,1,0:T(8,128)}, u32[]{:S(2)}, u32[]{:S(2)}) %collective-permute-start.11) | collective-permute-done | bytes 540704 | tf_op jit(solution)/shard_map/slab0_column/ppermute | solution.py:539
  42.3 1.9 %collective-permute-done.9.e_a = f32[2,2,264,128]{3,2,1,0:T(8,128)S(1)} collective-permute-done((f32[2,2,264,128]{3,2,1,0:T(8,128)S(1)}, f32[2,2,264,128]{3,2,1,0:T(8,128)S(1)}, u32[]{:S(2)}, u32[]{:S(2)}) %collective-permute-start.9) | collective-permute-done | bytes 540704 | tf_op jit(solution)/shard_map/slab0_pair/ppermute | solution.py:544
  44.2 6.3 %collective-permute-start.16 = (f32[2,2,264,128]{3,2,1,0:T(8,128)S(1)}, f32[2,2,264,128]{3,2,1,0:T(8,128)}, u32[]{:S(2)}, u32[]{:S(2)}) collective-permute-start(f32[2,2,264,128]{3,2,1,0:T(8,128)S(1)} %collective-permute-done.9.e_a), channel_id=1, source_target_pairs={{0,2},{2,4},{4,6},{3,1},{5,3},{7,5},{8,10},{10,12},{12,14},{11,9},... | collective-permute-start | bytes 1622024 | tf_op jit(solution)/shard_map/slab0_ahead/ppermute | solution.py:572
  51.6 4.1 %collective-permute-start.14 = (f32[264,128]{1,0:T(8,128)}, f32[264,128]{1,0:T(8,128)}, u32[]{:S(2)}, u32[]{:S(2)}) collective-permute-start(f32[264,128]{1,0:T(8,128)} %get-tuple-element.48), channel_id=1, source_target_pairs={{0,2},{2,4},{4,6},{3,1},{5,3},{7,5},{8,10},{10,12},{12,14},{11,9},... | collective-permute-start | bytes 405512 | tf_op jit(solution)/shard_map/far_layers/ppermute | solution.py:550
  59.5 3.7 %expand.1.v = f32[4,8,264,128]{3,2,1,0:T(8,128)S(1)} custom-call(s32[3]{0:T(128)S(1)} %copy-done.8, s32[16]{0:T(128)S(1)} %pad_add_fusion.1.where, f32[2,136,128]{2,1,0:T(8,128)S(1)} %pad_maximum_fusion.refs_0_, f32[2,136,128]{2,1,0:T(8,128)S(1)} %collective-permute-done.6.refs_1_, f32[2,136,128]{2,1,0:T(8,128)S(1)} %copy-done.5, f32[2,136,128]{2,1,0:T(8,128)S(1)} %copy-done.7), custom_call_target="tpu_custom_call" | custom-call | bytes 26214400 | tf_op jit(solution)/shard_map/expand/pallas_call | solution.py:557
  64.4 4.6 %collective-permute-start.19 = (f32[2,2,264,128]{3,2,1,0:T(8,128)}, f32[2,2,264,128]{3,2,1,0:T(8,128)S(1)}, u32[]{:S(2)}, u32[]{:S(2)}) collective-permute-start(f32[2,2,264,128]{3,2,1,0:T(8,128)} %collective-permute-done.12.e_b), channel_id=1, source_target_pairs={{0,2},{2,4},{4,6},{3,1},{5,3},{7,5},{8,10},{10,12},{12,14},{11,9},... | collective-permute-start | bytes 1622024 | tf_op jit(solution)/shard_map/slab0_ahead/ppermute | solution.py:573
  69.6 13.1 %first_step.1 = (f32[2,4,7,280,128]{4,3,2,1,0:T(8,128)S(1)}, f32[4,2,280,128]{3,2,1,0:T(8,128)S(1)}, f32[2,4,2,280,128]{4,3,2,1,0:T(8,128)S(1)}, f32[2,2,264,128]{3,2,1,0:T(8,128)S(1)}) custom-call(s32[3]{0:T(128)S(1)} %copy-done.8, f32[1056,128]{1,0:T(8,128)S(1)} %get-tuple-element.37.rate_m, f32[1056,128]{1,0:T(8,128)S(1)} %collective-permute-done.1.rate_e, ...), custom_call_target="tpu_custom_call" | custom-call | bytes 41943040 | tf_op jit(solution)/shard_map/first_step/pallas_call | solution.py:580
  82.9 5.0 %collective-permute-start.20 = (f32[2,2,264,128]{3,2,1,0:T(8,128)S(1)}, f32[2,2,264,128]{3,2,1,0:T(8,128)S(1)}, u32[]{:S(2)}, u32[]{:S(2)}) collective-permute-start(f32[2,2,264,128]{3,2,1,0:T(8,128)S(1)} %collective-permute-done.18), channel_id=1, source_target_pairs={{0,2},{2,4},{4,6},{3,1},{5,3},{7,5},{8,10},{10,12},{12,14},{11,9},... | collective-permute-start | bytes 1622024 | tf_op jit(solution)/shard_map/slab1_ahead/ppermute | solution.py:578
  89.0 6.5 %collective-permute-done.20.l_a = f32[2,2,264,128]{3,2,1,0:T(8,128)S(1)} collective-permute-done((f32[2,2,264,128]{3,2,1,0:T(8,128)S(1)}, f32[2,2,264,128]{3,2,1,0:T(8,128)S(1)}, u32[]{:S(2)}, u32[]{:S(2)}) %collective-permute-start.20) | collective-permute-done | bytes 540704 | tf_op jit(solution)/shard_map/slab1_ahead/ppermute | solution.py:578
  95.4 2.3 %collective-permute-done.17.e_b = f32[2,2,264,128]{3,2,1,0:T(8,128)S(1)} collective-permute-done((f32[2,2,264,128]{3,2,1,0:T(8,128)S(1)}, f32[2,2,264,128]{3,2,1,0:T(8,128)S(1)}, u32[]{:S(2)}, u32[]{:S(2)}) %collective-permute-start.17) | collective-permute-done | bytes 540704 | tf_op jit(solution)/shard_map/slab1_pair/ppermute | solution.py:605
  98.6 15.3 %second_step.1 = (f32[2,2,4,512,128]{4,3,2,1,0:T(8,128)}, f32[2,2,4,256,128]{4,3,2,1,0:T(8,128)}, f32[2,2,16,128]{3,2,1,0:T(8,128)S(1)}, f32[2,2,16,128]{3,2,1,0:T(8,128)S(1)}) custom-call(s32[3]{0:T(128)S(1)} %copy-done.8, f32[1056,128]{1,0:T(8,128)S(1)} %get-tuple-element.37.rate_m, f32[1056,128]{1,0:T(8,128)} %copy-done.3, f32[1056,128]{1,0:T(8,128)} %copy-done, ...), custom_call_target="tpu_custom_call" | custom-call | bytes 57671680 | tf_op jit(solution)/shard_map/second_step/pallas_call | solution.py:628
  114.5 4.1 %collective-permute-start.23 = (f32[2,2,16,128]{3,2,1,0:T(8,128)S(1)}, f32[2,2,16,128]{3,2,1,0:T(8,128)S(1)}, u32[]{:S(2)}, u32[]{:S(2)}) collective-permute-start(f32[2,2,16,128]{3,2,1,0:T(8,128)S(1)} %get-tuple-element.62), channel_id=1, source_target_pairs={{0,1},{1,0},{2,3},{3,2},{4,5},{5,4},{6,7},{7,6},{8,9},{9,8},{10,11... | collective-permute-start | bytes 98312 | tf_op jit(solution)/shard_map/means_near/ppermute | solution.py:663
  122.3 1.6 %collective-permute-start.27 = (f32[2,2,32,128]{3,2,1,0:T(8,128)S(1)}, f32[2,2,32,128]{3,2,1,0:T(8,128)S(1)}, u32[]{:S(2)}, u32[]{:S(2)}) collective-permute-start(f32[2,2,32,128]{3,2,1,0:T(8,128)S(1)} %get-tuple-element.66), channel_id=1, source_target_pairs={{0,2},{1,3},{2,0},{3,1},{4,6},{5,7},{6,4},{7,5},{8,10},{9,11},{10,... | collective-permute-start | bytes 196616 | tf_op jit(solution)/shard_map/means_space/ppermute | solution.py:673
  124.5 2.3 %collective-permute-start.25 = (f32[2,2,32,128]{3,2,1,0:T(8,128)S(1)}, f32[2,2,32,128]{3,2,1,0:T(8,128)S(1)}, u32[]{:S(2)}, u32[]{:S(2)}) collective-permute-start(f32[2,2,32,128]{3,2,1,0:T(8,128)S(1)} %broadcast_select_fusion.6), channel_id=1, source_target_pairs={{0,6},{1,7},{2,4},{3,5},{4,2},{5,3},{6,0},{7,1},{8,14},{9,15},{10,... | collective-permute-start | bytes 196616 | tf_op jit(solution)/shard_map/means_space/ppermute | solution.py:673
  128.7 3.0 %finish.1 = f32[2,2,4,512,128]{4,3,2,1,0:T(8,128)} custom-call(s32[3]{0:T(128)} %pad_add_fusion.scal, f32[2,2,4,512,128]{4,3,2,1,0:T(8,128)} %get-tuple-element.60.held, f32[2,2,4,256,128]{4,3,2,1,0:T(8,128)} %copy-done.14), custom_call_target="tpu_custom_call", output_to_operand_aliasing={{}: (1, {})} | custom-call | bytes 8388608 | tf_op jit(solution)/shard_map/finish/pallas_call | solution.py:674
  (101 shorter events, 25.2 us)
Async XLA Ops:
  4.9 7.6 %collective-permute-start = (f32[2,4,264,128]{3,2,1,0:T(8,128)S(1)}, f32[2,4,264,128]{3,2,1,0:T(8,128)}, u32[]{:S(2)}, u32[]{:S(2)}) collective-permute-start(f32[2,4,264,128]{3,2,1,0:T(8,128)S(1)} %get-tuple-element.36), channel_id=1, source_target_pairs={{0,8},{8,0},{16,24},{24,16},{1,9},{9,1},{17,25},{25,17},{2,10},{10... | collective-permute-start | bytes 3244040 | tf_op jit(solution)/shard_map/store_core/ppermute | solution.py:509
  9.5 8.2 %collective-permute-start.5 = (f32[136,128]{1,0:T(8,128)S(1)}, f32[136,128]{1,0:T(8,128)S(1)}, u32[]{:S(2)}, u32[]{:S(2)}) collective-permute-start(f32[136,128]{1,0:T(8,128)S(1)} %window.1), channel_id=1, source_target_pairs={{0,1},{1,0},{2,3},{3,2},{4,5},{5,4},{6,7},{7,6},{8,9},{9,8},{10,11... | collective-permute-start | bytes 208904 | tf_op jit(solution)/shard_map/directions_pair/ppermute | solution.py:530
  13.8 14.0 %collective-permute-start.3 = (f32[2,2,264,128]{3,2,1,0:T(8,128)S(1)}, f32[2,2,264,128]{3,2,1,0:T(8,128)S(1)}, u32[]{:S(2)}, u32[]{:S(2)}) collective-permute-start(f32[2,2,264,128]{3,2,1,0:T(8,128)S(1)} %slice_select_fusion), channel_id=1, source_target_pairs={{0,16},{8,24},{16,0},{24,8},{1,17},{9,25},{17,1},{25,9},{2,18},{10... | collective-permute-start | bytes 1622024 | tf_op jit(solution)/shard_map/slab0_column/ppermute | solution.py:538
  17.7 15.1 %collective-permute-start.1 = (f32[1056,128]{1,0:T(8,128)S(1)}, f32[1056,128]{1,0:T(8,128)S(1)}, u32[]{:S(2)}, u32[]{:S(2)}) collective-permute-start(f32[1056,128]{1,0:T(8,128)S(1)} %get-tuple-element.37.rate_m), channel_id=1, source_target_pairs={{0,1},{1,0},{2,3},{3,2},{4,5},{5,4},{6,7},{7,6},{8,9},{9,8},{10,11... | collective-permute-start | bytes 1622024 | tf_op jit(solution)/shard_map/rate_pair/ppermute | solution.py:536
  18.2 11.2 %collective-permute-start.6 = (f32[2,136,128]{2,1,0:T(8,128)S(1)}, f32[2,136,128]{2,1,0:T(8,128)S(1)}, u32[]{:S(2)}, u32[]{:S(2)}) collective-permute-start(f32[2,136,128]{2,1,0:T(8,128)S(1)} %pad_maximum_fusion.refs_0_), channel_id=1, source_target_pairs={{0,2},{1,3},{2,0},{3,1},{4,6},{5,7},{6,4},{7,5},{8,10},{9,11},{10,... | collective-permute-start | bytes 417800 | tf_op jit(solution)/shard_map/directions_space/ppermute | solution.py:534
  19.9 12.9 %collective-permute-start.7 = (f32[2,136,128]{2,1,0:T(8,128)S(1)}, f32[2,136,128]{2,1,0:T(8,128)S(1)}, u32[]{:S(2)}, u32[]{:S(2)}) collective-permute-start(f32[2,136,128]{2,1,0:T(8,128)S(1)} %pad_maximum_fusion.refs_0_), channel_id=1, source_target_pairs={{0,4},{1,5},{2,6},{3,7},{4,0},{5,1},{6,2},{7,3},{8,12},{9,13},{10,... | collective-permute-start | bytes 417800 | tf_op jit(solution)/shard_map/directions_space/ppermute | solution.py:534
  22.5 10.3 %collective-permute-start.8 = (f32[2,136,128]{2,1,0:T(8,128)S(1)}, f32[2,136,128]{2,1,0:T(8,128)S(1)}, u32[]{:S(2)}, u32[]{:S(2)}) collective-permute-start(f32[2,136,128]{2,1,0:T(8,128)S(1)} %pad_maximum_fusion.refs_0_), channel_id=1, source_target_pairs={{0,6},{1,7},{2,4},{3,5},{4,2},{5,3},{6,0},{7,1},{8,14},{9,15},{10,... | collective-permute-start | bytes 417800 | tf_op jit(solution)/shard_map/directions_space/ppermute | solution.py:534
  27.8 13.4 %collective-permute-start.11 = (f32[2,2,264,128]{3,2,1,0:T(8,128)}, f32[2,2,264,128]{3,2,1,0:T(8,128)}, u32[]{:S(2)}, u32[]{:S(2)}) collective-permute-start(f32[2,2,264,128]{3,2,1,0:T(8,128)} %get-tuple-element.45), channel_id=1, source_target_pairs={{0,16},{8,24},{16,0},{24,8},{1,17},{9,25},{17,1},{25,9},{2,18},{10... | collective-permute-start | bytes 1622024 | tf_op jit(solution)/shard_map/slab0_column/ppermute | solution.py:539
  32.8 11.3 %collective-permute-start.9 = (f32[2,2,264,128]{3,2,1,0:T(8,128)S(1)}, f32[2,2,264,128]{3,2,1,0:T(8,128)S(1)}, u32[]{:S(2)}, u32[]{:S(2)}) collective-permute-start(f32[2,2,264,128]{3,2,1,0:T(8,128)S(1)} %broadcast_select_fusion.1.s_a), channel_id=1, source_target_pairs={{0,1},{1,0},{2,3},{3,2},{4,5},{5,4},{6,7},{7,6},{8,9},{9,8},{10,11... | collective-permute-start | bytes 1622024 | tf_op jit(solution)/shard_map/slab0_pair/ppermute | solution.py:544
  35.1 16.5 %collective-permute-start.2 = (f32[1056,128]{1,0:T(8,128)S(1)}, f32[1056,128]{1,0:T(8,128)S(1)}, u32[]{:S(2)}, u32[]{:S(2)}) collective-permute-start(f32[1056,128]{1,0:T(8,128)S(1)} %collective-permute-done.1.rate_e), channel_id=1, source_target_pairs={{0,2},{2,4},{4,6},{3,1},{5,3},{7,5},{8,10},{10,12},{12,14},{11,9},... | collective-permute-start | bytes 1622024 | tf_op jit(solution)/shard_map/rate_ahead/ppermute | solution.py:541
  44.2 19.6 %collective-permute-start.16 = (f32[2,2,264,128]{3,2,1,0:T(8,128)S(1)}, f32[2,2,264,128]{3,2,1,0:T(8,128)}, u32[]{:S(2)}, u32[]{:S(2)}) collective-permute-start(f32[2,2,264,128]{3,2,1,0:T(8,128)S(1)} %collective-permute-done.9.e_a), channel_id=1, source_target_pairs={{0,2},{2,4},{4,6},{3,1},{5,3},{7,5},{8,10},{10,12},{12,14},{11,9},... | collective-permute-start | bytes 1622024 | tf_op jit(solution)/shard_map/slab0_ahead/ppermute | solution.py:572
  50.5 13.2 %collective-permute-start.12 = (f32[2,2,264,128]{3,2,1,0:T(8,128)S(1)}, f32[2,2,264,128]{3,2,1,0:T(8,128)}, u32[]{:S(2)}, u32[]{:S(2)}) collective-permute-start(f32[2,2,264,128]{3,2,1,0:T(8,128)S(1)} %broadcast_select_fusion.s_b), channel_id=1, source_target_pairs={{0,1},{1,0},{2,3},{3,2},{4,5},{5,4},{6,7},{7,6},{8,9},{9,8},{10,11... | collective-permute-start | bytes 1622024 | tf_op jit(solution)/shard_map/slab0_pair/ppermute | solution.py:568
  50.5 18.5 %collective-permute-start.10 = (f32[2,2,264,128]{3,2,1,0:T(8,128)}, f32[2,2,264,128]{3,2,1,0:T(8,128)}, u32[]{:S(2)}, u32[]{:S(2)}) collective-permute-start(f32[2,2,264,128]{3,2,1,0:T(8,128)} %get-tuple-element.43), channel_id=1, source_target_pairs={{0,16},{8,24},{16,0},{24,8},{1,17},{9,25},{17,1},{25,9},{2,18},{10... | collective-permute-start | bytes 1622024 | tf_op jit(solution)/shard_map/slab1_column/ppermute | solution.py:552
  51.6 12.1 %collective-permute-start.14 = (f32[264,128]{1,0:T(8,128)}, f32[264,128]{1,0:T(8,128)}, u32[]{:S(2)}, u32[]{:S(2)}) collective-permute-start(f32[264,128]{1,0:T(8,128)} %get-tuple-element.48), channel_id=1, source_target_pairs={{0,2},{2,4},{4,6},{3,1},{5,3},{7,5},{8,10},{10,12},{12,14},{11,9},... | collective-permute-start | bytes 405512 | tf_op jit(solution)/shard_map/far_layers/ppermute | solution.py:550
  55.7 8.0 %collective-permute-start.13 = (f32[264,128]{1,0:T(8,128)}, f32[264,128]{1,0:T(8,128)}, u32[]{:S(2)}, u32[]{:S(2)}) collective-permute-start(f32[264,128]{1,0:T(8,128)} %get-tuple-element.47), channel_id=1, source_target_pairs={{2,0},{4,2},{6,4},{1,3},{3,5},{5,7},{10,8},{12,10},{14,12},{9,11},... | collective-permute-start | bytes 405512 | tf_op jit(solution)/shard_map/far_layers/ppermute | solution.py:549
  63.8 19.0 %collective-permute-start.15 = (f32[2,2,264,128]{3,2,1,0:T(8,128)S(1)}, f32[2,2,264,128]{3,2,1,0:T(8,128)S(1)}, u32[]{:S(2)}, u32[]{:S(2)}) collective-permute-start(f32[2,2,264,128]{3,2,1,0:T(8,128)S(1)} %copy-done.12), channel_id=1, source_target_pairs={{0,16},{8,24},{16,0},{24,8},{1,17},{9,25},{17,1},{25,9},{2,18},{10... | collective-permute-start | bytes 1622024 | tf_op jit(solution)/shard_map/slab1_column/ppermute | solution.py:570
  64.4 18.4 %collective-permute-start.19 = (f32[2,2,264,128]{3,2,1,0:T(8,128)}, f32[2,2,264,128]{3,2,1,0:T(8,128)S(1)}, u32[]{:S(2)}, u32[]{:S(2)}) collective-permute-start(f32[2,2,264,128]{3,2,1,0:T(8,128)} %collective-permute-done.12.e_b), channel_id=1, source_target_pairs={{0,2},{2,4},{4,6},{3,1},{5,3},{7,5},{8,10},{10,12},{12,14},{11,9},... | collective-permute-start | bytes 1622024 | tf_op jit(solution)/shard_map/slab0_ahead/ppermute | solution.py:573
  69.1 13.7 %collective-permute-start.18 = (f32[2,2,264,128]{3,2,1,0:T(8,128)S(1)}, f32[2,2,264,128]{3,2,1,0:T(8,128)S(1)}, u32[]{:S(2)}, u32[]{:S(2)}) collective-permute-start(f32[2,2,264,128]{3,2,1,0:T(8,128)S(1)} %broadcast_select_fusion.3.s_a), channel_id=1, source_target_pairs={{0,1},{1,0},{2,3},{3,2},{4,5},{5,4},{6,7},{7,6},{8,9},{9,8},{10,11... | collective-permute-start | bytes 1622024 | tf_op jit(solution)/shard_map/slab1_pair/ppermute | solution.py:576
  82.9 12.6 %collective-permute-start.20 = (f32[2,2,264,128]{3,2,1,0:T(8,128)S(1)}, f32[2,2,264,128]{3,2,1,0:T(8,128)S(1)}, u32[]{:S(2)}, u32[]{:S(2)}) collective-permute-start(f32[2,2,264,128]{3,2,1,0:T(8,128)S(1)} %collective-permute-done.18), channel_id=1, source_target_pairs={{0,2},{2,4},{4,6},{3,1},{5,3},{7,5},{8,10},{10,12},{12,14},{11,9},... | collective-permute-start | bytes 1622024 | tf_op jit(solution)/shard_map/slab1_ahead/ppermute | solution.py:578
  87.9 9.8 %collective-permute-start.17 = (f32[2,2,264,128]{3,2,1,0:T(8,128)S(1)}, f32[2,2,264,128]{3,2,1,0:T(8,128)S(1)}, u32[]{:S(2)}, u32[]{:S(2)}) collective-permute-start(f32[2,2,264,128]{3,2,1,0:T(8,128)S(1)} %broadcast_select_fusion.2.s_b), channel_id=1, source_target_pairs={{0,1},{1,0},{2,3},{3,2},{4,5},{5,4},{6,7},{7,6},{8,9},{9,8},{10,11... | collective-permute-start | bytes 1622024 | tf_op jit(solution)/shard_map/slab1_pair/ppermute | solution.py:605
  113.9 8.4 %collective-permute-start.21 = (f32[2,2,4,256,128]{4,3,2,1,0:T(8,128)}, f32[2,2,4,256,128]{4,3,2,1,0:T(8,128)S(1)}, u32[]{:S(2)}, u32[]{:S(2)}) collective-permute-start(f32[2,2,4,256,128]{4,3,2,1,0:T(8,128)} %get-tuple-element.61), channel_id=1, source_target_pairs={{0,8},{8,0},{16,24},{24,16},{1,9},{9,1},{17,25},{25,17},{2,10},{10... | collective-permute-start | bytes 6291464 | tf_op jit(solution)/shard_map/tangent_core/ppermute | solution.py:665
  122.3 9.4 %collective-permute-start.27 = (f32[2,2,32,128]{3,2,1,0:T(8,128)S(1)}, f32[2,2,32,128]{3,2,1,0:T(8,128)S(1)}, u32[]{:S(2)}, u32[]{:S(2)}) collective-permute-start(f32[2,2,32,128]{3,2,1,0:T(8,128)S(1)} %get-tuple-element.66), channel_id=1, source_target_pairs={{0,2},{1,3},{2,0},{3,1},{4,6},{5,7},{6,4},{7,5},{8,10},{9,11},{10,... | collective-permute-start | bytes 196616 | tf_op jit(solution)/shard_map/means_space/ppermute | solution.py:673
  124.0 8.0 %collective-permute-start.26 = (f32[2,2,32,128]{3,2,1,0:T(8,128)S(1)}, f32[2,2,32,128]{3,2,1,0:T(8,128)S(1)}, u32[]{:S(2)}, u32[]{:S(2)}) collective-permute-start(f32[2,2,32,128]{3,2,1,0:T(8,128)S(1)} %get-tuple-element.65), channel_id=1, source_target_pairs={{0,4},{1,5},{2,6},{3,7},{4,0},{5,1},{6,2},{7,3},{8,12},{9,13},{10,... | collective-permute-start | bytes 196616 | tf_op jit(solution)/shard_map/means_space/ppermute | solution.py:673
  124.5 7.5 %collective-permute-start.25 = (f32[2,2,32,128]{3,2,1,0:T(8,128)S(1)}, f32[2,2,32,128]{3,2,1,0:T(8,128)S(1)}, u32[]{:S(2)}, u32[]{:S(2)}) collective-permute-start(f32[2,2,32,128]{3,2,1,0:T(8,128)S(1)} %broadcast_select_fusion.6), channel_id=1, source_target_pairs={{0,6},{1,7},{2,4},{3,5},{4,2},{5,3},{6,0},{7,1},{8,14},{9,15},{10,... | collective-permute-start | bytes 196616 | tf_op jit(solution)/shard_map/means_space/ppermute | solution.py:673
  (24 other events, 203.3 us)
